TPU v7x, 256 devices: a whole 4x4x8 slice. The times are simulated.
256 devices in a mesh: dp: 2 (over z_hi), row: 8 (over x, core), col: 16 (over z_lo, y).
Axes of the slice: x: 4, y: 4, z: 8 (z_hi: 2, z_lo: 4; z = z_hi * 4 + z_lo), core: 2. Of those that a mesh axis runs over, the one named last changes fastest.
Arguments:
- tokens: bfloat16 [8192, 6144], P(('dp', 'row'), 'col'), may hold values from -60 to 60
- layernorm_gain: float32 [6144], P('col'), may hold values from 0.1 to 1.9
- w_query: bfloat16 [6144, 6144], P('row', 'col'), may hold values from -0.078125 to 0.078125
- cotangent: bfloat16 [8192, 6144], P(('dp', 'row'), 'col'), may hold values from -2 to 2
Outputs:
- query: bfloat16 [8192, 6144], P(('dp', 'row'), 'col')
- token_gradient: bfloat16 [8192, 6144], P(('dp', 'row'), 'col')
- grad_w: float32 [6144, 6144], P('row', 'col')
All inputs are finite; a program needn't handle non-finite values.
Results may differ from a plain program's by a relative error of at most 0.0049.
Values may be sent and summed in bfloat16 or wider, within the bound.
No kernel may reach another device: no remote copies, remote signals or barrier semaphores. Data moves between devices by JAX's collectives and lax.ppermute only.
A program may use at most 128 MiB of HBM per device.

v0:
```python
import jax
import jax.numpy as jnp
from jax import lax
from jax.sharding import PartitionSpec as P


def on_device(tokens, layernorm_gain, w_query, cotangent):
    values = tokens.astype(jnp.float32)
    width = values.shape[1] * lax.axis_size("col")
    mean_x = lax.psum(jnp.sum(values, axis=1), "col") / width
    centered_input = values - mean_x[:, None]
    var_x = lax.psum(jnp.sum(centered_input * centered_input, axis=1), "col") / width
    inverse_deviation = lax.rsqrt(var_x + 1e-06)[:, None]
    standardized_input = centered_input * inverse_deviation
    normed_tokens = (standardized_input * layernorm_gain[None, :]).astype(jnp.bfloat16)
    full_rows = lax.all_gather(normed_tokens, "col", axis=1, tiled=True)
    columns = full_rows
    query = jnp.dot(
        columns,
        lax.all_gather(w_query, "row", axis=0, tiled=True),
        preferred_element_type=jnp.float32,
    ).astype(jnp.bfloat16)
    input_partial = lax.dot_general(
        cotangent,
        lax.all_gather(w_query, "row", axis=0, tiled=True),
        (((1,), (1,)), ((), ())),
        preferred_element_type=jnp.float32,
    )
    grad_normed = lax.psum_scatter(input_partial, "col", scatter_dimension=1, tiled=True)
    gradient_standardized = grad_normed * layernorm_gain[None, :]
    first_moment_term, second_moment_term = lax.psum(
        (
            jnp.sum(gradient_standardized, axis=1),
            jnp.sum(gradient_standardized * standardized_input, axis=1),
        ),
        "col",
    )
    first_moment_term = first_moment_term[:, None] / width
    second_moment_term = second_moment_term[:, None] / width
    token_gradient = (
        (gradient_standardized - first_moment_term - standardized_input * second_moment_term)
        * inverse_deviation
    ).astype(jnp.bfloat16)
    columns = full_rows
    partial_grad = lax.psum_scatter(
        lax.dot_general(
            columns, cotangent, (((0,), (0,)), ((), ())), preferred_element_type=jnp.float32
        ),
        "row",
        scatter_dimension=0,
        tiled=True,
    )
    grad_w = lax.psum(partial_grad, "dp")
    return (query, token_gradient, grad_w)


def solution(mesh):
    in_specs = (P(("dp", "row"), "col"), P("col"), P("row", "col"), P(("dp", "row"), "col"))
    out_specs = (P(("dp", "row"), "col"), P(("dp", "row"), "col"), P("row", "col"))
    return jax.shard_map(
        on_device, mesh=mesh, in_specs=in_specs, out_specs=out_specs, check_vma=False
    )
```

profile of v0, /device:TPU:1, one launch (start us, length us, event | category | flops | bytes accessed | tf_op | source)
XLA Modules:
  0.0 501.7 jit_solution(11175826139320616776)
XLA Ops:
  7.2 0.0 copy-start
  7.2 0.0 all-gather.5.cloned.1.call-start
  7.2 0.7 all-gather.5.cloned.1.call-update
  7.9 0.0 reduce-scatter.3.cloned.1.call-start
  8.0 43.0 %all-gather.5.cloned.1.call-done = bf16[6144,384]{1,0:T(8,128)(2,1)} async-done(((bf16[768,384]{1,0:T(8,128)(2,1)}), bf16[6144,384]{1,0:T(8,128)(2,1)}) %all-gather.5.cloned.1.call-update) | async-done | bytes 4718608 | tf_op jit(solution)/shard_map/all_gather | solution.py:20
  50.9 0.0 copy-done
  50.9 8.7 %fusion.11 = f32[512,6144]{1,0:T(8,128)} fusion(bf16[512,384]{1,0:T(8,128)(2,1)S(1)} %copy-done, bf16[6144,384]{1,0:T(8,128)(2,1)} %all-gather.5.cloned.1.call-done), kind=kOutput, calls=%fused_computation.19 | convolution fusion | flops 2415919104 | bytes 17694720 | tf_op jit(solution)/shard_map/dot_general | solution.py:23
  59.7 0.0 copy-start.1
  59.7 0.0 copy-start.2
  59.7 0.0 reduce-scatter.3.cloned.1.call-update
  59.7 0.0 all-gather.3.cloned.1.call-start
  59.7 0.9 copy-done.1
  60.7 0.1 convert_reduce_fusion
  60.8 39.3 %psum.35 = f32[512]{0:T(512)S(1)} all-reduce(f32[512]{0:T(512)S(1)} %convert_reduce_fusion), channel_id=1, replica_groups=mesh['dp'=2,'row'=8,'col'=16] {'col'}, use_global_device_ids=true, to_apply=%region_1.0 | all-reduce | flops 512 | bytes 4096 | tf_op jit(solution)/shard_map/psum | solution.py:10
  100.1 0.3 fusion.10
  100.4 34.6 %psum.36 = f32[512]{0:T(512)S(1)} all-reduce(f32[512]{0:T(512)S(1)} %fusion.10), channel_id=1, replica_groups=mesh['dp'=2,'row'=8,'col'=16] {'col'}, use_global_device_ids=true, to_apply=%region_3.0 | all-reduce | flops 512 | bytes 4096 | tf_op jit(solution)/shard_map/psum | solution.py:12
  135.0 70.6 %reduce-scatter.3.cloned.1.call-done = f32[512,384]{1,0:T(8,128)} async-done(((f32[512,6144]{1,0:T(8,128)}), f32[512,384]{1,0:T(8,128)}) %reduce-scatter.3.cloned.1.call-update) | async-done | bytes 786448 | tf_op jit(solution)/shard_map/reduce_scatter | solution.py:29
  205.6 0.0 copy-done.2
  205.6 1.6 multiply_reduce_fusion
  207.2 31.5 %all-reduce = (f32[512]{0:T(512)S(1)}, f32[512]{0:T(512)S(1)}) all-reduce(f32[512]{0:T(512)S(1)} %get-tuple-element.4, f32[512]{0:T(512)S(1)} %get-tuple-element.3), channel_id=1, replica_groups=mesh['dp'=2,'row'=8,'col'=16] {'col'}, use_global_device_ids=true, to_apply=%region_8.0 | all-reduce | flops 1024 | bytes 8192 | tf_op jit(solution)/shard_map/psum | solution.py:31
  238.7 2.3 fusion.9
  241.0 0.0 all-gather.3.cloned.1.call-update
  241.1 0.0 reduce-scatter.5.cloned.1.call-start
  241.1 92.6 %all-gather.3.cloned.1.call-done = bf16[512,6144]{1,0:T(8,128)(2,1)} async-done(((bf16[512,384]{1,0:T(8,128)(2,1)}), bf16[512,6144]{1,0:T(8,128)(2,1)}) %all-gather.3.cloned.1.call-update) | async-done | bytes 6291472 | tf_op jit(solution)/shard_map/all_gather | solution.py:16
  333.7 9.9 %fusion.12 = f32[6144,384]{1,0:T(8,128)} fusion(bf16[512,6144]{1,0:T(8,128)(2,1)} %all-gather.3.cloned.1.call-done, bf16[512,384]{1,0:T(8,128)(2,1)S(1)} %copy-done), kind=kOutput, calls=%fused_computation.20 | convolution fusion | flops 2415919104 | bytes 16121856 | tf_op jit(solution)/shard_map/dot_general | solution.py:46
  343.6 0.0 reduce-scatter.5.cloned.1.call-update
  343.6 0.0 all-reduce.3.cloned.1.call-start
  343.7 62.8 %reduce-scatter.5.cloned.1.call-done = f32[768,384]{1,0:T(8,128)} async-done(((f32[6144,384]{1,0:T(8,128)}), f32[768,384]{1,0:T(8,128)}) %reduce-scatter.5.cloned.1.call-update) | async-done | bytes 1179664 | tf_op jit(solution)/shard_map/reduce_scatter | solution.py:45
  406.5 0.0 all-reduce.3.cloned.1.call-update
  406.5 8.3 %convolution_convert_fusion = bf16[512,384]{1,0:T(8,128)(2,1)} fusion(bf16[512,6144]{1,0:T(8,128)(2,1)} %all-gather.3.cloned.1.call-done, bf16[6144,384]{1,0:T(8,128)(2,1)} %all-gather.5.cloned.1.call-done), kind=kOutput, calls=%fused_computation | convolution fusion | flops 2416115712 | bytes 11403264 | tf_op jit(solution)/shard_map/dot_general | solution.py:18
  414.8 78.0 %all-reduce.3.cloned.1.call-done = f32[768,384]{1,0:T(8,128)} async-done(((f32[768,384]{1,0:T(8,128)}), f32[768,384]{1,0:T(8,128)}) %all-reduce.3.cloned.1.call-update) | async-done | bytes 1179664 | tf_op jit(solution)/shard_map/psum | solution.py:53
  492.8 2.4 copy.8
  (3 shorter events, 0.0 us)
Async XLA Ops:
  7.2 43.8 %copy-start = (bf16[512,384]{1,0:T(8,128)(2,1)S(1)}, bf16[512,384]{1,0:T(8,128)(2,1)}, u32[]{:S(2)}) copy-start(bf16[512,384]{1,0:T(8,128)(2,1)} %param.7) | copy-start | bytes 1179652
  7.2 43.8 %all-gather.5.cloned.1.call-start = ((), (), s32[]{:S(2)}) async-start(), calls=%async_computation.3 | async-start | bytes 5308416 | tf_op jit(solution)/shard_map/all_gather | solution.py:20
  7.9 197.7 %reduce-scatter.3.cloned.1.call-start = ((), (), s32[]{:S(2)}) async-start(), calls=%async_computation.4 | async-start | bytes 13369344 | tf_op jit(solution)/shard_map/reduce_scatter | solution.py:29
  59.7 1.0 copy-start.1
  59.7 145.9 %copy-start.2 = (f32[384]{0:T(512)S(1)}, f32[384]{0:T(512)}, u32[]{:S(2)}) copy-start(f32[384]{0:T(512)} %param.5) | copy-start | bytes 4612
  59.7 274.0 %all-gather.3.cloned.1.call-start = ((), (), s32[]{:S(2)}) async-start(), calls=%async_computation.2 | async-start | bytes 6684672 | tf_op jit(solution)/shard_map/all_gather | solution.py:16
  241.1 165.4 %reduce-scatter.5.cloned.1.call-start = ((), (), s32[]{:S(2)}) async-start(), calls=%async_computation.5 | async-start | bytes 10616832 | tf_op jit(solution)/shard_map/reduce_scatter | solution.py:45
  343.6 149.2 %all-reduce.3.cloned.1.call-start = ((), (), s32[]{:S(2)}) async-start(), calls=%async_computation.6 | async-start | bytes 2359296 | tf_op jit(solution)/shard_map/psum | solution.py:53
Sparse Core Ops, SparseCore 0:
  9.8 41.0 all-gather.4
  59.8 145.7 reduce-scatter.2
  241.2 92.5 all-gather.2
  343.8 62.6 reduce-scatter.4
  408.9 83.8 all-reduce.2
where the time goes:
time: 502 us
  waiting for transfers between devices  348 us (69%)
  blocking collectives  105 us (21%)
  matrix products  26.9 us (5%)
  between operations  13.8 us (3%)
    all_gather x1, waiting for transfers between devices, on_device(): full_rows = lax.all_gather(normed_tokens, 'col', axis=1, tiled=True)  92.6 us
    psum x1, waiting for transfers between devices, on_device(): grad_w = lax.psum(partial_grad, 'dp')  78 us
    reduce_scatter x1, waiting for transfers between devices, on_device(): lax.psum_scatter(input_partial, 'col', scatter_dimension=1, tiled=True)  70.6 us
    reduce_scatter x1, waiting for transfers between devices, on_device(): lax.psum_scatter(lax.dot_general(columns, cotangent, (((0,), (0,)), ((),...  62.8 us
    all_gather x1, waiting for transfers between devices, on_device(): lax.all_gather(w_query, 'row', axis=0, tiled=True)  43 us
    psum x1, blocking collectives, on_device(): mean_x = lax.psum(jnp.sum(values, axis=1), 'col') / width  39.3 us
    psum x1, blocking collectives, on_device(): lax.psum(jnp.sum(centered_input * centered_input, axis=1), 'col') / width  34.6 us
    psum x1, blocking collectives, on_device(): lax.psum((jnp.sum(gradient_standardized, axis=1), jnp.sum(gradient_standa...  31.5 us
  transfers between devices with their start and end apart: 5, of which 5 were waited for; matrix products, arithmetic and copies ran while one was open for 2% of the time, Pallas kernels for 0%

commit v1 on v0

v1 whole, which is shorter than its diff:
```python
import itertools

import jax
import jax.numpy as jnp
from jax import lax
from jax.experimental import pallas as pl
from jax.experimental.pallas import tpu as pltpu
from jax.sharding import Mesh, PartitionSpec as P

AXES = ("dp", "x", "c", "z", "y")
SIZES = dict(dp=2, x=4, c=2, z=4, y=4)
T = 512
F = 384
VMEM_LIMIT = 40 * 1024 * 1024
F32 = jnp.float32
BF16 = jnp.bfloat16


def send(value, axes, to):
    coords = list(itertools.product(*(range(SIZES[a]) for a in axes)))
    flat = {c: i for i, c in enumerate(coords)}
    perm = [(flat[c], flat[tuple(to(*c))]) for c in coords]
    return lax.ppermute(value, axes if len(axes) > 1 else axes[0], perm)


def swap(value, axis, e):
    return send(value, (axis,), lambda i: (i ^ e,))


def dot_nt(a, b):
    return lax.dot_general(a, b, (((1,), (1,)), ((), ())), preferred_element_type=F32)


def dot_nn(a, b):
    return lax.dot_general(a, b, (((1,), (0,)), ((), ())), preferred_element_type=F32)


def load_all(copies):
    for c in copies:
        c.start()


def lanes(e, width=F):
    return pl.ds(e * width, width)


def call(kernel, out_shape, scratch, flops, nbytes, n_any, n_vmem):
    def outer(*args):
        return pl.pallas_call(
            kernel,
            out_shape=out_shape,
            in_specs=[pl.BlockSpec(memory_space=pl.ANY)] * n_any
            + [pl.BlockSpec(memory_space=pltpu.VMEM)] * n_vmem,
            out_specs=jax.tree.map(lambda _: pl.BlockSpec(memory_space=pltpu.VMEM), out_shape),
            scratch_shapes=scratch,
            compiler_params=pltpu.CompilerParams(vmem_limit_bytes=VMEM_LIMIT),
            cost_estimate=pl.CostEstimate(flops=flops, bytes_accessed=nbytes, transcendentals=0),
        )(*args)

    return outer


def gw_other_kernel(*refs):
    normed, cots = refs[0:4], refs[4:8]
    outs, turned = refs[8:12], refs[12]
    nbuf, cbuf, sems = refs[13:]
    x, c, z = lax.axis_index("x"), lax.axis_index("c"), lax.axis_index("z")
    copies = [pltpu.make_async_copy(normed[e], nbuf.at[z ^ e], sems.at[e]) for e in range(4)]
    copies += [
        pltpu.make_async_copy(cots[e], cbuf.at[e // 2, :, lanes(e % 2)], sems.at[4 + e])
        for e in range(4)
    ]
    load_all(copies)
    for cp in copies:
        cp.wait()
    for e in range(4):
        row = x ^ e
        nt = nbuf[row].T
        turned[e] = nt
        outs[e][...] = dot_nn(nt, cbuf[1 - c]).astype(BF16)


def gw_own_kernel(*refs):
    turned, cots, other = refs[0], refs[1:5], refs[5:9]
    outs = refs[9:13]
    tbuf, cbuf, obuf, sems = refs[13:]
    c = lax.axis_index("c")
    copies = [pltpu.make_async_copy(turned, tbuf, sems.at[0])]
    copies += [
        pltpu.make_async_copy(cots[e], cbuf.at[e // 2, :, lanes(e % 2)], sems.at[1 + e])
        for e in range(4)
    ]
    copies += [pltpu.make_async_copy(other[e], obuf.at[e], sems.at[5 + e]) for e in range(4)]
    load_all(copies)
    for cp in copies:
        cp.wait()
    for e in range(4):
        total = dot_nn(tbuf[e], cbuf[c]) + obuf[e].astype(F32)
        outs[e][...] = total.astype(outs[e].dtype)


def weight_copies(mine, theirs, wbuf, sems, first, x, c):
    copies = []
    for e in range(4):
        copies.append(pltpu.make_async_copy(mine[e], wbuf.at[x ^ e, c], sems.at[first + 2 * e]))
        copies.append(
            pltpu.make_async_copy(theirs[e], wbuf.at[x ^ e, 1 - c], sems.at[first + 2 * e + 1])
        )
    return copies


def back_kernel(*refs):
    mine, theirs, cots, normed = refs[0:4], refs[4:8], refs[8:12], refs[12:16]
    gains = refs[16]
    outs, sums = refs[17:21], refs[21]
    wbuf, cbuf, nbuf, sems = refs[22:]
    x, c, z = lax.axis_index("x"), lax.axis_index("c"), lax.axis_index("z")
    copies = weight_copies(mine, theirs, wbuf, sems, 0, x, c)
    copies += [
        pltpu.make_async_copy(cots[e], cbuf.at[e // 2, :, lanes(e % 2)], sems.at[8 + e])
        for e in range(4)
    ]
    copies += [pltpu.make_async_copy(normed[e], nbuf.at[e], sems.at[12 + e]) for e in range(4)]
    load_all(copies)
    for cp in copies:
        cp.wait()
    first = jnp.zeros((T, 1), F32)
    second = jnp.zeros((T, 1), F32)
    for e in (3, 2, 1, 0):
        rows = z ^ e
        part = dot_nt(cbuf[0], wbuf[rows, 0]) + dot_nt(cbuf[1], wbuf[rows, 1])
        first = first + jnp.sum(part * gains[e : e + 1, :], axis=1, keepdims=True)
        second = second + jnp.sum(part * nbuf[e].astype(F32), axis=1, keepdims=True)
        outs[e][...] = part.astype(outs[e].dtype)
    lane = lax.broadcasted_iota(jnp.int32, (T, 128), 1)
    both = jnp.where(lane == 0, first, second)
    sums[...] = both.T[:8]


def query_kernel(*refs):
    mine, theirs, normed = refs[0:4], refs[4:8], refs[8:12]
    outs = refs[12:16]
    wbuf, nbuf, sems = refs[16:]
    x, c, z = lax.axis_index("x"), lax.axis_index("c"), lax.axis_index("z")
    copies = weight_copies(mine, theirs, wbuf, sems, 0, x, c)
    copies += [pltpu.make_async_copy(normed[e], nbuf.at[z ^ e], sems.at[8 + e]) for e in range(4)]
    load_all(copies)
    for cp in copies:
        cp.wait()
    for half in (1, 0):
        part = dot_nn(nbuf[0], wbuf[0, half])
        for k in range(1, 4):
            part = part + dot_nn(nbuf[k], wbuf[k, half])
        for a in range(2):
            out = outs[2 * half + a]
            out[...] = part[:, a * F : (a + 1) * F].astype(out.dtype)


def shape(*dims, dtype=BF16):
    return jax.ShapeDtypeStruct(dims, dtype)


def merge(means, squares, count):
    mean = sum(means) / len(means)
    spread = sum((m - mean) * (m - mean) for m in means)
    return mean, sum(squares) + count * spread


def on_device(tokens, gain, w, cot):
    c, z, y = lax.axis_index("c"), lax.axis_index("z"), lax.axis_index("y")
    odd = y % 2

    def to_a(s, yy):
        return ((yy >> 1) ^ s, 2 * s + (yy & 1))

    def to_b(s, yy):
        return ((yy >> 1) ^ s, 2 * s + 1 - (yy & 1))

    wa = send(lax.dynamic_slice(w, (odd * F, 0), (F, F)), ("c", "y"), to_a)
    wb = send(lax.dynamic_slice(w, ((1 - odd) * F, 0), (F, F)), ("c", "y"), to_b)
    w_mine = [jnp.concatenate([wa, wb], axis=1)]
    w_mine += [swap(w_mine[0], "x", e) for e in (1, 2, 3)]
    w_theirs = [swap(m, "c", 1) for m in w_mine]

    tok = [tokens] + [swap(tokens, "z", e) for e in (1, 2, 3)]
    cots = [cot] + [swap(cot, "y", e) for e in (1, 2, 3)]

    values = tokens.astype(F32)
    own_mean = jnp.sum(values, axis=1) / F
    centred = values - own_mean[:, None]
    own = jnp.stack([own_mean, jnp.sum(centred * centred, axis=1)])
    parts = [own] + [swap(own, "y", e) for e in (1, 2, 3)]
    mean_y, squares_y = merge([p[0] for p in parts], [p[1] for p in parts], F)
    packet = jnp.concatenate([mean_y, squares_y, gain])
    packets = [packet] + [swap(packet, "z", e) for e in (1, 2, 3)]
    mean, squares = merge([p[:T] for p in packets], [p[T : 2 * T] for p in packets], 4 * F)
    gains = [p[2 * T :] for p in packets]
    width = 16 * F
    inverse = lax.rsqrt(squares / width + 1e-06)[:, None]
    mean = mean[:, None]

    def standardize(block):
        return (block.astype(F32) - mean) * inverse

    normed = [(standardize(b) * g[None, :]).astype(BF16) for b, g in zip(tok, gains)]

    dma = pltpu.SemaphoreType.DMA
    gw = call(
        gw_other_kernel,
        [shape(F, 2 * F)] * 4 + [shape(4, F, T)],
        [pltpu.VMEM((4, T, F), BF16), pltpu.VMEM((2, T, 2 * F), BF16), dma((8,))],
        2 * T * 4 * F * 2 * F,
        7_000_000,
        8,
        0,
    )(*normed, *cots)
    turned = gw[4]
    gw_theirs = [swap(g, "c", 1) for g in gw[:4]]

    back = call(
        back_kernel,
        [shape(T, F, dtype=F32)] + [shape(T, F)] * 3 + [shape(8, T, dtype=F32)],
        [
            pltpu.VMEM((4, 2, F, 2 * F), BF16),
            pltpu.VMEM((2, T, 2 * F), BF16),
            pltpu.VMEM((4, T, F), BF16),
            dma((16,)),
        ],
        2 * T * 4 * F * 4 * F,
        12_000_000,
        16,
        1,
    )(*w_mine, *w_theirs, *cots, *normed, jnp.stack(gains))
    grad_parts = [back[0]] + [swap(back[e], "z", e) for e in (1, 2, 3)]

    gw_sum = call(
        gw_own_kernel,
        [shape(F, 2 * F, dtype=F32)] + [shape(F, 2 * F)] * 3,
        [
            pltpu.VMEM((4, F, T), BF16),
            pltpu.VMEM((2, T, 2 * F), BF16),
            pltpu.VMEM((4, F, 2 * F), BF16),
            dma((9,)),
        ],
        2 * T * 4 * F * 2 * F,
        9_000_000,
        9,
        0,
    )(turned, *cots, *gw_theirs)
    gw_parts = [gw_sum[0]] + [swap(gw_sum[e], "x", e) for e in (1, 2, 3)]

    query_out = call(
        query_kernel,
        [shape(T, F, dtype=F32)] + [shape(T, F)] * 3,
        [pltpu.VMEM((4, 2, F, 2 * F), BF16), pltpu.VMEM((4, T, F), BF16), dma((12,))],
        2 * T * 4 * F * 4 * F,
        9_000_000,
        12,
        0,
    )(*w_mine, *w_theirs, *normed)
    query_parts = [query_out[0]] + [swap(query_out[e], "y", e) for e in (1, 2, 3)]

    block = sum(p.astype(F32) for p in gw_parts).astype(BF16)

    def home(a):
        return lambda d, cc, yy: (d, yy >> 1, yy ^ (2 * cc + a))

    def away(a):
        return lambda d, cc, yy: (1 - d, yy >> 1, yy ^ (2 * cc + a))

    halves = [block[:, :F], block[:, F:]]
    far = [send(halves[a], ("dp", "c", "y"), away(a)) for a in (0, 1)]
    near = [send(halves[a], ("dp", "c", "y"), home(a)) for a in (0, 1)]
    got_a, got_b = (n.astype(F32) + f.astype(F32) for n, f in zip(near, far))
    even = odd == 0
    grad_w = jnp.concatenate([jnp.where(even, got_a, got_b), jnp.where(even, got_b, got_a)])

    sums = back[4][:2]
    sums = sums + sum(swap(sums, "y", e) for e in (1, 2, 3))
    sums = sums + sum(swap(sums, "z", e) for e in (1, 2, 3))
    first, second = sums[0][:, None] / width, sums[1][:, None] / width
    grad_hat = sum(p.astype(F32) for p in grad_parts) * gain[None, :]
    token_gradient = ((grad_hat - first - standardize(tokens) * second) * inverse).astype(BF16)
    query = sum(p.astype(F32) for p in query_parts).astype(BF16)
    return query, token_gradient, grad_w


def solution(mesh):
    fine = Mesh(mesh.devices.reshape([SIZES[a] for a in AXES]), AXES)
    rows, cols = ("dp", "x", "c"), ("z", "y")
    in_specs = (P(rows, cols), P(cols), P(("x", "c"), cols), P(rows, cols))
    out_specs = (P(rows, cols), P(rows, cols), P(("x", "c"), cols))
    return jax.shard_map(
        on_device, mesh=fine, in_specs=in_specs, out_specs=out_specs, check_vma=False
    )
```

time: 502 us -> 194 us (0.39)
  waiting for transfers between devices: 348 us -> 73.5 us
  blocking collectives: 105 us -> 0 us
  starting transfers between devices: 0.2 us -> 79.6 us
  matrix products: 26.9 us -> 0 us
  Pallas kernels: 0 us -> 16.7 us
  between operations: 13.8 us -> 1.13 us
  local copies, waits for them, and re-layouts: 3.29 us -> 13.5 us
    all_gather x2 -> x0, waiting for transfers between devices: 136 us -> none  [the longest x1 92.6 us: on_device(): full_rows = lax.all_gather(normed_tokens, 'col', axis=1, tiled=True)]
    reduce_scatter x2 -> x0, waiting for transfers between devices: 133 us -> none  [the longest x1 70.6 us: on_device(): lax.psum_scatter(input_partial, 'col', scatter_dimension=1, tiled=True)]
    psum x3 -> x0, blocking collectives: 105 us -> none  [the longest x1 39.3 us: on_device(): mean_x = lax.psum(jnp.sum(values, axis=1), 'col') / width]
    ppermute x0 -> x44, starting transfers between devices: none -> 79.6 us  [send(): return lax.ppermute(value, axes if len(axes) > 1 else axes[0], perm)]
    psum x1 -> x0, waiting for transfers between devices: 78 us -> none  [on_device(): grad_w = lax.psum(partial_grad, 'dp')]
    ppermute x0 -> x44, waiting for transfers between devices: none -> 73.5 us  [send(): return lax.ppermute(value, axes if len(axes) > 1 else axes[0], perm)]
    dot_general x3 -> x0, matrix products: 26.9 us -> none  [the longest x1 9.88 us: on_device(): lax.dot_general(columns, cotangent, (((0,), (0,)), ((), ())), preferred_e...]
    pallas_call x0 -> x4, Pallas kernels: none -> 16.7 us  [outer(): pl.pallas_call(kernel, out_shape=out_shape, in_specs=[pl.BlockSpec(memory...]
  transfers between devices with their start and end apart: 5 -> 44, of which waited for: 5 -> 15; matrix products, arithmetic and copies ran while one was open for 2% -> 5% of each run, Pallas kernels for 0% -> 9%
where the time goes in v1:
time: 194 us; the launch traced here: 193 us
  starting transfers between devices  79.6 us (41%)
  waiting for transfers between devices  73.5 us (38%)
  Pallas kernels  16.7 us (9%)
  local copies, waits for them, and re-layouts  13.5 us (7%)
  other arithmetic  8.74 us (5%)
    ppermute x44, starting transfers between devices, send(): return lax.ppermute(value, axes if len(axes) > 1 else axes[0], perm)  79.6 us
    ppermute x44, waiting for transfers between devices, send(): return lax.ppermute(value, axes if len(axes) > 1 else axes[0], perm)  73.5 us
    pallas_call x4, Pallas kernels, outer(): pl.pallas_call(kernel, out_shape=out_shape, in_specs=[pl.BlockSpec(memory...  16.7 us
    unnamed x63, local copies, waits for them, and re-layouts  11.6 us
  transfers between devices with their start and end apart: 44, of which 15 were waited for; matrix products, arithmetic and copies ran while one was open for 5% of the time, Pallas kernels for 9%

profile of v1, /device:TPU:1, one launch (start us, length us, event | category | flops | bytes accessed | tf_op | source)
XLA Modules:
  0.0 193.1 jit_solution(16242671849527751088)
XLA Ops:
  0.7 5.3 %collective-permute-start.17 = (bf16[512,384]{1,0:T(8,128)(2,1)}, bf16[512,384]{1,0:T(8,128)(2,1)S(1)}, u32[]{:S(2)}, u32[]{:S(2)}) collective-permute-start(bf16[512,384]{1,0:T(8,128)(2,1)} %param.4), channel_id=1, source_target_pairs={{0,12},{4,8},{8,4},{12,0},{1,13},{5,9},{9,5},{13,1},{2,14},{6,10},... | collective-permute-start | bytes 1179656 | tf_op jit(solution)/shard_map/ppermute | solution.py:23
  8.4 2.8 %collective-permute-start.11 = (f32[2,512]{1,0:T(2,128)S(1)}, f32[2,512]{1,0:T(2,128)S(1)}, u32[]{:S(2)}, u32[]{:S(2)}) collective-permute-start(f32[2,512]{1,0:T(2,128)S(1)} %pad_maximum_fusion.3), channel_id=1, source_target_pairs={{0,3},{1,2},{2,1},{3,0},{4,7},{5,6},{6,5},{7,4},{8,11},{9,10},{10,... | collective-permute-start | bytes 12296 | tf_op jit(solution)/shard_map/ppermute | solution.py:23
  13.4 1.9 collective-permute-done.10
  15.3 2.8 %collective-permute-start = (bf16[384,384]{1,0:T(8,128)(2,1)S(1)}, bf16[384,384]{1,0:T(8,128)(2,1)S(1)}, u32[]{:S(2)}, u32[]{:S(2)}) collective-permute-start(bf16[384,384]{1,0:T(8,128)(2,1)S(1)} %get-tuple-element.48), channel_id=1, source_target_pairs={{0,0},{1,1},{2,16},{3,17},{16,18},{17,19},{18,2},{19,3},{4,4},{5,5... | collective-permute-start | bytes 884744 | tf_op jit(solution)/shard_map/ppermute | solution.py:23
  18.1 2.0 %collective-permute-start.1 = (bf16[384,384]{1,0:T(8,128)(2,1)S(1)}, bf16[384,384]{1,0:T(8,128)(2,1)S(1)}, u32[]{:S(2)}, u32[]{:S(2)}) collective-permute-start(bf16[384,384]{1,0:T(8,128)(2,1)S(1)} %get-tuple-element.47), channel_id=1, source_target_pairs={{0,1},{1,0},{2,17},{3,16},{16,19},{17,18},{18,3},{19,2},{4,5},{5,4... | collective-permute-start | bytes 884744 | tf_op jit(solution)/shard_map/ppermute | solution.py:23
  20.2 7.4 %collective-permute-done = bf16[384,384]{1,0:T(8,128)(2,1)S(1)} collective-permute-done((bf16[384,384]{1,0:T(8,128)(2,1)S(1)}, bf16[384,384]{1,0:T(8,128)(2,1)S(1)}, u32[]{:S(2)}, u32[]{:S(2)}) %collective-permute-start) | collective-permute-done | bytes 294944 | tf_op jit(solution)/shard_map/ppermute | solution.py:23
  27.6 2.8 %collective-permute-start.14 = (f32[1408]{0:T(1024)S(1)}, f32[1408]{0:T(1024)S(1)}, u32[]{:S(2)}, u32[]{:S(2)}) collective-permute-start(f32[1408]{0:T(1024)S(1)} %pad_maximum_fusion.1), channel_id=1, source_target_pairs={{0,12},{4,8},{8,4},{12,0},{1,13},{5,9},{9,5},{13,1},{2,14},{6,10},... | collective-permute-start | bytes 16904 | tf_op jit(solution)/shard_map/ppermute | solution.py:23
  32.1 8.0 %collective-permute-start.13 = (f32[1408]{0:T(1024)S(1)}, f32[1408]{0:T(1024)S(1)}, u32[]{:S(2)}, u32[]{:S(2)}) collective-permute-start(f32[1408]{0:T(1024)S(1)} %pad_maximum_fusion.1), channel_id=1, source_target_pairs={{0,8},{4,12},{8,0},{12,4},{1,9},{5,13},{9,1},{13,5},{2,10},{6,14},... | collective-permute-start | bytes 16904 | tf_op jit(solution)/shard_map/ppermute | solution.py:23
  42.6 2.9 %collective-permute-start.22 = (bf16[512,384]{1,0:T(8,128)(2,1)S(1)}, bf16[512,384]{1,0:T(8,128)(2,1)S(1)}, u32[]{:S(2)}, u32[]{:S(2)}) collective-permute-start(bf16[512,384]{1,0:T(8,128)(2,1)S(1)} %copy-done), channel_id=1, source_target_pairs={{0,2},{1,3},{2,0},{3,1},{4,6},{5,7},{6,4},{7,5},{8,10},{9,11},{10,... | collective-permute-start | bytes 1179656 | tf_op jit(solution)/shard_map/ppermute | solution.py:23
  47.6 2.5 %collective-permute-start.3 = (bf16[384,768]{1,0:T(8,128)(2,1)S(1)}, bf16[384,768]{1,0:T(8,128)(2,1)S(1)}, u32[]{:S(2)}, u32[]{:S(2)}) collective-permute-start(bf16[384,768]{1,0:T(8,128)(2,1)S(1)} %constant_dynamic-update-slice_fusion.refs_0_), channel_id=1, source_target_pairs={{0,64},{32,96},{64,0},{96,32},{1,65},{33,97},{65,1},{97,33},{2,66}... | collective-permute-start | bytes 1769480 | tf_op jit(solution)/shard_map/ppermute | solution.py:23
  51.5 8.4 %collective-permute-done.22.refs_10_.refs_6_.refs_3_ = bf16[512,384]{1,0:T(8,128)(2,1)S(1)} collective-permute-done((bf16[512,384]{1,0:T(8,128)(2,1)S(1)}, bf16[512,384]{1,0:T(8,128)(2,1)S(1)}, u32[]{:S(2)}, u32[]{:S(2)}) %collective-permute-start.22) | collective-permute-done | bytes 393248 | tf_op jit(solution)/shard_map/ppermute | solution.py:23
  60.8 2.4 %shard_map.69 = (bf16[384,768]{1,0:T(8,128)(2,1)S(1)}, bf16[384,768]{1,0:T(8,128)(2,1)S(1)}, bf16[384,768]{1,0:T(8,128)(2,1)S(1)}, bf16[384,768]{1,0:T(8,128)(2,1)S(1)}, bf16[4,384,512]{2,1,0:T(8,128)(2,1)S(1)}) custom-call(bf16[512,384]{1,0:T(8,128)(2,1)S(1)} %get-tuple-element.54.refs_8_.refs_12_.refs_0_, ...), custom_call_target="tpu_custom_call" | custom-call | flops 1207959552 | bytes 7000000 | tf_op jit(solution)/shard_map/pallas_call | solution.py:49
  63.2 6.1 %collective-permute-start.33 = (bf16[384,768]{1,0:T(8,128)(2,1)S(1)}, bf16[384,768]{1,0:T(8,128)(2,1)S(1)}, u32[]{:S(2)}, u32[]{:S(2)}) collective-permute-start(bf16[384,768]{1,0:T(8,128)(2,1)S(1)} %get-tuple-element.31), channel_id=1, source_target_pairs={{0,16},{16,0},{1,17},{17,1},{2,18},{18,2},{3,19},{19,3},{4,20},{20... | collective-permute-start | bytes 1769480 | tf_op jit(solution)/shard_map/ppermute | solution.py:23
  69.9 2.3 %collective-permute-done.3.refs_2_ = bf16[384,768]{1,0:T(8,128)(2,1)S(1)} collective-permute-done((bf16[384,768]{1,0:T(8,128)(2,1)S(1)}, bf16[384,768]{1,0:T(8,128)(2,1)S(1)}, u32[]{:S(2)}, u32[]{:S(2)}) %collective-permute-start.3) | collective-permute-done | bytes 589856 | tf_op jit(solution)/shard_map/ppermute | solution.py:23
  72.2 4.8 %collective-permute-start.36 = (bf16[384,768]{1,0:T(8,128)(2,1)S(1)}, bf16[384,768]{1,0:T(8,128)(2,1)S(1)}, u32[]{:S(2)}, u32[]{:S(2)}) collective-permute-start(bf16[384,768]{1,0:T(8,128)(2,1)S(1)} %get-tuple-element.34), channel_id=1, source_target_pairs={{0,16},{16,0},{1,17},{17,1},{2,18},{18,2},{3,19},{19,3},{4,20},{20... | collective-permute-start | bytes 1769480 | tf_op jit(solution)/shard_map/ppermute | solution.py:23
  77.0 3.4 %collective-permute-start.5 = (bf16[384,768]{1,0:T(8,128)(2,1)S(1)}, bf16[384,768]{1,0:T(8,128)(2,1)S(1)}, u32[]{:S(2)}, u32[]{:S(2)}) collective-permute-start(bf16[384,768]{1,0:T(8,128)(2,1)S(1)} %constant_dynamic-update-slice_fusion.refs_0_), channel_id=1, source_target_pairs={{0,16},{16,0},{1,17},{17,1},{2,18},{18,2},{3,19},{19,3},{4,20},{20... | collective-permute-start | bytes 1769480 | tf_op jit(solution)/shard_map/ppermute | solution.py:23
  81.0 3.1 %shard_map.70 = (f32[384,768]{1,0:T(8,128)S(1)}, bf16[384,768]{1,0:T(8,128)(2,1)}, bf16[384,768]{1,0:T(8,128)(2,1)}, bf16[384,768]{1,0:T(8,128)(2,1)}) custom-call(bf16[4,384,512]{2,1,0:T(8,128)(2,1)S(1)} %get-tuple-element.30.refs_0_, bf16[512,384]{1,0:T(8,128)(2,1)S(1)} %copy-done, bf16[512,384]{1,0:T(8,128)(2,1)S(1)} %collective-permute-done.21.refs_9_.refs_5_.refs_2_, ...), custom_call_target="tpu_custom_call" | custom-call | flops 1207959552 | bytes 9000000 | tf_op jit(solution)/shard_map/pallas_call | solution.py:49
  85.0 2.5 %collective-permute-start.37 = (bf16[384,768]{1,0:T(8,128)(2,1)}, bf16[384,768]{1,0:T(8,128)(2,1)}, u32[]{:S(2)}, u32[]{:S(2)}) collective-permute-start(bf16[384,768]{1,0:T(8,128)(2,1)} %get-tuple-element.36), channel_id=1, source_target_pairs={{0,32},{32,0},{64,96},{96,64},{1,33},{33,1},{65,97},{97,65},{2,34}... | collective-permute-start | bytes 1769480 | tf_op jit(solution)/shard_map/ppermute | solution.py:23
  87.6 5.8 %shard_map.68 = (f32[512,384]{1,0:T(8,128)S(1)}, bf16[512,384]{1,0:T(8,128)(2,1)S(1)}, bf16[512,384]{1,0:T(8,128)(2,1)S(1)}, bf16[512,384]{1,0:T(8,128)(2,1)S(1)}, f32[8,512]{1,0:T(8,128)S(1)}) custom-call(bf16[384,768]{1,0:T(8,128)(2,1)S(1)} %constant_dynamic-update-slice_fusion.refs_0_, bf16[384,768]{1,0:T(8,128)(2,1)S(1)} %collective-permute-done.2.refs_1_, ...), custom_call_target="tpu_custom_call" | custom-call | flops 2415919104 | bytes 12000000 | tf_op jit(solution)/shard_map/pallas_call | solution.py:49
  96.3 1.9 collective-permute-start.29
  98.2 2.4 %collective-permute-done.29 = f32[2,512]{1,0:T(2,128)} collective-permute-done((f32[2,512]{1,0:T(2,128)}, f32[2,512]{1,0:T(2,128)}, u32[]{:S(2)}, u32[]{:S(2)}) %collective-permute-start.29) | collective-permute-done | bytes 4128 | tf_op jit(solution)/shard_map/ppermute | solution.py:23
  109.3 5.3 %shard_map.67 = (f32[512,384]{1,0:T(8,128)S(1)}, bf16[512,384]{1,0:T(8,128)(2,1)S(1)}, bf16[512,384]{1,0:T(8,128)(2,1)S(1)}, bf16[512,384]{1,0:T(8,128)(2,1)S(1)}) custom-call(bf16[384,768]{1,0:T(8,128)(2,1)S(1)} %copy-done.2, bf16[384,768]{1,0:T(8,128)(2,1)S(1)} %copy-done.4, bf16[384,768]{1,0:T(8,128)(2,1)S(1)} %copy-done.6, ...), custom_call_target="tpu_custom_call" | custom-call | flops 2415919104 | bytes 9000000 | tf_op jit(solution)/shard_map/pallas_call | solution.py:49
  122.5 10.7 %collective-permute-start.41 = (bf16[384,384]{1,0:T(8,128)(2,1)S(1)}, bf16[384,384]{1,0:T(8,128)(2,1)S(1)}, u32[]{:S(2)}, u32[]{:S(2)}) collective-permute-start(bf16[384,384]{1,0:T(8,128)(2,1)S(1)} %get-tuple-element.46), channel_id=1, source_target_pairs={{0,128},{1,129},{2,146},{3,147},{16,130},{17,131},{18,144},{19,145... | collective-permute-start | bytes 884744 | tf_op jit(solution)/shard_map/ppermute | solution.py:23
  133.1 1.9 collective-permute-start.40
  135.2 3.5 %collective-permute-start.42 = (bf16[384,384]{1,0:T(8,128)(2,1)S(1)}, bf16[384,384]{1,0:T(8,128)(2,1)S(1)}, u32[]{:S(2)}, u32[]{:S(2)}) collective-permute-start(bf16[384,384]{1,0:T(8,128)(2,1)S(1)} %get-tuple-element.45), channel_id=1, source_target_pairs={{0,1},{1,0},{2,19},{3,18},{16,3},{17,2},{18,17},{19,16},{128,129},... | collective-permute-start | bytes 884744 | tf_op jit(solution)/shard_map/ppermute | solution.py:23
  138.7 2.6 %collective-permute-done.41 = bf16[384,384]{1,0:T(8,128)(2,1)S(1)} collective-permute-done((bf16[384,384]{1,0:T(8,128)(2,1)S(1)}, bf16[384,384]{1,0:T(8,128)(2,1)S(1)}, u32[]{:S(2)}, u32[]{:S(2)}) %collective-permute-start.41) | collective-permute-done | bytes 294944 | tf_op jit(solution)/shard_map/ppermute | solution.py:23
  141.3 5.7 %collective-permute-done.40 = bf16[384,384]{1,0:T(8,128)(2,1)S(1)} collective-permute-done((bf16[384,384]{1,0:T(8,128)(2,1)S(1)}, bf16[384,384]{1,0:T(8,128)(2,1)S(1)}, u32[]{:S(2)}, u32[]{:S(2)}) %collective-permute-start.40) | collective-permute-done | bytes 294944 | tf_op jit(solution)/shard_map/ppermute | solution.py:23
  147.0 10.4 %collective-permute-done.43 = bf16[384,384]{1,0:T(8,128)(2,1)S(1)} collective-permute-done((bf16[384,384]{1,0:T(8,128)(2,1)S(1)}, bf16[384,384]{1,0:T(8,128)(2,1)S(1)}, u32[]{:S(2)}, u32[]{:S(2)}) %collective-permute-start.43) | collective-permute-done | bytes 294944 | tf_op jit(solution)/shard_map/ppermute | solution.py:23
  157.4 2.0 %collective-permute-start.26 = (bf16[512,384]{1,0:T(8,128)(2,1)S(1)}, bf16[512,384]{1,0:T(8,128)(2,1)S(1)}, u32[]{:S(2)}, u32[]{:S(2)}) collective-permute-start(bf16[512,384]{1,0:T(8,128)(2,1)S(1)} %copy-done.22), channel_id=1, source_target_pairs={{0,12},{4,8},{8,4},{12,0},{1,13},{5,9},{9,5},{13,1},{2,14},{6,10},... | collective-permute-start | bytes 1179656 | tf_op jit(solution)/shard_map/ppermute | solution.py:23
  162.4 2.2 %collective-permute-done.18 = bf16[512,384]{1,0:T(8,128)(2,1)S(1)} collective-permute-done((bf16[512,384]{1,0:T(8,128)(2,1)S(1)}, bf16[512,384]{1,0:T(8,128)(2,1)S(1)}, u32[]{:S(2)}, u32[]{:S(2)}) %collective-permute-start.18) | collective-permute-done | bytes 393248 | tf_op jit(solution)/shard_map/ppermute | solution.py:23
  165.5 3.7 %collective-permute-done.26 = bf16[512,384]{1,0:T(8,128)(2,1)S(1)} collective-permute-done((bf16[512,384]{1,0:T(8,128)(2,1)S(1)}, bf16[512,384]{1,0:T(8,128)(2,1)S(1)}, u32[]{:S(2)}, u32[]{:S(2)}) %collective-permute-start.26) | collective-permute-done | bytes 393248 | tf_op jit(solution)/shard_map/ppermute | solution.py:23
  169.2 22.8 %collective-permute-done.25 = bf16[512,384]{1,0:T(8,128)(2,1)S(1)} collective-permute-done((bf16[512,384]{1,0:T(8,128)(2,1)S(1)}, bf16[512,384]{1,0:T(8,128)(2,1)S(1)}, u32[]{:S(2)}, u32[]{:S(2)}) %collective-permute-start.25) | collective-permute-done | bytes 393248 | tf_op jit(solution)/shard_map/ppermute | solution.py:23
  (154 shorter events, 39.8 us)
Async XLA Ops:
  0.7 44.9 %collective-permute-start.17 = (bf16[512,384]{1,0:T(8,128)(2,1)}, bf16[512,384]{1,0:T(8,128)(2,1)S(1)}, u32[]{:S(2)}, u32[]{:S(2)}) collective-permute-start(bf16[512,384]{1,0:T(8,128)(2,1)} %param.4), channel_id=1, source_target_pairs={{0,12},{4,8},{8,4},{12,0},{1,13},{5,9},{9,5},{13,1},{2,14},{6,10},... | collective-permute-start | bytes 1179656 | tf_op jit(solution)/shard_map/ppermute | solution.py:23
  11.9 34.4 %collective-permute-start.15 = (bf16[512,384]{1,0:T(8,128)(2,1)}, bf16[512,384]{1,0:T(8,128)(2,1)S(1)}, u32[]{:S(2)}, u32[]{:S(2)}) collective-permute-start(bf16[512,384]{1,0:T(8,128)(2,1)} %param.4), channel_id=1, source_target_pairs={{0,4},{4,0},{8,12},{12,8},{1,5},{5,1},{9,13},{13,9},{2,6},{6,2},{1... | collective-permute-start | bytes 1179656 | tf_op jit(solution)/shard_map/ppermute | solution.py:23
  13.1 34.5 %collective-permute-start.16 = (bf16[512,384]{1,0:T(8,128)(2,1)S(1)}, bf16[512,384]{1,0:T(8,128)(2,1)S(1)}, u32[]{:S(2)}, u32[]{:S(2)}) collective-permute-start(bf16[512,384]{1,0:T(8,128)(2,1)S(1)} %copy-done.23), channel_id=1, source_target_pairs={{0,8},{4,12},{8,0},{12,4},{1,9},{5,13},{9,1},{13,5},{2,10},{6,14},... | collective-permute-start | bytes 1179656 | tf_op jit(solution)/shard_map/ppermute | solution.py:23
  15.3 12.3 %collective-permute-start = (bf16[384,384]{1,0:T(8,128)(2,1)S(1)}, bf16[384,384]{1,0:T(8,128)(2,1)S(1)}, u32[]{:S(2)}, u32[]{:S(2)}) collective-permute-start(bf16[384,384]{1,0:T(8,128)(2,1)S(1)} %get-tuple-element.48), channel_id=1, source_target_pairs={{0,0},{1,1},{2,16},{3,17},{16,18},{17,19},{18,2},{19,3},{4,4},{5,5... | collective-permute-start | bytes 884744 | tf_op jit(solution)/shard_map/ppermute | solution.py:23
  18.1 22.0 %collective-permute-start.1 = (bf16[384,384]{1,0:T(8,128)(2,1)S(1)}, bf16[384,384]{1,0:T(8,128)(2,1)S(1)}, u32[]{:S(2)}, u32[]{:S(2)}) collective-permute-start(bf16[384,384]{1,0:T(8,128)(2,1)S(1)} %get-tuple-element.47), channel_id=1, source_target_pairs={{0,1},{1,0},{2,17},{3,16},{16,19},{17,18},{18,3},{19,2},{4,5},{5,4... | collective-permute-start | bytes 884744 | tf_op jit(solution)/shard_map/ppermute | solution.py:23
  41.1 9.6 %collective-permute-start.21 = (bf16[512,384]{1,0:T(8,128)(2,1)S(1)}, bf16[512,384]{1,0:T(8,128)(2,1)S(1)}, u32[]{:S(2)}, u32[]{:S(2)}) collective-permute-start(bf16[512,384]{1,0:T(8,128)(2,1)S(1)} %copy-done), channel_id=1, source_target_pairs={{0,1},{1,0},{2,3},{3,2},{4,5},{5,4},{6,7},{7,6},{8,9},{9,8},{10,11... | collective-permute-start | bytes 1179656 | tf_op jit(solution)/shard_map/ppermute | solution.py:23
  42.6 17.4 %collective-permute-start.22 = (bf16[512,384]{1,0:T(8,128)(2,1)S(1)}, bf16[512,384]{1,0:T(8,128)(2,1)S(1)}, u32[]{:S(2)}, u32[]{:S(2)}) collective-permute-start(bf16[512,384]{1,0:T(8,128)(2,1)S(1)} %copy-done), channel_id=1, source_target_pairs={{0,2},{1,3},{2,0},{3,1},{4,6},{5,7},{6,4},{7,5},{8,10},{9,11},{10,... | collective-permute-start | bytes 1179656 | tf_op jit(solution)/shard_map/ppermute | solution.py:23
  45.5 15.3 %collective-permute-start.23 = (bf16[512,384]{1,0:T(8,128)(2,1)S(1)}, bf16[512,384]{1,0:T(8,128)(2,1)S(1)}, u32[]{:S(2)}, u32[]{:S(2)}) collective-permute-start(bf16[512,384]{1,0:T(8,128)(2,1)S(1)} %copy-done), channel_id=1, source_target_pairs={{0,3},{1,2},{2,1},{3,0},{4,7},{5,6},{6,5},{7,4},{8,11},{9,10},{10,... | collective-permute-start | bytes 1179656 | tf_op jit(solution)/shard_map/ppermute | solution.py:23
  46.3 23.2 %collective-permute-start.2 = (bf16[384,768]{1,0:T(8,128)(2,1)S(1)}, bf16[384,768]{1,0:T(8,128)(2,1)S(1)}, u32[]{:S(2)}, u32[]{:S(2)}) collective-permute-start(bf16[384,768]{1,0:T(8,128)(2,1)S(1)} %constant_dynamic-update-slice_fusion.refs_0_), channel_id=1, source_target_pairs={{0,32},{32,0},{64,96},{96,64},{1,33},{33,1},{65,97},{97,65},{2,34}... | collective-permute-start | bytes 1769480 | tf_op jit(solution)/shard_map/ppermute | solution.py:23
  47.6 24.6 %collective-permute-start.3 = (bf16[384,768]{1,0:T(8,128)(2,1)S(1)}, bf16[384,768]{1,0:T(8,128)(2,1)S(1)}, u32[]{:S(2)}, u32[]{:S(2)}) collective-permute-start(bf16[384,768]{1,0:T(8,128)(2,1)S(1)} %constant_dynamic-update-slice_fusion.refs_0_), channel_id=1, source_target_pairs={{0,64},{32,96},{64,0},{96,32},{1,65},{33,97},{65,1},{97,33},{2,66}... | collective-permute-start | bytes 1769480 | tf_op jit(solution)/shard_map/ppermute | solution.py:23
  50.7 26.3 %collective-permute-start.4 = (bf16[384,768]{1,0:T(8,128)(2,1)S(1)}, bf16[384,768]{1,0:T(8,128)(2,1)S(1)}, u32[]{:S(2)}, u32[]{:S(2)}) collective-permute-start(bf16[384,768]{1,0:T(8,128)(2,1)S(1)} %constant_dynamic-update-slice_fusion.refs_0_), channel_id=1, source_target_pairs={{0,96},{32,64},{64,32},{96,0},{1,97},{33,65},{65,33},{97,1},{2,98}... | collective-permute-start | bytes 1769480 | tf_op jit(solution)/shard_map/ppermute | solution.py:23
  63.2 17.1 %collective-permute-start.33 = (bf16[384,768]{1,0:T(8,128)(2,1)S(1)}, bf16[384,768]{1,0:T(8,128)(2,1)S(1)}, u32[]{:S(2)}, u32[]{:S(2)}) collective-permute-start(bf16[384,768]{1,0:T(8,128)(2,1)S(1)} %get-tuple-element.31), channel_id=1, source_target_pairs={{0,16},{16,0},{1,17},{17,1},{2,18},{18,2},{3,19},{19,3},{4,20},{20... | collective-permute-start | bytes 1769480 | tf_op jit(solution)/shard_map/ppermute | solution.py:23
  69.4 11.1 %collective-permute-start.34 = (bf16[384,768]{1,0:T(8,128)(2,1)S(1)}, bf16[384,768]{1,0:T(8,128)(2,1)S(1)}, u32[]{:S(2)}, u32[]{:S(2)}) collective-permute-start(bf16[384,768]{1,0:T(8,128)(2,1)S(1)} %get-tuple-element.32), channel_id=1, source_target_pairs={{0,16},{16,0},{1,17},{17,1},{2,18},{18,2},{3,19},{19,3},{4,20},{20... | collective-permute-start | bytes 1769480 | tf_op jit(solution)/shard_map/ppermute | solution.py:23
  69.5 11.4 %collective-permute-start.35 = (bf16[384,768]{1,0:T(8,128)(2,1)S(1)}, bf16[384,768]{1,0:T(8,128)(2,1)S(1)}, u32[]{:S(2)}, u32[]{:S(2)}) collective-permute-start(bf16[384,768]{1,0:T(8,128)(2,1)S(1)} %get-tuple-element.33), channel_id=1, source_target_pairs={{0,16},{16,0},{1,17},{17,1},{2,18},{18,2},{3,19},{19,3},{4,20},{20... | collective-permute-start | bytes 1769480 | tf_op jit(solution)/shard_map/ppermute | solution.py:23
  84.1 34.4 %collective-permute-start.39 = (bf16[384,768]{1,0:T(8,128)(2,1)}, bf16[384,768]{1,0:T(8,128)(2,1)}, u32[]{:S(2)}, u32[]{:S(2)}) collective-permute-start(bf16[384,768]{1,0:T(8,128)(2,1)} %get-tuple-element.38), channel_id=1, source_target_pairs={{0,96},{32,64},{64,32},{96,0},{1,97},{33,65},{65,33},{97,1},{2,98}... | collective-permute-start | bytes 1769480 | tf_op jit(solution)/shard_map/ppermute | solution.py:23
  84.9 34.4 %collective-permute-start.38 = (bf16[384,768]{1,0:T(8,128)(2,1)}, bf16[384,768]{1,0:T(8,128)(2,1)}, u32[]{:S(2)}, u32[]{:S(2)}) collective-permute-start(bf16[384,768]{1,0:T(8,128)(2,1)} %get-tuple-element.37), channel_id=1, source_target_pairs={{0,64},{32,96},{64,0},{96,32},{1,65},{33,97},{65,1},{97,33},{2,66}... | collective-permute-start | bytes 1769480 | tf_op jit(solution)/shard_map/ppermute | solution.py:23
  85.0 35.7 %collective-permute-start.37 = (bf16[384,768]{1,0:T(8,128)(2,1)}, bf16[384,768]{1,0:T(8,128)(2,1)}, u32[]{:S(2)}, u32[]{:S(2)}) collective-permute-start(bf16[384,768]{1,0:T(8,128)(2,1)} %get-tuple-element.36), channel_id=1, source_target_pairs={{0,32},{32,0},{64,96},{96,64},{1,33},{33,1},{65,97},{97,65},{2,34}... | collective-permute-start | bytes 1769480 | tf_op jit(solution)/shard_map/ppermute | solution.py:23
  98.2 16.4 %collective-permute-start.27 = (f32[2,512]{1,0:T(2,128)}, f32[2,512]{1,0:T(2,128)S(1)}, u32[]{:S(2)}, u32[]{:S(2)}) collective-permute-start(f32[2,512]{1,0:T(2,128)} %slice.75), channel_id=1, source_target_pairs={{0,1},{1,0},{2,3},{3,2},{4,5},{5,4},{6,7},{7,6},{8,9},{9,8},{10,11... | collective-permute-start | bytes 12296 | tf_op jit(solution)/shard_map/ppermute | solution.py:23
  100.6 15.9 %collective-permute-start.28 = (f32[2,512]{1,0:T(2,128)}, f32[2,512]{1,0:T(2,128)S(1)}, u32[]{:S(2)}, u32[]{:S(2)}) collective-permute-start(f32[2,512]{1,0:T(2,128)} %slice.75), channel_id=1, source_target_pairs={{0,2},{1,3},{2,0},{3,1},{4,6},{5,7},{6,4},{7,5},{8,10},{9,11},{10,... | collective-permute-start | bytes 12296 | tf_op jit(solution)/shard_map/ppermute | solution.py:23
  114.7 45.0 %collective-permute-start.20 = (bf16[512,384]{1,0:T(8,128)(2,1)S(1)}, bf16[512,384]{1,0:T(8,128)(2,1)S(1)}, u32[]{:S(2)}, u32[]{:S(2)}) collective-permute-start(bf16[512,384]{1,0:T(8,128)(2,1)S(1)} %get-tuple-element.24), channel_id=1, source_target_pairs={{0,3},{1,2},{2,1},{3,0},{4,7},{5,6},{6,5},{7,4},{8,11},{9,10},{10,... | collective-permute-start | bytes 1179656 | tf_op jit(solution)/shard_map/ppermute | solution.py:23
  117.1 16.0 %collective-permute-start.32 = (f32[2,512]{1,0:T(2,128)S(1)}, f32[2,512]{1,0:T(2,128)S(1)}, u32[]{:S(2)}, u32[]{:S(2)}) collective-permute-start(f32[2,512]{1,0:T(2,128)S(1)} %add_add_fusion.1), channel_id=1, source_target_pairs={{0,12},{4,8},{8,4},{12,0},{1,13},{5,9},{9,5},{13,1},{2,14},{6,10},... | collective-permute-start | bytes 12296 | tf_op jit(solution)/shard_map/ppermute | solution.py:23
  118.5 16.5 %collective-permute-start.30 = (f32[2,512]{1,0:T(2,128)S(1)}, f32[2,512]{1,0:T(2,128)S(1)}, u32[]{:S(2)}, u32[]{:S(2)}) collective-permute-start(f32[2,512]{1,0:T(2,128)S(1)} %add_add_fusion.1), channel_id=1, source_target_pairs={{0,4},{4,0},{8,12},{12,8},{1,5},{5,1},{9,13},{13,9},{2,6},{6,2},{1... | collective-permute-start | bytes 12296 | tf_op jit(solution)/shard_map/ppermute | solution.py:23
  119.3 15.8 %collective-permute-start.31 = (f32[2,512]{1,0:T(2,128)S(1)}, f32[2,512]{1,0:T(2,128)S(1)}, u32[]{:S(2)}, u32[]{:S(2)}) collective-permute-start(f32[2,512]{1,0:T(2,128)S(1)} %add_add_fusion.1), channel_id=1, source_target_pairs={{0,8},{4,12},{8,0},{12,4},{1,9},{5,13},{9,1},{13,5},{2,10},{6,14},... | collective-permute-start | bytes 12296 | tf_op jit(solution)/shard_map/ppermute | solution.py:23
  122.5 18.8 %collective-permute-start.41 = (bf16[384,384]{1,0:T(8,128)(2,1)S(1)}, bf16[384,384]{1,0:T(8,128)(2,1)S(1)}, u32[]{:S(2)}, u32[]{:S(2)}) collective-permute-start(bf16[384,384]{1,0:T(8,128)(2,1)S(1)} %get-tuple-element.46), channel_id=1, source_target_pairs={{0,128},{1,129},{2,146},{3,147},{16,130},{17,131},{18,144},{19,145... | collective-permute-start | bytes 884744 | tf_op jit(solution)/shard_map/ppermute | solution.py:23
  133.1 13.8 %collective-permute-start.40 = (bf16[384,384]{1,0:T(8,128)(2,1)S(1)}, bf16[384,384]{1,0:T(8,128)(2,1)S(1)}, u32[]{:S(2)}, u32[]{:S(2)}) collective-permute-start(bf16[384,384]{1,0:T(8,128)(2,1)S(1)} %get-tuple-element.46), channel_id=1, source_target_pairs={{0,0},{1,1},{2,18},{3,19},{16,2},{17,3},{18,16},{19,17},{128,128},... | collective-permute-start | bytes 884744 | tf_op jit(solution)/shard_map/ppermute | solution.py:23
  135.1 22.3 %collective-permute-start.43 = (bf16[384,384]{1,0:T(8,128)(2,1)S(1)}, bf16[384,384]{1,0:T(8,128)(2,1)S(1)}, u32[]{:S(2)}, u32[]{:S(2)}) collective-permute-start(bf16[384,384]{1,0:T(8,128)(2,1)S(1)} %get-tuple-element.45), channel_id=1, source_target_pairs={{0,129},{1,128},{2,147},{3,146},{16,131},{17,130},{18,145},{19,144... | collective-permute-start | bytes 884744 | tf_op jit(solution)/shard_map/ppermute | solution.py:23
  135.2 24.2 %collective-permute-start.42 = (bf16[384,384]{1,0:T(8,128)(2,1)S(1)}, bf16[384,384]{1,0:T(8,128)(2,1)S(1)}, u32[]{:S(2)}, u32[]{:S(2)}) collective-permute-start(bf16[384,384]{1,0:T(8,128)(2,1)S(1)} %get-tuple-element.45), channel_id=1, source_target_pairs={{0,1},{1,0},{2,19},{3,18},{16,3},{17,2},{18,17},{19,16},{128,129},... | collective-permute-start | bytes 884744 | tf_op jit(solution)/shard_map/ppermute | solution.py:23
  141.2 21.1 %collective-permute-start.19 = (bf16[512,384]{1,0:T(8,128)(2,1)S(1)}, bf16[512,384]{1,0:T(8,128)(2,1)S(1)}, u32[]{:S(2)}, u32[]{:S(2)}) collective-permute-start(bf16[512,384]{1,0:T(8,128)(2,1)S(1)} %get-tuple-element.23), channel_id=1, source_target_pairs={{0,2},{1,3},{2,0},{3,1},{4,6},{5,7},{6,4},{7,5},{8,10},{9,11},{10,... | collective-permute-start | bytes 1179656 | tf_op jit(solution)/shard_map/ppermute | solution.py:23
  147.0 17.6 %collective-permute-start.18 = (bf16[512,384]{1,0:T(8,128)(2,1)S(1)}, bf16[512,384]{1,0:T(8,128)(2,1)S(1)}, u32[]{:S(2)}, u32[]{:S(2)}) collective-permute-start(bf16[512,384]{1,0:T(8,128)(2,1)S(1)} %get-tuple-element.22), channel_id=1, source_target_pairs={{0,1},{1,0},{2,3},{3,2},{4,5},{5,4},{6,7},{7,6},{8,9},{9,8},{10,11... | collective-permute-start | bytes 1179656 | tf_op jit(solution)/shard_map/ppermute | solution.py:23
  157.4 11.8 %collective-permute-start.26 = (bf16[512,384]{1,0:T(8,128)(2,1)S(1)}, bf16[512,384]{1,0:T(8,128)(2,1)S(1)}, u32[]{:S(2)}, u32[]{:S(2)}) collective-permute-start(bf16[512,384]{1,0:T(8,128)(2,1)S(1)} %copy-done.22), channel_id=1, source_target_pairs={{0,12},{4,8},{8,4},{12,0},{1,13},{5,9},{9,5},{13,1},{2,14},{6,10},... | collective-permute-start | bytes 1179656 | tf_op jit(solution)/shard_map/ppermute | solution.py:23
  159.4 32.6 %collective-permute-start.25 = (bf16[512,384]{1,0:T(8,128)(2,1)S(1)}, bf16[512,384]{1,0:T(8,128)(2,1)S(1)}, u32[]{:S(2)}, u32[]{:S(2)}) collective-permute-start(bf16[512,384]{1,0:T(8,128)(2,1)S(1)} %copy-done.20), channel_id=1, source_target_pairs={{0,8},{4,12},{8,0},{12,4},{1,9},{5,13},{9,1},{13,5},{2,10},{6,14},... | collective-permute-start | bytes 1179656 | tf_op jit(solution)/shard_map/ppermute | solution.py:23
  160.3 31.6 %collective-permute-start.24 = (bf16[512,384]{1,0:T(8,128)(2,1)S(1)}, bf16[512,384]{1,0:T(8,128)(2,1)S(1)}, u32[]{:S(2)}, u32[]{:S(2)}) collective-permute-start(bf16[512,384]{1,0:T(8,128)(2,1)S(1)} %copy-done.18), channel_id=1, source_target_pairs={{0,4},{4,0},{8,12},{12,8},{1,5},{5,1},{9,13},{13,9},{2,6},{6,2},{1... | collective-permute-start | bytes 1179656 | tf_op jit(solution)/shard_map/ppermute | solution.py:23
  (43 other events, 451.4 us)

commit v2 on v1

v2 whole, which is shorter than its diff:
```python
import itertools

import jax
import jax.numpy as jnp
from jax import lax
from jax.experimental import pallas as pl
from jax.experimental.pallas import tpu as pltpu
from jax.sharding import Mesh, PartitionSpec as P

AXES = ("dp", "x", "c", "z", "y")
SIZES = dict(dp=2, x=4, c=2, z=4, y=4)
T = 512
F = 384
VMEM_LIMIT = 60 * 1024 * 1024
F32 = jnp.float32
BF16 = jnp.bfloat16


def send(value, axes, to):
    coords = list(itertools.product(*(range(SIZES[a]) for a in axes)))
    flat = {c: i for i, c in enumerate(coords)}
    perm = [(flat[c], flat[tuple(to(*c))]) for c in coords]
    return lax.ppermute(value, axes if len(axes) > 1 else axes[0], perm)


def swap(value, axis, e):
    return send(value, (axis,), lambda i: (i ^ e,))


def dot_nt(a, b):
    return lax.dot_general(a, b, (((1,), (1,)), ((), ())), preferred_element_type=F32)


def dot_nn(a, b):
    return lax.dot_general(a, b, (((1,), (0,)), ((), ())), preferred_element_type=F32)


def load_all(copies):
    for c in copies:
        c.start()


def lanes(e, width=F):
    return pl.ds(e * width, width)


def call(kernel, out_shape, scratch, cost, n_any, n_vmem):
    def outer(*args):
        return pl.pallas_call(
            kernel,
            out_shape=out_shape,
            in_specs=[pl.BlockSpec(memory_space=pl.ANY)] * n_any
            + [pl.BlockSpec(memory_space=pltpu.VMEM)] * n_vmem,
            out_specs=jax.tree.map(lambda _: pl.BlockSpec(memory_space=pltpu.VMEM), out_shape),
            scratch_shapes=scratch,
            compiler_params=pltpu.CompilerParams(vmem_limit_bytes=VMEM_LIMIT),
            cost_estimate=pl.CostEstimate(flops=cost, bytes_accessed=cost, transcendentals=0),
        )(*args)

    return outer


def cot_copies(cots, cbuf, sems, first):
    y = lax.axis_index("y")
    return [
        pltpu.make_async_copy(cots.at[y ^ e], cbuf.at[e // 2, :, lanes(e % 2)], sems.at[first + e])
        for e in range(4)
    ]


def gw_other_kernel(*refs):
    normed, cots = refs[0:4], refs[4]
    outs, turned = refs[5:9], refs[9]
    nbuf, cbuf, sems = refs[10:]
    x, c, z = lax.axis_index("x"), lax.axis_index("c"), lax.axis_index("z")
    copies = [pltpu.make_async_copy(normed[e], nbuf.at[z ^ e], sems.at[e]) for e in range(4)]
    copies += cot_copies(cots, cbuf, sems, 4)
    load_all(copies)
    for cp in copies:
        cp.wait()
    for e in range(4):
        row = x ^ e
        nt = nbuf[row].T
        turned[e] = nt
        outs[e][...] = dot_nn(nt, cbuf[1 - c]).astype(BF16)


def gw_own_kernel(*refs):
    turned, cots, other = refs[0], refs[1], refs[2:6]
    outs = refs[6:10]
    tbuf, cbuf, obuf, sems = refs[10:]
    c = lax.axis_index("c")
    copies = [pltpu.make_async_copy(turned, tbuf, sems.at[0])]
    copies += cot_copies(cots, cbuf, sems, 1)
    copies += [pltpu.make_async_copy(other[e], obuf.at[e], sems.at[5 + e]) for e in range(4)]
    load_all(copies)
    for cp in copies:
        cp.wait()
    for e in range(4):
        total = dot_nn(tbuf[e], cbuf[c]) + obuf[e].astype(F32)
        outs[e][...] = total.astype(outs[e].dtype)


def weight_copies(mine, theirs, wbuf, sems, first, x, c):
    copies = []
    for e in range(4):
        copies.append(pltpu.make_async_copy(mine[e], wbuf.at[x ^ e, c], sems.at[first + 2 * e]))
        copies.append(
            pltpu.make_async_copy(theirs[e], wbuf.at[x ^ e, 1 - c], sems.at[first + 2 * e + 1])
        )
    return copies


def back_kernel(*refs):
    mine, theirs, cots = refs[0:4], refs[4:8], refs[8]
    outs = refs[9:13]
    wbuf, cbuf, sems = refs[13:]
    x, c, z = lax.axis_index("x"), lax.axis_index("c"), lax.axis_index("z")
    copies = weight_copies(mine, theirs, wbuf, sems, 0, x, c)
    copies += cot_copies(cots, cbuf, sems, 8)
    load_all(copies)
    for cp in copies:
        cp.wait()
    for e in (3, 2, 1, 0):
        rows = z ^ e
        part = dot_nt(cbuf[0], wbuf[rows, 0]) + dot_nt(cbuf[1], wbuf[rows, 1])
        outs[e][...] = part.astype(outs[e].dtype)


def sums_kernel(*refs):
    parts, normed, gains, sums = refs[0:4], refs[4:8], refs[8], refs[9]
    first = jnp.zeros((T, 1), F32)
    second = jnp.zeros((T, 1), F32)
    for e in range(4):
        part = parts[e][...].astype(F32)
        first = first + jnp.sum(part * gains[e : e + 1, :], axis=1, keepdims=True)
        second = second + jnp.sum(part * normed[e][...].astype(F32), axis=1, keepdims=True)
    lane = lax.broadcasted_iota(jnp.int32, (T, 128), 1)
    both = jnp.where(lane == 0, first, second)
    sums[...] = both.T[:8]


def query_kernel(*refs):
    mine, theirs, normed = refs[0:4], refs[4:8], refs[8:12]
    out = refs[12]
    wbuf, nbuf, sems = refs[13:]
    x, c, z, y = (lax.axis_index(a) for a in "xczy")
    copies = weight_copies(mine, theirs, wbuf, sems, 0, x, c)
    copies += [pltpu.make_async_copy(normed[e], nbuf.at[z ^ e], sems.at[8 + e]) for e in range(4)]
    load_all(copies)
    for cp in copies:
        cp.wait()
    for half in range(2):
        part = dot_nn(nbuf[0], wbuf[0, half])
        for k in range(1, 4):
            part = part + dot_nn(nbuf[k], wbuf[k, half])
        for a in range(2):
            out[y ^ (2 * half + a)] = part[:, a * F : (a + 1) * F].astype(BF16)


def shape(*dims, dtype=BF16):
    return jax.ShapeDtypeStruct(dims, dtype)


def after(value, dep):
    return lax.optimization_barrier((value, dep))


def merge(a, b, count):
    gap = a[0] - b[0]
    return jnp.stack([0.5 * (a[0] + b[0]), a[1] + b[1] + (0.5 * count) * gap * gap])


def on_device(tokens, gain, w, cot):
    z, y = lax.axis_index("z"), lax.axis_index("y")
    odd = y % 2

    def to_a(s, yy):
        return ((yy >> 1) ^ s, 2 * s + (yy & 1))

    def to_b(s, yy):
        return ((yy >> 1) ^ s, 2 * s + 1 - (yy & 1))

    wa = send(lax.dynamic_slice(w, (odd * F, 0), (F, F)), ("c", "y"), to_a)
    wb = send(lax.dynamic_slice(w, ((1 - odd) * F, 0), (F, F)), ("c", "y"), to_b)
    values = tokens.astype(F32)
    own_mean = jnp.sum(values, axis=1) / F
    centred = values - own_mean[:, None]
    stat = jnp.stack([own_mean, jnp.sum(centred * centred, axis=1)])
    stat = merge(stat, swap(stat, "y", 1), F)
    stat = merge(stat, swap(stat, "y", 2), 2 * F)

    tok1, tok2 = swap(tokens, "z", 1), swap(tokens, "z", 2)
    tok = [tokens, tok1, tok2, swap(tok2, "z", 1)]

    cot, wa, wb, stat = lax.optimization_barrier((cot, wa, wb, stat))
    cots = lax.all_to_all(jnp.broadcast_to(cot, (4, T, F)), "y", 0, 0, tiled=True)

    w0 = jnp.concatenate([wa, wb], axis=1)
    w1 = swap(w0, "x", 1)
    w3 = swap(w0, "x", 3)
    w_mine = [w0, w1, swap(w0, "x", 2), w3]
    w_theirs = [swap(m, "c", 1) for m in w_mine]

    packet = jnp.concatenate([stat.reshape(-1), gain])
    other = swap(packet, "z", 1)
    stat = merge(stat, other[: 2 * T].reshape(2, T), 4 * F)
    packet = jnp.concatenate([stat.reshape(-1), gain, other[2 * T :]])
    other2 = swap(packet, "z", 2)
    stat = merge(stat, other2[: 2 * T].reshape(2, T), 8 * F)
    gains = [gain, other[2 * T :], other2[2 * T : 2 * T + F], other2[2 * T + F :]]

    width = 16 * F
    inverse = lax.rsqrt(stat[1] / width + 1e-06)[:, None]
    mean = stat[0][:, None]

    def standardize(block):
        return (block.astype(F32) - mean) * inverse

    normed = [(standardize(b) * g[None, :]).astype(BF16) for b, g in zip(tok, gains)]

    dma = pltpu.SemaphoreType.DMA
    gw = call(
        gw_other_kernel,
        [shape(F, 2 * F)] * 4 + [shape(4, F, T)],
        [pltpu.VMEM((4, T, F), BF16), pltpu.VMEM((2, T, 2 * F), BF16), dma((8,))],
        1,
        5,
        0,
    )(*normed, cots)
    turned = gw[4]
    gw_theirs = [swap(g, "c", 1) for g in gw[:4]]

    w_theirs, turned = after(w_theirs, turned)
    back = call(
        back_kernel,
        [shape(T, F, dtype=F32)] + [shape(T, F)] * 3,
        [pltpu.VMEM((4, 2, F, 2 * F), BF16), pltpu.VMEM((2, T, 2 * F), BF16), dma((12,))],
        40_000_000,
        9,
        0,
    )(*w_mine, *w_theirs, cots)
    turned, back = after(turned, back)
    gw_sum = call(
        gw_own_kernel,
        [shape(F, 2 * F, dtype=F32)] + [shape(F, 2 * F)] * 3,
        [
            pltpu.VMEM((4, F, T), BF16),
            pltpu.VMEM((2, T, 2 * F), BF16),
            pltpu.VMEM((4, F, 2 * F), BF16),
            dma((9,)),
        ],
        1,
        6,
        0,
    )(turned, cots, *gw_theirs)
    relay = swap(back[3], "z", 1)
    grad1 = swap(back[1], "z", 1)
    relay, gw_sum = after(relay, gw_sum)
    message = (back[2].astype(F32) + relay.astype(F32)).astype(BF16)
    normed, message, gw_sum = lax.optimization_barrier((normed, message, gw_sum))
    grad2 = swap(message, "z", 2)
    grad_parts = [back[0], grad1, grad2]

    gw_parts = [gw_sum[0]] + [swap(gw_sum[e], "x", e) for e in (1, 2, 3)]

    sums = call(sums_kernel, shape(8, T, dtype=F32), [], 1, 0, 9)(
        *back, *normed, jnp.stack(gains)
    )[:2]
    sums = lax.all_to_all(jnp.broadcast_to(sums, (16, 2, T)), ("z", "y"), 0, 0, tiled=True)
    sums = jnp.sum(sums, axis=0)

    query_out = call(
        query_kernel,
        shape(4, T, F),
        [pltpu.VMEM((4, 2, F, 2 * F), BF16), pltpu.VMEM((4, T, F), BF16), dma((12,))],
        1,
        12,
        0,
    )(*w_mine, *w_theirs, *normed)
    block = sum(p.astype(F32) for p in gw_parts).astype(BF16)

    def home(a):
        return lambda d, cc, yy: (d, yy >> 1, yy ^ (2 * cc + a))

    def away(a):
        return lambda d, cc, yy: (1 - d, yy >> 1, yy ^ (2 * cc + a))

    block, grad_parts, sums, query_out = lax.optimization_barrier((block, grad_parts, sums, query_out))
    halves = [block[:, :F], block[:, F:]]
    far = [send(halves[a], ("dp", "c", "y"), away(a)) for a in (0, 1)]
    near = [send(halves[a], ("dp", "c", "y"), home(a)) for a in (0, 1)]

    query_parts = lax.all_to_all(query_out, "y", 0, 0, tiled=True)

    got_a, got_b = (n.astype(F32) + f.astype(F32) for n, f in zip(near, far))
    even = odd == 0
    grad_w = jnp.concatenate([jnp.where(even, got_a, got_b), jnp.where(even, got_b, got_a)])

    first, second = sums[0][:, None] / width, sums[1][:, None] / width
    grad_hat = sum(p.astype(F32) for p in grad_parts) * gain[None, :]
    token_gradient = ((grad_hat - first - standardize(tokens) * second) * inverse).astype(BF16)
    query = jnp.sum(query_parts.astype(F32), axis=0).astype(BF16)
    return query, token_gradient, grad_w


def solution(mesh):
    fine = Mesh(mesh.devices.reshape([SIZES[a] for a in AXES]), AXES)
    rows, cols = ("dp", "x", "c"), ("z", "y")
    in_specs = (P(rows, cols), P(cols), P(("x", "c"), cols), P(rows, cols))
    out_specs = (P(rows, cols), P(rows, cols), P(("x", "c"), cols))
    return jax.shard_map(
        on_device, mesh=fine, in_specs=in_specs, out_specs=out_specs, check_vma=False
    )
```

time: 194 us -> 161 us (0.83)
  waiting for transfers between devices: 73.5 us -> 46.6 us
  starting transfers between devices: 79.6 us -> 63.7 us
  Pallas kernels: 16.7 us -> 27.6 us
  local copies, waits for them, and re-layouts: 13.5 us -> 7.46 us
  other arithmetic: 8.74 us -> 13.4 us
    ppermute x44 -> x30, starting transfers between devices: 79.6 us -> 50.6 us  [send(): return lax.ppermute(value, axes if len(axes) > 1 else axes[0], perm)]
    ppermute x44 -> x30, waiting for transfers between devices: 73.5 us -> 46.6 us  [send(): return lax.ppermute(value, axes if len(axes) > 1 else axes[0], perm)]
    all_to_all x0 -> x3, starting transfers between devices: none -> 13.1 us  [the longest x1 4.84 us: on_device(): lax.all_to_all(jnp.broadcast_to(sums, (16, 2, T)), ('z', 'y'), 0, 0, tile...]
    pallas_call x4 -> x5, Pallas kernels: 16.7 us -> 27.6 us  [outer(): pl.pallas_call(kernel, out_shape=out_shape, in_specs=[pl.BlockSpec(memory...]
    unnamed x63 -> x39, local copies, waits for them, and re-layouts: 11.6 us -> 3.34 us
    convert_element_type x1, other arithmetic: 0.55 us -> 2.69 us  [on_device(): (standardize(b) * g[None, :]).astype(BF16)]
    broadcast_in_dim x0 -> x2, local copies, waits for them, and re-layouts: none -> 1.96 us  [the longest x1 1.32 us: on_device(): jnp.broadcast_to(cot, (4, T, F))]
  transfers between devices with their start and end apart: 44 -> 33, of which waited for: 15 -> 10; matrix products, arithmetic and copies ran while one was open for 5% -> 8% of each run, Pallas kernels for 9% -> 17%
where the time goes in v2:
time: 161 us; the launch traced here: 160 us
  starting transfers between devices  63.7 us (40%)
  waiting for transfers between devices  46.6 us (29%)
  Pallas kernels  27.6 us (17%)
  other arithmetic  13.4 us (8%)
  local copies, waits for them, and re-layouts  7.46 us (5%)
    ppermute x30, starting transfers between devices, send(): return lax.ppermute(value, axes if len(axes) > 1 else axes[0], perm)  50.6 us
    ppermute x30, waiting for transfers between devices, send(): return lax.ppermute(value, axes if len(axes) > 1 else axes[0], perm)  46.6 us
    pallas_call x5, Pallas kernels, outer(): pl.pallas_call(kernel, out_shape=out_shape, in_specs=[pl.BlockSpec(memory...  27.6 us
    all_to_all x1, starting transfers between devices, on_device(): lax.all_to_all(jnp.broadcast_to(sums, (16, 2, T)), ('z', 'y'), 0, 0, tile...  4.84 us
    all_to_all x1, starting transfers between devices, on_device(): query_parts = lax.all_to_all(query_out, 'y', 0, 0, tiled=True)  4.15 us
    all_to_all x1, starting transfers between devices, on_device(): lax.all_to_all(jnp.broadcast_to(cot, (4, T, F)), 'y', 0, 0, tiled=True)  4.12 us
    unnamed x39, local copies, waits for them, and re-layouts  3.34 us
  transfers between devices with their start and end apart: 33, of which 10 were waited for; matrix products, arithmetic and copies ran while one was open for 8% of the time, Pallas kernels for 17%

profile of v2, /device:TPU:1, one launch (start us, length us, event | category | flops | bytes accessed | tf_op | source)
XLA Modules:
  0.0 159.8 jit_solution(12692787197727957429)
XLA Ops:
  3.1 2.2 %collective-permute-start.2 = (f32[2,512]{1,0:T(2,128)S(1)}, f32[2,512]{1,0:T(2,128)S(1)}, u32[]{:S(2)}, u32[]{:S(2)}) collective-permute-start(f32[2,512]{1,0:T(2,128)S(1)} %pad_maximum_fusion.4), channel_id=1, source_target_pairs={{0,1},{1,0},{2,3},{3,2},{4,5},{5,4},{6,7},{7,6},{8,9},{9,8},{10,11... | collective-permute-start | bytes 12296 | tf_op jit(solution)/shard_map/ppermute | solution.py:23
  5.3 3.0 %collective-permute-start.7 = (bf16[512,384]{1,0:T(8,128)(2,1)}, bf16[512,384]{1,0:T(8,128)(2,1)S(1)}, u32[]{:S(2)}, u32[]{:S(2)}) collective-permute-start(bf16[512,384]{1,0:T(8,128)(2,1)} %param.4), channel_id=1, source_target_pairs={{0,8},{4,12},{8,0},{12,4},{1,9},{5,13},{9,1},{13,5},{2,10},{6,14},... | collective-permute-start | bytes 1179656 | tf_op jit(solution)/shard_map/ppermute | solution.py:23
  8.3 1.6 %collective-permute-start.6 = (bf16[512,384]{1,0:T(8,128)(2,1)}, bf16[512,384]{1,0:T(8,128)(2,1)}, u32[]{:S(2)}, u32[]{:S(2)}) collective-permute-start(bf16[512,384]{1,0:T(8,128)(2,1)} %param.4), channel_id=1, source_target_pairs={{0,4},{4,0},{8,12},{12,8},{1,5},{5,1},{9,13},{13,9},{2,6},{6,2},{1... | collective-permute-start | bytes 1179656 | tf_op jit(solution)/shard_map/ppermute | solution.py:23
  10.0 2.7 %collective-permute-start.3 = (f32[2,512]{1,0:T(2,128)S(1)}, f32[2,512]{1,0:T(2,128)S(1)}, u32[]{:S(2)}, u32[]{:S(2)}) collective-permute-start(f32[2,512]{1,0:T(2,128)S(1)} %pad_maximum_fusion.5), channel_id=1, source_target_pairs={{0,2},{1,3},{2,0},{3,1},{4,6},{5,7},{6,4},{7,5},{8,10},{9,11},{10,... | collective-permute-start | bytes 12296 | tf_op jit(solution)/shard_map/ppermute | solution.py:23
  12.9 4.7 %collective-permute-start = (bf16[384,384]{1,0:T(8,128)(2,1)S(1)}, bf16[384,384]{1,0:T(8,128)(2,1)S(1)}, u32[]{:S(2)}, u32[]{:S(2)}) collective-permute-start(bf16[384,384]{1,0:T(8,128)(2,1)S(1)} %get-tuple-element.102), channel_id=1, source_target_pairs={{0,0},{1,1},{2,16},{3,17},{16,18},{17,19},{18,2},{19,3},{4,4},{5,5... | collective-permute-start | bytes 884744 | tf_op jit(solution)/shard_map/ppermute | solution.py:23
  17.6 5.9 %collective-permute-done.1 = bf16[384,384]{1,0:T(8,128)(2,1)S(1)} collective-permute-done((bf16[384,384]{1,0:T(8,128)(2,1)S(1)}, bf16[384,384]{1,0:T(8,128)(2,1)S(1)}, u32[]{:S(2)}, u32[]{:S(2)}) %collective-permute-start.1) | collective-permute-done | bytes 294944 | tf_op jit(solution)/shard_map/ppermute | solution.py:23
  24.3 2.6 %collective-permute-start.14 = (bf16[384,768]{1,0:T(8,128)(2,1)S(1)}, bf16[384,768]{1,0:T(8,128)(2,1)S(1)}, u32[]{:S(2)}, u32[]{:S(2)}) collective-permute-start(bf16[384,768]{1,0:T(8,128)(2,1)S(1)} %constant_dynamic-update-slice_fusion.refs_0_), channel_id=1, source_target_pairs={{0,96},{32,64},{64,32},{96,0},{1,97},{33,65},{65,33},{97,1},{2,98}... | collective-permute-start | bytes 1769480 | tf_op jit(solution)/shard_map/ppermute | solution.py:23
  28.7 4.1 %all-to-all-start = ((bf16[4,512,384]{2,1,0:T(8,128)(2,1)}), bf16[4,512,384]{2,1,0:T(8,128)(2,1)S(1)}, u32[]{:S(2)}, u32[]{:S(2)}) async-start(bf16[4,512,384]{2,1,0:T(8,128)(2,1)} %broadcast_in_dim.21), calls=%async_computation | async-start | bytes 3145728 | tf_op jit(solution)/shard_map/all_to_all | solution.py:197
  34.3 1.7 %collective-permute-start.5 = (f32[1792]{0:T(1024)S(1)}, f32[1792]{0:T(1024)S(1)}, u32[]{:S(2)}, u32[]{:S(2)}) collective-permute-start(f32[1792]{0:T(1024)S(1)} %pad_maximum_fusion.2), channel_id=1, source_target_pairs={{0,8},{4,12},{8,0},{12,4},{1,9},{5,13},{9,1},{13,5},{2,10},{6,14},... | collective-permute-start | bytes 21512 | tf_op jit(solution)/shard_map/ppermute | solution.py:23
  36.1 2.1 %collective-permute-done.5 = f32[1792]{0:T(1024)S(1)} collective-permute-done((f32[1792]{0:T(1024)S(1)}, f32[1792]{0:T(1024)S(1)}, u32[]{:S(2)}, u32[]{:S(2)}) %collective-permute-start.5) | collective-permute-done | bytes 7200 | tf_op jit(solution)/shard_map/ppermute | solution.py:23
  39.6 1.7 %collective-permute-start.8 = (bf16[512,384]{1,0:T(8,128)(2,1)S(1)}, bf16[512,384]{1,0:T(8,128)(2,1)S(1)}, u32[]{:S(2)}, u32[]{:S(2)}) collective-permute-start(bf16[512,384]{1,0:T(8,128)(2,1)S(1)} %collective-permute-done.7), channel_id=1, source_target_pairs={{0,4},{4,0},{8,12},{12,8},{1,5},{5,1},{9,13},{13,9},{2,6},{6,2},{1... | collective-permute-start | bytes 1179656 | tf_op jit(solution)/shard_map/ppermute | solution.py:23
  41.3 11.9 %collective-permute-done.14.refs_3_ = bf16[384,768]{1,0:T(8,128)(2,1)S(1)} collective-permute-done((bf16[384,768]{1,0:T(8,128)(2,1)S(1)}, bf16[384,768]{1,0:T(8,128)(2,1)S(1)}, u32[]{:S(2)}, u32[]{:S(2)}) %collective-permute-start.14) | collective-permute-done | bytes 589856 | tf_op jit(solution)/shard_map/ppermute | solution.py:23
  54.8 2.7 %multiply_convert_fusion = (bf16[512,384]{1,0:T(8,128)(2,1)}, bf16[512,384]{1,0:T(8,128)(2,1)}, bf16[512,384]{1,0:T(8,128)(2,1)}, bf16[512,384]{1,0:T(8,128)(2,1)}) fusion(bf16[512,384]{1,0:T(8,128)(2,1)S(1)} %collective-permute-done.8, f32[384]{0:T(512)S(1)} %get-tuple-element.107, f32[512]{0:T(512)S(1)} %get-tuple-element.104, ...), kind=kLoop, calls=%fused_computation.15 | loop fusion | flops 3932160 | bytes 3155968 | tf_op jit(solution)/shard_map/convert_element_type | solution.py:220
  58.7 4.7 %shard_map.67 = (bf16[384,768]{1,0:T(8,128)(2,1)}, bf16[384,768]{1,0:T(8,128)(2,1)}, bf16[384,768]{1,0:T(8,128)(2,1)}, bf16[384,768]{1,0:T(8,128)(2,1)}, bf16[4,384,512]{2,1,0:T(8,128)(2,1)}) custom-call(bf16[512,384]{1,0:T(8,128)(2,1)} %get-tuple-element.87.refs_0_.refs_4_.refs_8_, bf16[512,384]{1,0:T(8,128)(2,1)} %get-tuple-element.88.refs_1_.refs_5_.refs_9_, ...), custom_call_target="tpu_custom_call" | custom-call | flops 1 | bytes 1 | tf_op jit(solution)/shard_map/pallas_call | solution.py:49
  64.6 7.2 %shard_map.68 = (f32[512,384]{1,0:T(8,128)}, bf16[512,384]{1,0:T(8,128)(2,1)}, bf16[512,384]{1,0:T(8,128)(2,1)}, bf16[512,384]{1,0:T(8,128)(2,1)}) custom-call(bf16[384,768]{1,0:T(8,128)(2,1)} %copy-done.2, bf16[384,768]{1,0:T(8,128)(2,1)} %collective-permute-done.10.refs_1_, bf16[384,768]{1,0:T(8,128)(2,1)} %collective-permute-done.12.refs_2_, ...), custom_call_target="tpu_custom_call" | custom-call | flops 40000000 | bytes 40000000 | tf_op jit(solution)/shard_map/pallas_call | solution.py:49
  71.8 1.5 collective-permute-start.16
  75.5 4.8 %shard_map.69 = (f32[384,768]{1,0:T(8,128)}, bf16[384,768]{1,0:T(8,128)(2,1)}, bf16[384,768]{1,0:T(8,128)(2,1)}, bf16[384,768]{1,0:T(8,128)(2,1)}) custom-call(bf16[4,384,512]{2,1,0:T(8,128)(2,1)} %get-tuple-element.66.refs_0_, bf16[4,512,384]{2,1,0:T(8,128)(2,1)} %copy-done, bf16[384,768]{1,0:T(8,128)(2,1)} %copy-done.8, bf16[384,768]{1,0:T(8,128)(2,1)} %copy-done.9, ...), custom_call_target="tpu_custom_call" | custom-call | flops 1 | bytes 1 | tf_op jit(solution)/shard_map/pallas_call | solution.py:49
  80.3 2.3 %collective-permute-done.16 = bf16[512,384]{1,0:T(8,128)(2,1)S(1)} collective-permute-done((bf16[512,384]{1,0:T(8,128)(2,1)}, bf16[512,384]{1,0:T(8,128)(2,1)S(1)}, u32[]{:S(2)}, u32[]{:S(2)}) %collective-permute-start.16) | collective-permute-done | bytes 393248 | tf_op jit(solution)/shard_map/ppermute | solution.py:23
  84.5 2.7 %collective-permute-start.22 = (bf16[384,768]{1,0:T(8,128)(2,1)}, bf16[384,768]{1,0:T(8,128)(2,1)S(1)}, u32[]{:S(2)}, u32[]{:S(2)}) collective-permute-start(bf16[384,768]{1,0:T(8,128)(2,1)} %get-tuple-element.82), channel_id=1, source_target_pairs={{0,64},{32,96},{64,0},{96,32},{1,65},{33,97},{65,1},{97,33},{2,66}... | collective-permute-start | bytes 1769480 | tf_op jit(solution)/shard_map/ppermute | solution.py:23
  87.9 3.3 %shard_map.70 = f32[8,512]{1,0:T(8,128)} custom-call(f32[512,384]{1,0:T(8,128)} %get-tuple-element.92.refs_0_, bf16[512,384]{1,0:T(8,128)(2,1)} %get-tuple-element.85.refs_1_, bf16[512,384]{1,0:T(8,128)(2,1)} %get-tuple-element.64.refs_2_, bf16[512,384]{1,0:T(8,128)(2,1)} %get-tuple-element.65.refs_3_, ...), custom_call_target="tpu_custom_call" | custom-call | flops 1 | bytes 1 | tf_op jit(solution)/shard_map/pallas_call | solution.py:49
  92.6 4.8 %all-to-all-start.1 = ((f32[16,2,512]{2,1,0:T(2,128)}), f32[16,2,512]{2,1,0:T(2,128)S(1)}, u32[]{:S(2)}, u32[]{:S(2)}) async-start(f32[16,2,512]{2,1,0:T(2,128)} %broadcast_in_dim.26), calls=%async_computation.1 | async-start | bytes 131072 | tf_op jit(solution)/shard_map/all_to_all | solution.py:270
  98.8 2.1 %collective-permute-start.25 = (bf16[512,384]{1,0:T(8,128)(2,1)}, bf16[512,384]{1,0:T(8,128)(2,1)}, u32[]{:S(2)}, u32[]{:S(2)}) collective-permute-start(bf16[512,384]{1,0:T(8,128)(2,1)} %add_convert_fusion.1), channel_id=1, source_target_pairs={{0,8},{4,12},{8,0},{12,4},{1,9},{5,13},{9,1},{13,5},{2,10},{6,14},... | collective-permute-start | bytes 1179656 | tf_op jit(solution)/shard_map/ppermute | solution.py:23
  100.9 7.6 %shard_map.71 = bf16[4,512,384]{2,1,0:T(8,128)(2,1)} custom-call(bf16[384,768]{1,0:T(8,128)(2,1)} %copy-done.2, bf16[384,768]{1,0:T(8,128)(2,1)} %collective-permute-done.10.refs_1_, bf16[384,768]{1,0:T(8,128)(2,1)} %collective-permute-done.12.refs_2_, bf16[384,768]{1,0:T(8,128)(2,1)} %copy-done.4, bf16[384,768]{1,0:T(8,128)(2,1)} %collective-permute-done.9.refs_4_, ...), custom_call_target="tpu_custom_call" | custom-call | flops 1 | bytes 1 | tf_op jit(solution)/shard_map/pallas_call | solution.py:49
  108.5 3.8 %collective-permute-done.22 = bf16[384,768]{1,0:T(8,128)(2,1)S(1)} collective-permute-done((bf16[384,768]{1,0:T(8,128)(2,1)}, bf16[384,768]{1,0:T(8,128)(2,1)S(1)}, u32[]{:S(2)}, u32[]{:S(2)}) %collective-permute-start.22) | collective-permute-done | bytes 589856 | tf_op jit(solution)/shard_map/ppermute | solution.py:23
  112.3 2.2 %collective-permute-done.23 = bf16[384,768]{1,0:T(8,128)(2,1)} collective-permute-done((bf16[384,768]{1,0:T(8,128)(2,1)}, bf16[384,768]{1,0:T(8,128)(2,1)}, u32[]{:S(2)}, u32[]{:S(2)}) %collective-permute-start.23) | collective-permute-done | bytes 589856 | tf_op jit(solution)/shard_map/ppermute | solution.py:23
  116.1 4.1 %all-to-all-start.2 = ((bf16[4,512,384]{2,1,0:T(8,128)(2,1)}), bf16[4,512,384]{2,1,0:T(8,128)(2,1)S(1)}, u32[]{:S(2)}, u32[]{:S(2)}) async-start(bf16[4,512,384]{2,1,0:T(8,128)(2,1)} %shard_map.71), calls=%async_computation.2 | async-start | bytes 3145728 | tf_op jit(solution)/shard_map/all_to_all | solution.py:294
  120.3 12.2 %collective-permute-start.29 = (bf16[384,384]{1,0:T(8,128)(2,1)S(1)}, bf16[384,384]{1,0:T(8,128)(2,1)S(1)}, u32[]{:S(2)}, u32[]{:S(2)}) collective-permute-start(bf16[384,384]{1,0:T(8,128)(2,1)S(1)} %get-tuple-element.99), channel_id=1, source_target_pairs={{0,129},{1,128},{2,147},{3,146},{16,131},{17,130},{18,145},{19,144... | collective-permute-start | bytes 884744 | tf_op jit(solution)/shard_map/ppermute | solution.py:23
  132.9 4.0 %collective-permute-start.26 = (bf16[384,384]{1,0:T(8,128)(2,1)S(1)}, bf16[384,384]{1,0:T(8,128)(2,1)S(1)}, u32[]{:S(2)}, u32[]{:S(2)}) collective-permute-start(bf16[384,384]{1,0:T(8,128)(2,1)S(1)} %get-tuple-element.100), channel_id=1, source_target_pairs={{0,0},{1,1},{2,18},{3,19},{16,2},{17,3},{18,16},{19,17},{128,128},... | collective-permute-start | bytes 884744 | tf_op jit(solution)/shard_map/ppermute | solution.py:23
  137.0 2.3 %fusion.8 = bf16[512,384]{1,0:T(8,128)(2,1)} fusion(bf16[512,384]{1,0:T(8,128)(2,1)S(1)} %copy-done.1, bf16[512,384]{1,0:T(8,128)(2,1)} %collective-permute-done.25, f32[512,384]{1,0:T(8,128)S(1)} %copy-done.3, bf16[512,384]{1,0:T(8,128)(2,1)} %collective-permute-done.24, f32[512]{0:T(512)S(1)} %bitcast.25, f32[512]{0:T(512)S(1)} %bitcast.24, ...), kind=kLoop, calls=%fused_computation.13 | loop fusion | flops 2555904 | bytes 2369024 | tf_op jit(solution)/shard_map/convert_element_type | solution.py:302
  139.3 5.5 %collective-permute-done.29 = bf16[384,384]{1,0:T(8,128)(2,1)S(1)} collective-permute-done((bf16[384,384]{1,0:T(8,128)(2,1)S(1)}, bf16[384,384]{1,0:T(8,128)(2,1)S(1)}, u32[]{:S(2)}, u32[]{:S(2)}) %collective-permute-start.29) | collective-permute-done | bytes 294944 | tf_op jit(solution)/shard_map/ppermute | solution.py:23
  144.8 8.7 %collective-permute-done.28 = bf16[384,384]{1,0:T(8,128)(2,1)S(1)} collective-permute-done((bf16[384,384]{1,0:T(8,128)(2,1)S(1)}, bf16[384,384]{1,0:T(8,128)(2,1)S(1)}, u32[]{:S(2)}, u32[]{:S(2)}) %collective-permute-start.28) | collective-permute-done | bytes 294944 | tf_op jit(solution)/shard_map/ppermute | solution.py:23
  153.5 3.9 %collective-permute-done.27 = bf16[384,384]{1,0:T(8,128)(2,1)S(1)} collective-permute-done((bf16[384,384]{1,0:T(8,128)(2,1)S(1)}, bf16[384,384]{1,0:T(8,128)(2,1)S(1)}, u32[]{:S(2)}, u32[]{:S(2)}) %collective-permute-start.27) | collective-permute-done | bytes 294944 | tf_op jit(solution)/shard_map/ppermute | solution.py:23
  (114 shorter events, 24.2 us)
Async XLA Ops:
  3.1 6.8 %collective-permute-start.2 = (f32[2,512]{1,0:T(2,128)S(1)}, f32[2,512]{1,0:T(2,128)S(1)}, u32[]{:S(2)}, u32[]{:S(2)}) collective-permute-start(f32[2,512]{1,0:T(2,128)S(1)} %pad_maximum_fusion.4), channel_id=1, source_target_pairs={{0,1},{1,0},{2,3},{3,2},{4,5},{5,4},{6,7},{7,6},{8,9},{9,8},{10,11... | collective-permute-start | bytes 12296 | tf_op jit(solution)/shard_map/ppermute | solution.py:23
  5.3 33.1 %collective-permute-start.7 = (bf16[512,384]{1,0:T(8,128)(2,1)}, bf16[512,384]{1,0:T(8,128)(2,1)S(1)}, u32[]{:S(2)}, u32[]{:S(2)}) collective-permute-start(bf16[512,384]{1,0:T(8,128)(2,1)} %param.4), channel_id=1, source_target_pairs={{0,8},{4,12},{8,0},{12,4},{1,9},{5,13},{9,1},{13,5},{2,10},{6,14},... | collective-permute-start | bytes 1179656 | tf_op jit(solution)/shard_map/ppermute | solution.py:23
  8.3 31.3 %collective-permute-start.6 = (bf16[512,384]{1,0:T(8,128)(2,1)}, bf16[512,384]{1,0:T(8,128)(2,1)}, u32[]{:S(2)}, u32[]{:S(2)}) collective-permute-start(bf16[512,384]{1,0:T(8,128)(2,1)} %param.4), channel_id=1, source_target_pairs={{0,4},{4,0},{8,12},{12,8},{1,5},{5,1},{9,13},{13,9},{2,6},{6,2},{1... | collective-permute-start | bytes 1179656 | tf_op jit(solution)/shard_map/ppermute | solution.py:23
  10.0 7.6 %collective-permute-start.3 = (f32[2,512]{1,0:T(2,128)S(1)}, f32[2,512]{1,0:T(2,128)S(1)}, u32[]{:S(2)}, u32[]{:S(2)}) collective-permute-start(f32[2,512]{1,0:T(2,128)S(1)} %pad_maximum_fusion.5), channel_id=1, source_target_pairs={{0,2},{1,3},{2,0},{3,1},{4,6},{5,7},{6,4},{7,5},{8,10},{9,11},{10,... | collective-permute-start | bytes 12296 | tf_op jit(solution)/shard_map/ppermute | solution.py:23
  12.8 10.7 %collective-permute-start.1 = (bf16[384,384]{1,0:T(8,128)(2,1)S(1)}, bf16[384,384]{1,0:T(8,128)(2,1)S(1)}, u32[]{:S(2)}, u32[]{:S(2)}) collective-permute-start(bf16[384,384]{1,0:T(8,128)(2,1)S(1)} %get-tuple-element.101), channel_id=1, source_target_pairs={{0,1},{1,0},{2,17},{3,16},{16,19},{17,18},{18,3},{19,2},{4,5},{5,4... | collective-permute-start | bytes 884744 | tf_op jit(solution)/shard_map/ppermute | solution.py:23
  12.9 10.6 %collective-permute-start = (bf16[384,384]{1,0:T(8,128)(2,1)S(1)}, bf16[384,384]{1,0:T(8,128)(2,1)S(1)}, u32[]{:S(2)}, u32[]{:S(2)}) collective-permute-start(bf16[384,384]{1,0:T(8,128)(2,1)S(1)} %get-tuple-element.102), channel_id=1, source_target_pairs={{0,0},{1,1},{2,16},{3,17},{16,18},{17,19},{18,2},{19,3},{4,4},{5,5... | collective-permute-start | bytes 884744 | tf_op jit(solution)/shard_map/ppermute | solution.py:23
  24.1 8.7 %collective-permute-start.4 = (f32[1408]{0:T(1024)S(1)}, f32[1408]{0:T(1024)}, u32[]{:S(2)}, u32[]{:S(2)}) collective-permute-start(f32[1408]{0:T(1024)S(1)} %pad_maximum_fusion.1), channel_id=1, source_target_pairs={{0,4},{4,0},{8,12},{12,8},{1,5},{5,1},{9,13},{13,9},{2,6},{6,2},{1... | collective-permute-start | bytes 16904 | tf_op jit(solution)/shard_map/ppermute | solution.py:23
  24.3 28.9 %collective-permute-start.14 = (bf16[384,768]{1,0:T(8,128)(2,1)S(1)}, bf16[384,768]{1,0:T(8,128)(2,1)S(1)}, u32[]{:S(2)}, u32[]{:S(2)}) collective-permute-start(bf16[384,768]{1,0:T(8,128)(2,1)S(1)} %constant_dynamic-update-slice_fusion.refs_0_), channel_id=1, source_target_pairs={{0,96},{32,64},{64,32},{96,0},{1,97},{33,65},{65,33},{97,1},{2,98}... | collective-permute-start | bytes 1769480 | tf_op jit(solution)/shard_map/ppermute | solution.py:23
  26.9 27.1 %collective-permute-start.12 = (bf16[384,768]{1,0:T(8,128)(2,1)S(1)}, bf16[384,768]{1,0:T(8,128)(2,1)}, u32[]{:S(2)}, u32[]{:S(2)}) collective-permute-start(bf16[384,768]{1,0:T(8,128)(2,1)S(1)} %constant_dynamic-update-slice_fusion.refs_0_), channel_id=1, source_target_pairs={{0,64},{32,96},{64,0},{96,32},{1,65},{33,97},{65,1},{97,33},{2,66}... | collective-permute-start | bytes 1769480 | tf_op jit(solution)/shard_map/ppermute | solution.py:23
  28.7 28.7 %all-to-all-start = ((bf16[4,512,384]{2,1,0:T(8,128)(2,1)}), bf16[4,512,384]{2,1,0:T(8,128)(2,1)S(1)}, u32[]{:S(2)}, u32[]{:S(2)}) async-start(bf16[4,512,384]{2,1,0:T(8,128)(2,1)} %broadcast_in_dim.21), calls=%async_computation | async-start | bytes 3145728 | tf_op jit(solution)/shard_map/all_to_all | solution.py:197
  38.1 16.0 %collective-permute-start.10 = (bf16[384,768]{1,0:T(8,128)(2,1)S(1)}, bf16[384,768]{1,0:T(8,128)(2,1)}, u32[]{:S(2)}, u32[]{:S(2)}) collective-permute-start(bf16[384,768]{1,0:T(8,128)(2,1)S(1)} %constant_dynamic-update-slice_fusion.refs_0_), channel_id=1, source_target_pairs={{0,32},{32,0},{64,96},{96,64},{1,33},{33,1},{65,97},{97,65},{2,34}... | collective-permute-start | bytes 1769480 | tf_op jit(solution)/shard_map/ppermute | solution.py:23
  38.4 25.4 %collective-permute-start.9 = (bf16[384,768]{1,0:T(8,128)(2,1)S(1)}, bf16[384,768]{1,0:T(8,128)(2,1)}, u32[]{:S(2)}, u32[]{:S(2)}) collective-permute-start(bf16[384,768]{1,0:T(8,128)(2,1)S(1)} %constant_dynamic-update-slice_fusion.refs_0_), channel_id=1, source_target_pairs={{0,16},{16,0},{1,17},{17,1},{2,18},{18,2},{3,19},{19,3},{4,20},{20... | collective-permute-start | bytes 1769480 | tf_op jit(solution)/shard_map/ppermute | solution.py:23
  39.6 15.1 %collective-permute-start.8 = (bf16[512,384]{1,0:T(8,128)(2,1)S(1)}, bf16[512,384]{1,0:T(8,128)(2,1)S(1)}, u32[]{:S(2)}, u32[]{:S(2)}) collective-permute-start(bf16[512,384]{1,0:T(8,128)(2,1)S(1)} %collective-permute-done.7), channel_id=1, source_target_pairs={{0,4},{4,0},{8,12},{12,8},{1,5},{5,1},{9,13},{13,9},{2,6},{6,2},{1... | collective-permute-start | bytes 1179656 | tf_op jit(solution)/shard_map/ppermute | solution.py:23
  53.2 10.9 %collective-permute-start.15 = (bf16[384,768]{1,0:T(8,128)(2,1)S(1)}, bf16[384,768]{1,0:T(8,128)(2,1)}, u32[]{:S(2)}, u32[]{:S(2)}) collective-permute-start(bf16[384,768]{1,0:T(8,128)(2,1)S(1)} %collective-permute-done.14.refs_3_), channel_id=1, source_target_pairs={{0,16},{16,0},{1,17},{17,1},{2,18},{18,2},{3,19},{19,3},{4,20},{20... | collective-permute-start | bytes 1769480 | tf_op jit(solution)/shard_map/ppermute | solution.py:23
  54.0 10.3 %collective-permute-start.13 = (bf16[384,768]{1,0:T(8,128)(2,1)}, bf16[384,768]{1,0:T(8,128)(2,1)}, u32[]{:S(2)}, u32[]{:S(2)}) collective-permute-start(bf16[384,768]{1,0:T(8,128)(2,1)} %collective-permute-done.12.refs_2_), channel_id=1, source_target_pairs={{0,16},{16,0},{1,17},{17,1},{2,18},{18,2},{3,19},{19,3},{4,20},{20... | collective-permute-start | bytes 1769480 | tf_op jit(solution)/shard_map/ppermute | solution.py:23
  54.1 10.4 %collective-permute-start.11 = (bf16[384,768]{1,0:T(8,128)(2,1)}, bf16[384,768]{1,0:T(8,128)(2,1)}, u32[]{:S(2)}, u32[]{:S(2)}) collective-permute-start(bf16[384,768]{1,0:T(8,128)(2,1)} %collective-permute-done.10.refs_1_), channel_id=1, source_target_pairs={{0,16},{16,0},{1,17},{17,1},{2,18},{18,2},{3,19},{19,3},{4,20},{20... | collective-permute-start | bytes 1769480 | tf_op jit(solution)/shard_map/ppermute | solution.py:23
  63.3 10.0 %collective-permute-start.17 = (bf16[384,768]{1,0:T(8,128)(2,1)}, bf16[384,768]{1,0:T(8,128)(2,1)S(1)}, u32[]{:S(2)}, u32[]{:S(2)}) collective-permute-start(bf16[384,768]{1,0:T(8,128)(2,1)} %get-tuple-element.67), channel_id=1, source_target_pairs={{0,16},{16,0},{1,17},{17,1},{2,18},{18,2},{3,19},{19,3},{4,20},{20... | collective-permute-start | bytes 1769480 | tf_op jit(solution)/shard_map/ppermute | solution.py:23
  63.8 9.6 %collective-permute-start.18 = (bf16[384,768]{1,0:T(8,128)(2,1)}, bf16[384,768]{1,0:T(8,128)(2,1)S(1)}, u32[]{:S(2)}, u32[]{:S(2)}) collective-permute-start(bf16[384,768]{1,0:T(8,128)(2,1)} %get-tuple-element.68), channel_id=1, source_target_pairs={{0,16},{16,0},{1,17},{17,1},{2,18},{18,2},{3,19},{19,3},{4,20},{20... | collective-permute-start | bytes 1769480 | tf_op jit(solution)/shard_map/ppermute | solution.py:23
  64.1 9.3 %collective-permute-start.19 = (bf16[384,768]{1,0:T(8,128)(2,1)}, bf16[384,768]{1,0:T(8,128)(2,1)S(1)}, u32[]{:S(2)}, u32[]{:S(2)}) collective-permute-start(bf16[384,768]{1,0:T(8,128)(2,1)} %get-tuple-element.69), channel_id=1, source_target_pairs={{0,16},{16,0},{1,17},{17,1},{2,18},{18,2},{3,19},{19,3},{4,20},{20... | collective-permute-start | bytes 1769480 | tf_op jit(solution)/shard_map/ppermute | solution.py:23
  64.3 9.1 %collective-permute-start.20 = (bf16[384,768]{1,0:T(8,128)(2,1)}, bf16[384,768]{1,0:T(8,128)(2,1)S(1)}, u32[]{:S(2)}, u32[]{:S(2)}) collective-permute-start(bf16[384,768]{1,0:T(8,128)(2,1)} %get-tuple-element.70), channel_id=1, source_target_pairs={{0,16},{16,0},{1,17},{17,1},{2,18},{18,2},{3,19},{19,3},{4,20},{20... | collective-permute-start | bytes 1769480 | tf_op jit(solution)/shard_map/ppermute | solution.py:23
  71.8 10.8 %collective-permute-start.16 = (bf16[512,384]{1,0:T(8,128)(2,1)}, bf16[512,384]{1,0:T(8,128)(2,1)S(1)}, u32[]{:S(2)}, u32[]{:S(2)}) collective-permute-start(bf16[512,384]{1,0:T(8,128)(2,1)} %get-tuple-element.65.refs_3_), channel_id=1, source_target_pairs={{0,4},{4,0},{8,12},{12,8},{1,5},{5,1},{9,13},{13,9},{2,6},{6,2},{1... | collective-permute-start | bytes 1179656 | tf_op jit(solution)/shard_map/ppermute | solution.py:23
  83.4 25.1 %collective-permute-start.21 = (bf16[384,768]{1,0:T(8,128)(2,1)}, bf16[384,768]{1,0:T(8,128)(2,1)S(1)}, u32[]{:S(2)}, u32[]{:S(2)}) collective-permute-start(bf16[384,768]{1,0:T(8,128)(2,1)} %get-tuple-element.81), channel_id=1, source_target_pairs={{0,32},{32,0},{64,96},{96,64},{1,33},{33,1},{65,97},{97,65},{2,34}... | collective-permute-start | bytes 1769480 | tf_op jit(solution)/shard_map/ppermute | solution.py:23
  84.5 27.9 %collective-permute-start.22 = (bf16[384,768]{1,0:T(8,128)(2,1)}, bf16[384,768]{1,0:T(8,128)(2,1)S(1)}, u32[]{:S(2)}, u32[]{:S(2)}) collective-permute-start(bf16[384,768]{1,0:T(8,128)(2,1)} %get-tuple-element.82), channel_id=1, source_target_pairs={{0,64},{32,96},{64,0},{96,32},{1,65},{33,97},{65,1},{97,33},{2,66}... | collective-permute-start | bytes 1769480 | tf_op jit(solution)/shard_map/ppermute | solution.py:23
  87.1 27.4 %collective-permute-start.23 = (bf16[384,768]{1,0:T(8,128)(2,1)}, bf16[384,768]{1,0:T(8,128)(2,1)}, u32[]{:S(2)}, u32[]{:S(2)}) collective-permute-start(bf16[384,768]{1,0:T(8,128)(2,1)} %get-tuple-element.83), channel_id=1, source_target_pairs={{0,96},{32,64},{64,32},{96,0},{1,97},{33,65},{65,33},{97,1},{2,98}... | collective-permute-start | bytes 1769480 | tf_op jit(solution)/shard_map/ppermute | solution.py:23
  92.6 15.9 %all-to-all-start.1 = ((f32[16,2,512]{2,1,0:T(2,128)}), f32[16,2,512]{2,1,0:T(2,128)S(1)}, u32[]{:S(2)}, u32[]{:S(2)}) async-start(f32[16,2,512]{2,1,0:T(2,128)} %broadcast_in_dim.26), calls=%async_computation.1 | async-start | bytes 131072 | tf_op jit(solution)/shard_map/all_to_all | solution.py:270
  97.4 18.6 %collective-permute-start.24 = (bf16[512,384]{1,0:T(8,128)(2,1)}, bf16[512,384]{1,0:T(8,128)(2,1)}, u32[]{:S(2)}, u32[]{:S(2)}) collective-permute-start(bf16[512,384]{1,0:T(8,128)(2,1)} %get-tuple-element.85.refs_1_), channel_id=1, source_target_pairs={{0,4},{4,0},{8,12},{12,8},{1,5},{5,1},{9,13},{13,9},{2,6},{6,2},{1... | collective-permute-start | bytes 1179656 | tf_op jit(solution)/shard_map/ppermute | solution.py:23
  98.8 17.3 %collective-permute-start.25 = (bf16[512,384]{1,0:T(8,128)(2,1)}, bf16[512,384]{1,0:T(8,128)(2,1)}, u32[]{:S(2)}, u32[]{:S(2)}) collective-permute-start(bf16[512,384]{1,0:T(8,128)(2,1)} %add_convert_fusion.1), channel_id=1, source_target_pairs={{0,8},{4,12},{8,0},{12,4},{1,9},{5,13},{9,1},{13,5},{2,10},{6,14},... | collective-permute-start | bytes 1179656 | tf_op jit(solution)/shard_map/ppermute | solution.py:23
  116.1 42.7 %all-to-all-start.2 = ((bf16[4,512,384]{2,1,0:T(8,128)(2,1)}), bf16[4,512,384]{2,1,0:T(8,128)(2,1)S(1)}, u32[]{:S(2)}, u32[]{:S(2)}) async-start(bf16[4,512,384]{2,1,0:T(8,128)(2,1)} %shard_map.71), calls=%async_computation.2 | async-start | bytes 3145728 | tf_op jit(solution)/shard_map/all_to_all | solution.py:294
  120.3 24.5 %collective-permute-start.29 = (bf16[384,384]{1,0:T(8,128)(2,1)S(1)}, bf16[384,384]{1,0:T(8,128)(2,1)S(1)}, u32[]{:S(2)}, u32[]{:S(2)}) collective-permute-start(bf16[384,384]{1,0:T(8,128)(2,1)S(1)} %get-tuple-element.99), channel_id=1, source_target_pairs={{0,129},{1,128},{2,147},{3,146},{16,131},{17,130},{18,145},{19,144... | collective-permute-start | bytes 884744 | tf_op jit(solution)/shard_map/ppermute | solution.py:23
  132.4 21.1 %collective-permute-start.28 = (bf16[384,384]{1,0:T(8,128)(2,1)S(1)}, bf16[384,384]{1,0:T(8,128)(2,1)S(1)}, u32[]{:S(2)}, u32[]{:S(2)}) collective-permute-start(bf16[384,384]{1,0:T(8,128)(2,1)S(1)} %get-tuple-element.99), channel_id=1, source_target_pairs={{0,1},{1,0},{2,19},{3,18},{16,3},{17,2},{18,17},{19,16},{128,129},... | collective-permute-start | bytes 884744 | tf_op jit(solution)/shard_map/ppermute | solution.py:23
  132.4 25.0 %collective-permute-start.27 = (bf16[384,384]{1,0:T(8,128)(2,1)S(1)}, bf16[384,384]{1,0:T(8,128)(2,1)S(1)}, u32[]{:S(2)}, u32[]{:S(2)}) collective-permute-start(bf16[384,384]{1,0:T(8,128)(2,1)S(1)} %get-tuple-element.100), channel_id=1, source_target_pairs={{0,128},{1,129},{2,146},{3,147},{16,130},{17,131},{18,144},{19,145... | collective-permute-start | bytes 884744 | tf_op jit(solution)/shard_map/ppermute | solution.py:23
  132.9 24.5 %collective-permute-start.26 = (bf16[384,384]{1,0:T(8,128)(2,1)S(1)}, bf16[384,384]{1,0:T(8,128)(2,1)S(1)}, u32[]{:S(2)}, u32[]{:S(2)}) collective-permute-start(bf16[384,384]{1,0:T(8,128)(2,1)S(1)} %get-tuple-element.100), channel_id=1, source_target_pairs={{0,0},{1,1},{2,18},{3,19},{16,2},{17,3},{18,16},{19,17},{128,128},... | collective-permute-start | bytes 884744 | tf_op jit(solution)/shard_map/ppermute | solution.py:23
  (19 other events, 182.2 us)

commit v3 on v2

v3 whole, which is shorter than its diff:
```python
import functools
import itertools

import jax
import jax.numpy as jnp
from jax import lax
from jax.experimental import pallas as pl
from jax.experimental.pallas import tpu as pltpu
from jax.sharding import Mesh, PartitionSpec as P

AXES = ("dp", "x", "c", "z", "y")
SIZES = dict(dp=2, x=4, c=2, z=4, y=4)
T = 512
F = 384
MIB = 1024 * 1024
F32 = jnp.float32
BF16 = jnp.bfloat16


def send(value, axes, to):
    coords = list(itertools.product(*(range(SIZES[a]) for a in axes)))
    flat = {c: i for i, c in enumerate(coords)}
    perm = [(flat[c], flat[tuple(to(*c))]) for c in coords]
    return lax.ppermute(value, axes if len(axes) > 1 else axes[0], perm)


def swap(value, axis, e):
    return send(value, (axis,), lambda i: (i ^ e,))


def dot_nt(a, b):
    return lax.dot_general(a, b, (((1,), (1,)), ((), ())), preferred_element_type=F32)


def dot_nn(a, b):
    return lax.dot_general(a, b, (((1,), (0,)), ((), ())), preferred_element_type=F32)


def load_all(copies):
    for c in copies:
        c.start()


def lanes(e, width=F):
    return pl.ds(e * width, width)


def call(kernel, out_shape, scratch, cost, n_any, n_vmem, limit=10):
    def outer(*args):
        return pl.pallas_call(
            kernel,
            out_shape=out_shape,
            in_specs=[pl.BlockSpec(memory_space=pl.ANY)] * n_any
            + [pl.BlockSpec(memory_space=pltpu.VMEM)] * n_vmem,
            out_specs=jax.tree.map(lambda _: pl.BlockSpec(memory_space=pltpu.VMEM), out_shape),
            scratch_shapes=scratch,
            compiler_params=pltpu.CompilerParams(vmem_limit_bytes=limit * MIB),
            cost_estimate=pl.CostEstimate(flops=cost, bytes_accessed=cost, transcendentals=0),
        )(*args)

    return outer


def cot_copies(cots, cbuf, sems, first):
    y = lax.axis_index("y")
    return [
        pltpu.make_async_copy(cots.at[y ^ e], cbuf.at[e // 2, :, lanes(e % 2)], sems.at[first + e])
        for e in range(4)
    ]


def gw_other_kernel(*refs):
    normed, cots = refs[0:4], refs[4]
    out, turned = refs[5:7]
    nbuf, cbuf, sems = refs[7:]
    x, c, z = lax.axis_index("x"), lax.axis_index("c"), lax.axis_index("z")
    copies = [pltpu.make_async_copy(normed[e], nbuf.at[z ^ e], sems.at[e]) for e in range(4)]
    copies += cot_copies(cots, cbuf, sems, 4)
    load_all(copies)
    for cp in copies:
        cp.wait()
    for e in range(4):
        row = x ^ e
        nt = nbuf[row].T
        turned[e] = nt
        out[e] = dot_nn(nt, cbuf[1 - c]).astype(BF16)


def gw_own_kernel(*refs):
    cots, turned, other = refs[0:3]
    outs = refs[3:7]
    cbuf, sems = refs[7:]
    c, y = lax.axis_index("c"), lax.axis_index("y")
    copies = [
        pltpu.make_async_copy(cots.at[y ^ (2 * c + a)], cbuf.at[:, lanes(a)], sems.at[a])
        for a in range(2)
    ]
    load_all(copies)
    for cp in copies:
        cp.wait()
    for e in range(4):
        total = dot_nn(turned[e], cbuf[...]) + other[e].astype(F32)
        outs[e][...] = total.astype(outs[e].dtype)


def weight_copies(mine, theirs, wbuf, sems):
    x, c = lax.axis_index("x"), lax.axis_index("c")
    copies = []
    for e in range(4):
        rows = pl.ds(pl.multiple_of((x ^ e) * F, F), F)
        for half, part in ((c, mine[e]), (1 - c, theirs[e])):
            columns = pl.ds(pl.multiple_of(half * 2 * F, 2 * F), 2 * F)
            copies.append(
                pltpu.make_async_copy(part, wbuf.at[rows, columns], sems.at[x ^ e, half])
            )
    return copies


def write_rows(rows, sums):
    hi = sums.astype(BF16)
    rest = sums - hi.astype(F32)
    mid = rest.astype(BF16)
    low = (rest - mid.astype(F32)).astype(BF16)
    parts = jnp.concatenate([hi.astype(F32), mid.astype(F32), low.astype(F32)])
    tail = jnp.concatenate([parts[:, F:], jnp.zeros((6, 2 * F - T), F32)], axis=1)
    rows[...] = jnp.concatenate([parts[:, :F], tail, jnp.zeros((4, F), F32)]).astype(BF16)


def read_rows(rows):
    rows = rows.astype(F32)
    parts = jnp.concatenate([rows[:6], rows[6:12, : T - F]], axis=1)
    return parts[0:2] + parts[2:4] + parts[4:6]


def message_kernel(share, relay, sums, out, total):
    out[:T] = (share[...].astype(F32) + relay[:T].astype(F32)).astype(BF16)
    total[...] = sums[0:2] + read_rows(relay[T:])
    write_rows(out.at[T:], total[...])


def products_kernel(*refs):
    mine, theirs, cots, normed, gains = refs[0:4], refs[4:8], refs[8], refs[9:13], refs[13]
    outs, query, sums = refs[14:18], refs[18], refs[19]
    wbuf, cbuf, nbuf, wsems, csems, nsems = refs[20:]
    y, z = lax.axis_index("y"), lax.axis_index("z")
    columns = [
        pltpu.make_async_copy(cots.at[y ^ e], cbuf.at[:, lanes(e)], csems.at[e]) for e in range(4)
    ]
    load_all(columns)
    load_all(weight_copies(mine, theirs, wbuf, wsems))
    own = [pl.ds(pl.multiple_of((z ^ e) * F, F), F) for e in range(4)]
    features = [
        pltpu.make_async_copy(normed[e], nbuf.at[:, own[e]], nsems.at[e]) for e in range(4)
    ]
    load_all(features)
    for cp in columns + features:
        cp.wait()
    first = jnp.zeros((T, 1), F32)
    second = jnp.zeros((T, 1), F32)
    for e in (3, 2, 1, 0):
        for half in range(2):
            arrived = wbuf.at[own[e], lanes(half, 2 * F)]
            pltpu.make_async_copy(mine[0], arrived, wsems.at[z ^ e, half]).wait()
        part = dot_nt(cbuf[...], wbuf[own[e], :])
        first = first + jnp.sum(part * gains[e : e + 1, :], axis=1, keepdims=True)
        second = second + jnp.sum(part * nbuf[:, own[e]].astype(F32), axis=1, keepdims=True)
        outs[e][:T] = part.astype(outs[e].dtype)
    lane = lax.broadcasted_iota(jnp.int32, (T, 128), 1)
    sums[...] = jnp.where(lane == 0, first, second).T[:8]
    write_rows(outs[3].at[T:], sums[0:2])
    for half in range(2):
        part = dot_nn(nbuf[...], wbuf[:, lanes(half, 2 * F)])
        for a in range(2):
            query[y ^ (2 * half + a)] = part[:, a * F : (a + 1) * F].astype(BF16)


def shape(*dims, dtype=BF16):
    return jax.ShapeDtypeStruct(dims, dtype)


def after(value, dep):
    return lax.optimization_barrier((value, dep))


def merge(a, b, count):
    gap = a[0] - b[0]
    return jnp.stack([0.5 * (a[0] + b[0]), a[1] + b[1] + (0.5 * count) * gap * gap])


def on_device(tokens, gain, w, cot):
    z, y = lax.axis_index("z"), lax.axis_index("y")
    odd = y % 2

    def to_a(s, yy):
        return ((yy >> 1) ^ s, 2 * s + (yy & 1))

    def to_b(s, yy):
        return ((yy >> 1) ^ s, 2 * s + 1 - (yy & 1))

    wa = send(lax.dynamic_slice(w, (odd * F, 0), (F, F)), ("c", "y"), to_a)
    wb = send(lax.dynamic_slice(w, ((1 - odd) * F, 0), (F, F)), ("c", "y"), to_b)
    values = tokens.astype(F32)
    own_mean = jnp.sum(values, axis=1) / F
    centred = values - own_mean[:, None]
    stat = jnp.stack([own_mean, jnp.sum(centred * centred, axis=1)])
    stat = merge(stat, swap(stat, "y", 1), F)
    stat, wa, wb = lax.optimization_barrier((stat, wa, wb))
    stat = merge(stat, swap(stat, "y", 2), 2 * F)

    tok1, tok2 = swap(tokens, "z", 1), swap(tokens, "z", 2)
    tok2, tok1 = after(tok2, tok1)
    tok = [tokens, tok1, tok2, swap(tok2, "z", 1)]

    cot, wa, wb, stat = lax.optimization_barrier((cot, wa, wb, stat))
    cots = lax.all_to_all(jnp.broadcast_to(cot, (4, T, F)), "y", 0, 0, tiled=True)

    w0 = jnp.concatenate([wa, wb], axis=1)
    w1 = swap(w0, "x", 1)
    w3 = swap(w0, "x", 3)
    w_mine = [w0, w1, swap(w0, "x", 2), w3]
    stat, tok1 = after(stat, tok[1])
    packet = jnp.concatenate([stat.reshape(-1), gain])
    other = swap(packet, "z", 1)
    stat = merge(stat, other[: 2 * T].reshape(2, T), 4 * F)
    packet = jnp.concatenate([stat.reshape(-1), gain, other[2 * T :]])
    other2 = swap(packet, "z", 2)
    w_mine, tok[3], other2 = lax.optimization_barrier((w_mine, tok[3], other2))
    w_theirs = [swap(m, "c", 1) for m in w_mine]
    stat = merge(stat, other2[: 2 * T].reshape(2, T), 8 * F)
    gains = [gain, other[2 * T :], other2[2 * T : 2 * T + F], other2[2 * T + F :]]

    width = 16 * F
    inverse = lax.rsqrt(stat[1] / width + 1e-06)[:, None]
    mean = stat[0][:, None]

    def standardize(block):
        return (block.astype(F32) - mean) * inverse

    tok, w_theirs = after(tok, w_theirs)
    normed = [(standardize(b) * g[None, :]).astype(BF16) for b, g in zip(tok, gains)]

    dma = pltpu.SemaphoreType.DMA
    gw = call(
        gw_other_kernel,
        [shape(4, F, 2 * F), shape(4, F, T)],
        [pltpu.VMEM((4, T, F), BF16), pltpu.VMEM((2, T, 2 * F), BF16), dma((8,))],
        1,
        5,
        0,
    )(*normed, cots)
    turned = gw[1]
    gw_theirs = swap(gw[0], "c", 1)

    w_theirs, turned = after(w_theirs, turned)
    *back, query_out, sums = call(
        products_kernel,
        [shape(T, F, dtype=F32), shape(T, F), shape(T, F), shape(T + 16, F)]
        + [shape(4, T, F), shape(8, T, dtype=F32)],
        [
            pltpu.VMEM((4 * F, 4 * F), BF16),
            pltpu.VMEM((T, 4 * F), BF16),
            pltpu.VMEM((T, 4 * F), BF16),
            dma((4, 2)),
            dma((4,)),
            dma((4,)),
        ],
        40_000_000,
        13,
        1,
        15,
    )(*w_mine, *w_theirs, cots, *normed, jnp.stack(gains))
    turned, back = after(turned, back)
    gw_sum = call(
        gw_own_kernel,
        [shape(F, 2 * F, dtype=F32)] + [shape(F, 2 * F)] * 3,
        [pltpu.VMEM((T, 2 * F), BF16), dma((2,))],
        1,
        1,
        2,
    )(cots, turned, gw_theirs)
    gw_parts = [gw_sum[0]] + [swap(gw_sum[e], "x", e) for e in (1, 2, 3)]

    relay = swap(back[3], "z", 1)
    grad1 = swap(back[1], "z", 1)
    relay, gw_parts[0] = after(relay, gw_parts[0])
    query_out, relay = after(query_out, relay)
    message, sums = call(
        message_kernel, [shape(T + 16, F), shape(2, T, dtype=F32)], [], 1, 0, 3
    )(back[2], relay, sums)
    grad2 = swap(message, "z", 2)
    sums = sums + read_rows(grad2[T:])
    grad2 = grad2[:T]
    grad_parts = [back[0], grad1, grad2]


    block = sum(p.astype(F32) for p in gw_parts).astype(BF16)
    block, grad_parts[2] = after(block, grad_parts[2])
    blocks = [block[:, :F], block[:, F:]]

    def home(a):
        return lambda d, cc, yy: (d, yy >> 1, yy ^ (2 * cc + a))

    def away(a):
        return lambda d, cc, yy: (1 - d, yy >> 1, yy ^ (2 * cc + a))

    far = [send(blocks[a], ("dp", "c", "y"), away(a)) for a in (0, 1)]
    near = [send(blocks[a], ("dp", "c", "y"), home(a)) for a in (0, 1)]

    query_parts = lax.all_to_all(query_out, "y", 0, 0, tiled=True)

    query = jnp.sum(query_parts.astype(F32), axis=0).astype(BF16)
    far[1], query = after(far[1], query)
    sums, far = after(sums, far)
    sums = sums + sum(swap(sums, "y", e) for e in (1, 2, 3))
    got_a, got_b = (n.astype(F32) + f.astype(F32) for n, f in zip(near, far))
    even = odd == 0
    grad_w = jnp.concatenate([jnp.where(even, got_a, got_b), jnp.where(even, got_b, got_a)])
    first, second = sums[0][:, None] / width, sums[1][:, None] / width
    grad_hat = sum(p.astype(F32) for p in grad_parts) * gain[None, :]
    token_gradient = ((grad_hat - first - standardize(tokens) * second) * inverse).astype(BF16)
    return query, token_gradient, grad_w


def solution(mesh):
    fine = Mesh(mesh.devices.reshape([SIZES[a] for a in AXES]), AXES)
    rows, cols = ("dp", "x", "c"), ("z", "y")
    in_specs = (P(rows, cols), P(cols), P(("x", "c"), cols), P(rows, cols))
    out_specs = (P(rows, cols), P(rows, cols), P(("x", "c"), cols))
    return jax.shard_map(
        on_device, mesh=fine, in_specs=in_specs, out_specs=out_specs, check_vma=False
    )
```

time: 161 us -> 155 us (0.963)
  waiting for transfers between devices: 46.6 us -> 65.1 us
  Pallas kernels: 27.6 us -> 12.3 us
  starting transfers between devices: 63.7 us -> 53.2 us
  local copies, waits for them, and re-layouts: 7.46 us -> 9.14 us
    ppermute x30, waiting for transfers between devices: 46.6 us -> 65.1 us  [send(): return lax.ppermute(value, axes if len(axes) > 1 else axes[0], perm)]
    pallas_call x5 -> x4, Pallas kernels: 27.6 us -> 12.3 us  [outer(): pl.pallas_call(kernel, out_shape=out_shape, in_specs=[pl.BlockSpec(memory...]
    ppermute x30, starting transfers between devices: 50.6 us -> 45.2 us  [send(): return lax.ppermute(value, axes if len(axes) > 1 else axes[0], perm)]
    all_to_all x1 -> x0, starting transfers between devices: 4.84 us -> none  [on_device(): lax.all_to_all(jnp.broadcast_to(sums, (16, 2, T)), ('z', 'y'), 0, 0, tile...]
    unnamed x39 -> x49, local copies, waits for them, and re-layouts: 3.34 us -> 7.39 us
  transfers between devices with their start and end apart: 33 -> 32, of which waited for: 10 -> 14; matrix products, arithmetic and copies ran while one was open for 8% -> 6% of each run, Pallas kernels for 17% -> 6%
where the time goes in v3:
time: 155 us; the launch traced here: 153 us
  waiting for transfers between devices  65.1 us (42%)
  starting transfers between devices  53.2 us (34%)
  Pallas kernels  12.3 us (8%)
  other arithmetic  12.1 us (8%)
  local copies, waits for them, and re-layouts  9.14 us (6%)
    ppermute x30, waiting for transfers between devices, send(): return lax.ppermute(value, axes if len(axes) > 1 else axes[0], perm)  65.1 us
    ppermute x30, starting transfers between devices, send(): return lax.ppermute(value, axes if len(axes) > 1 else axes[0], perm)  45.2 us
    pallas_call x4, Pallas kernels, outer(): pl.pallas_call(kernel, out_shape=out_shape, in_specs=[pl.BlockSpec(memory...  12.3 us
    unnamed x49, local copies, waits for them, and re-layouts  7.39 us
    all_to_all x1, starting transfers between devices, on_device(): query_parts = lax.all_to_all(query_out, 'y', 0, 0, tiled=True)  4.35 us
    all_to_all x1, starting transfers between devices, on_device(): lax.all_to_all(jnp.broadcast_to(cot, (4, T, F)), 'y', 0, 0, tiled=True)  3.69 us
  transfers between devices with their start and end apart: 32, of which 14 were waited for; matrix products, arithmetic and copies ran while one was open for 6% of the time, Pallas kernels for 6%

profile of v3, /device:TPU:1, one launch (start us, length us, event | category | flops | bytes accessed | tf_op | source)
XLA Modules:
  0.0 152.9 jit_solution(5186994072760896920)
XLA Ops:
  3.1 2.2 %collective-permute-start.2 = (f32[2,512]{1,0:T(2,128)S(1)}, f32[2,512]{1,0:T(2,128)S(1)}, u32[]{:S(2)}, u32[]{:S(2)}) collective-permute-start(f32[2,512]{1,0:T(2,128)S(1)} %pad_maximum_fusion.5), channel_id=1, source_target_pairs={{0,1},{1,0},{2,3},{3,2},{4,5},{5,4},{6,7},{7,6},{8,9},{9,8},{10,11... | collective-permute-start | bytes 12296 | tf_op jit(solution)/shard_map/ppermute | solution.py:24
  5.4 2.0 %collective-permute-start.4 = (bf16[384,384]{1,0:T(8,128)(2,1)S(1)}, bf16[384,384]{1,0:T(8,128)(2,1)S(1)}, u32[]{:S(2)}, u32[]{:S(2)}) collective-permute-start(bf16[384,384]{1,0:T(8,128)(2,1)S(1)} %get-tuple-element.125), channel_id=1, source_target_pairs={{0,1},{1,0},{2,17},{3,16},{16,19},{17,18},{18,3},{19,2},{4,5},{5,4... | collective-permute-start | bytes 884744 | tf_op jit(solution)/shard_map/ppermute | solution.py:24
  7.4 3.9 %collective-permute-start.3 = (bf16[384,384]{1,0:T(8,128)(2,1)S(1)}, bf16[384,384]{1,0:T(8,128)(2,1)S(1)}, u32[]{:S(2)}, u32[]{:S(2)}) collective-permute-start(bf16[384,384]{1,0:T(8,128)(2,1)S(1)} %get-tuple-element.126), channel_id=1, source_target_pairs={{0,0},{1,1},{2,16},{3,17},{16,18},{17,19},{18,2},{19,3},{4,4},{5,5... | collective-permute-start | bytes 884744 | tf_op jit(solution)/shard_map/ppermute | solution.py:24
  12.8 4.1 %collective-permute-done.3 = bf16[384,384]{1,0:T(8,128)(2,1)S(1)} collective-permute-done((bf16[384,384]{1,0:T(8,128)(2,1)S(1)}, bf16[384,384]{1,0:T(8,128)(2,1)S(1)}, u32[]{:S(2)}, u32[]{:S(2)}) %collective-permute-start.3) | collective-permute-done | bytes 294944 | tf_op jit(solution)/shard_map/ppermute | solution.py:24
  16.9 2.1 %collective-permute-start.5 = (f32[2,512]{1,0:T(2,128)S(1)}, f32[2,512]{1,0:T(2,128)S(1)}, u32[]{:S(2)}, u32[]{:S(2)}) collective-permute-start(f32[2,512]{1,0:T(2,128)S(1)} %pad_maximum_fusion.6), channel_id=1, source_target_pairs={{0,2},{1,3},{2,0},{3,1},{4,6},{5,7},{6,4},{7,5},{8,10},{9,11},{10,... | collective-permute-start | bytes 12296 | tf_op jit(solution)/shard_map/ppermute | solution.py:24
  20.0 3.0 %collective-permute-start = (bf16[512,384]{1,0:T(8,128)(2,1)}, bf16[512,384]{1,0:T(8,128)(2,1)}, u32[]{:S(2)}, u32[]{:S(2)}) collective-permute-start(bf16[512,384]{1,0:T(8,128)(2,1)} %param.4), channel_id=1, source_target_pairs={{0,8},{4,12},{8,0},{12,4},{1,9},{5,13},{9,1},{13,5},{2,10},{6,14},... | collective-permute-start | bytes 1179656 | tf_op jit(solution)/shard_map/ppermute | solution.py:24
  23.1 2.6 %collective-permute-start.8 = (bf16[384,768]{1,0:T(8,128)(2,1)S(1)}, bf16[384,768]{1,0:T(8,128)(2,1)S(1)}, u32[]{:S(2)}, u32[]{:S(2)}) collective-permute-start(bf16[384,768]{1,0:T(8,128)(2,1)S(1)} %constant_dynamic-update-slice_fusion.refs_0_), channel_id=1, source_target_pairs={{0,96},{32,64},{64,32},{96,0},{1,97},{33,65},{65,33},{97,1},{2,98}... | collective-permute-start | bytes 1769480 | tf_op jit(solution)/shard_map/ppermute | solution.py:24
  27.8 3.7 %all-to-all-start = ((bf16[4,512,384]{2,1,0:T(8,128)(2,1)}), bf16[4,512,384]{2,1,0:T(8,128)(2,1)S(1)}, u32[]{:S(2)}, u32[]{:S(2)}) async-start(bf16[4,512,384]{2,1,0:T(8,128)(2,1)} %broadcast_in_dim.18), calls=%async_computation | async-start | bytes 3145728 | tf_op jit(solution)/shard_map/all_to_all | solution.py:215
  31.5 5.4 %collective-permute-done.1 = bf16[512,384]{1,0:T(8,128)(2,1)} collective-permute-done((bf16[512,384]{1,0:T(8,128)(2,1)}, bf16[512,384]{1,0:T(8,128)(2,1)}, u32[]{:S(2)}, u32[]{:S(2)}) %collective-permute-start.1) | collective-permute-done | bytes 393248 | tf_op jit(solution)/shard_map/ppermute | solution.py:24
  37.0 3.7 %collective-permute-done = bf16[512,384]{1,0:T(8,128)(2,1)} collective-permute-done((bf16[512,384]{1,0:T(8,128)(2,1)}, bf16[512,384]{1,0:T(8,128)(2,1)}, u32[]{:S(2)}, u32[]{:S(2)}) %collective-permute-start) | collective-permute-done | bytes 393248 | tf_op jit(solution)/shard_map/ppermute | solution.py:24
  44.8 5.3 %collective-permute-done.11 = f32[1792]{0:T(1024)S(1)} collective-permute-done((f32[1792]{0:T(1024)S(1)}, f32[1792]{0:T(1024)S(1)}, u32[]{:S(2)}, u32[]{:S(2)}) %collective-permute-start.11) | collective-permute-done | bytes 7200 | tf_op jit(solution)/shard_map/ppermute | solution.py:24
  50.1 2.3 %collective-permute-done.9 = bf16[512,384]{1,0:T(8,128)(2,1)S(1)} collective-permute-done((bf16[512,384]{1,0:T(8,128)(2,1)}, bf16[512,384]{1,0:T(8,128)(2,1)S(1)}, u32[]{:S(2)}, u32[]{:S(2)}) %collective-permute-start.9) | collective-permute-done | bytes 393248 | tf_op jit(solution)/shard_map/ppermute | solution.py:24
  59.4 1.8 %multiply_convert_fusion = (bf16[512,384]{1,0:T(8,128)(2,1)S(1)}, bf16[512,384]{1,0:T(8,128)(2,1)S(1)}, bf16[512,384]{1,0:T(8,128)(2,1)S(1)}, bf16[512,384]{1,0:T(8,128)(2,1)S(1)}) fusion(bf16[512,384]{1,0:T(8,128)(2,1)S(1)} %collective-permute-done.9, f32[384]{0:T(512)S(1)} %get-tuple-element.131, f32[512]{0:T(512)S(1)} %get-tuple-element.128, ...), kind=kLoop, calls=%fused_computation.12 | loop fusion | flops 3932160 | bytes 3155968 | tf_op jit(solution)/shard_map/convert_element_type | solution.py:240
  61.3 2.4 %shard_map.67 = (bf16[4,384,768]{2,1,0:T(8,128)(2,1)S(1)}, bf16[4,384,512]{2,1,0:T(8,128)(2,1)S(1)}) custom-call(bf16[512,384]{1,0:T(8,128)(2,1)S(1)} %get-tuple-element.142.refs_0_.refs_9_, bf16[512,384]{1,0:T(8,128)(2,1)S(1)} %get-tuple-element.140.refs_1_.refs_10_, bf16[512,384]{1,0:T(8,128)(2,1)S(1)} %get-tuple-element.141.refs_2_.refs_11_, ...), custom_call_target="tpu_custom_call" | custom-call | flops 1 | bytes 1 | tf_op jit(solution)/shard_map/pallas_call | solution.py:50
  66.4 7.6 %shard_map.68 = (f32[512,384]{1,0:T(8,128)S(1)}, bf16[512,384]{1,0:T(8,128)(2,1)S(1)}, bf16[512,384]{1,0:T(8,128)(2,1)S(1)}, bf16[528,384]{1,0:T(8,128)(2,1)S(1)...) custom-call(bf16[384,768]{1,0:T(8,128)(2,1)S(1)} %copy-done.2, ...), custom_call_target="tpu_custom_call" | custom-call | flops 40000000 | bytes 40000000 | tf_op jit(solution)/shard_map/pallas_call | solution.py:50
  74.0 2.1 %collective-permute-start.16 = (bf16[528,384]{1,0:T(8,128)(2,1)S(1)}, bf16[528,384]{1,0:T(8,128)(2,1)S(1)}, u32[]{:S(2)}, u32[]{:S(2)}) collective-permute-start(bf16[528,384]{1,0:T(8,128)(2,1)S(1)} %get-tuple-element.96), channel_id=1, source_target_pairs={{0,4},{4,0},{8,12},{12,8},{1,5},{5,1},{9,13},{13,9},{2,6},{6,2},{1... | collective-permute-start | bytes 1216520 | tf_op jit(solution)/shard_map/ppermute | solution.py:24
  76.1 2.1 %shard_map.69 = (f32[384,768]{1,0:T(8,128)S(1)}, bf16[384,768]{1,0:T(8,128)(2,1)}, bf16[384,768]{1,0:T(8,128)(2,1)}, bf16[384,768]{1,0:T(8,128)(2,1)S(1)}) custom-call(bf16[4,512,384]{2,1,0:T(8,128)(2,1)S(1)} %all-to-all-done.refs_4_.refs_8_.refs_0_, bf16[4,384,512]{2,1,0:T(8,128)(2,1)S(1)} %get-tuple-element.97.refs_1_, ...), custom_call_target="tpu_custom_call" | custom-call | flops 1 | bytes 1 | tf_op jit(solution)/shard_map/pallas_call | solution.py:50
  79.5 3.1 %collective-permute-start.19 = (bf16[384,768]{1,0:T(8,128)(2,1)}, bf16[384,768]{1,0:T(8,128)(2,1)}, u32[]{:S(2)}, u32[]{:S(2)}) collective-permute-start(bf16[384,768]{1,0:T(8,128)(2,1)} %get-tuple-element.102), channel_id=1, source_target_pairs={{0,64},{32,96},{64,0},{96,32},{1,65},{33,97},{65,1},{97,33},{2,66}... | collective-permute-start | bytes 1769480 | tf_op jit(solution)/shard_map/ppermute | solution.py:24
  82.6 3.2 %collective-permute-done.16.relay = bf16[528,384]{1,0:T(8,128)(2,1)S(1)} collective-permute-done((bf16[528,384]{1,0:T(8,128)(2,1)S(1)}, bf16[528,384]{1,0:T(8,128)(2,1)S(1)}, u32[]{:S(2)}, u32[]{:S(2)}) %collective-permute-start.16) | collective-permute-done | bytes 405536 | tf_op jit(solution)/shard_map/ppermute | solution.py:24
  86.0 1.9 %collective-permute-start.21 = (bf16[528,384]{1,0:T(8,128)(2,1)S(1)}, bf16[528,384]{1,0:T(8,128)(2,1)S(1)}, u32[]{:S(2)}, u32[]{:S(2)}) collective-permute-start(bf16[528,384]{1,0:T(8,128)(2,1)S(1)} %get-tuple-element.109), channel_id=1, source_target_pairs={{0,8},{4,12},{8,0},{12,4},{1,9},{5,13},{9,1},{13,5},{2,10},{6,14},... | collective-permute-start | bytes 1216520 | tf_op jit(solution)/shard_map/ppermute | solution.py:24
  87.9 4.3 %all-to-all-start.1 = ((bf16[4,512,384]{2,1,0:T(8,128)(2,1)}), bf16[4,512,384]{2,1,0:T(8,128)(2,1)}, u32[]{:S(2)}, u32[]{:S(2)}) async-start(bf16[4,512,384]{2,1,0:T(8,128)(2,1)} %copy-done), calls=%async_computation.1 | async-start | bytes 3145728 | tf_op jit(solution)/shard_map/all_to_all | solution.py:309
  92.6 13.6 %collective-permute-done.21 = bf16[528,384]{1,0:T(8,128)(2,1)S(1)} collective-permute-done((bf16[528,384]{1,0:T(8,128)(2,1)S(1)}, bf16[528,384]{1,0:T(8,128)(2,1)S(1)}, u32[]{:S(2)}, u32[]{:S(2)}) %collective-permute-start.21) | collective-permute-done | bytes 405536 | tf_op jit(solution)/shard_map/ppermute | solution.py:24
  106.2 2.4 %collective-permute-done.19 = bf16[384,768]{1,0:T(8,128)(2,1)} collective-permute-done((bf16[384,768]{1,0:T(8,128)(2,1)}, bf16[384,768]{1,0:T(8,128)(2,1)}, u32[]{:S(2)}, u32[]{:S(2)}) %collective-permute-start.19) | collective-permute-done | bytes 589856 | tf_op jit(solution)/shard_map/ppermute | solution.py:24
  108.6 1.8 %collective-permute-done.20 = bf16[384,768]{1,0:T(8,128)(2,1)} collective-permute-done((bf16[384,768]{1,0:T(8,128)(2,1)S(1)}, bf16[384,768]{1,0:T(8,128)(2,1)}, u32[]{:S(2)}, u32[]{:S(2)}) %collective-permute-start.20) | collective-permute-done | bytes 589856 | tf_op jit(solution)/shard_map/ppermute | solution.py:24
  110.4 1.7 %add_convert_fusion = bf16[384,768]{1,0:T(8,128)(2,1)S(1)} fusion(bf16[384,768]{1,0:T(8,128)(2,1)} %collective-permute-done.20, bf16[384,768]{1,0:T(8,128)(2,1)} %collective-permute-done.19, f32[384,768]{1,0:T(8,128)S(1)} %get-tuple-element.100, bf16[384,768]{1,0:T(8,128)(2,1)} %collective-permute-done.18), kind=kLoop, calls=%fused_computation.4 | loop fusion | flops 2064384 | bytes 3538944 | tf_op jit(solution)/shard_map/convert_element_type | solution.py:296
  112.2 3.2 %collective-permute-start.28 = (bf16[384,384]{1,0:T(8,128)(2,1)S(1)}, bf16[384,384]{1,0:T(8,128)(2,1)S(1)}, u32[]{:S(2)}, u32[]{:S(2)}) collective-permute-start(bf16[384,384]{1,0:T(8,128)(2,1)S(1)} %get-tuple-element.123), channel_id=1, source_target_pairs={{0,0},{1,1},{2,18},{3,19},{16,2},{17,3},{18,16},{19,17},{128,128},... | collective-permute-start | bytes 884744 | tf_op jit(solution)/shard_map/ppermute | solution.py:24
  115.4 5.3 %collective-permute-start.24 = (bf16[384,384]{1,0:T(8,128)(2,1)S(1)}, bf16[384,384]{1,0:T(8,128)(2,1)S(1)}, u32[]{:S(2)}, u32[]{:S(2)}) collective-permute-start(bf16[384,384]{1,0:T(8,128)(2,1)S(1)} %get-tuple-element.123), channel_id=1, source_target_pairs={{0,128},{1,129},{2,146},{3,147},{16,130},{17,131},{18,144},{19,145... | collective-permute-start | bytes 884744 | tf_op jit(solution)/shard_map/ppermute | solution.py:24
  120.7 1.6 %collective-permute-start.29 = (bf16[384,384]{1,0:T(8,128)(2,1)S(1)}, bf16[384,384]{1,0:T(8,128)(2,1)S(1)}, u32[]{:S(2)}, u32[]{:S(2)}) collective-permute-start(bf16[384,384]{1,0:T(8,128)(2,1)S(1)} %get-tuple-element.124), channel_id=1, source_target_pairs={{0,1},{1,0},{2,19},{3,18},{16,3},{17,2},{18,17},{19,16},{128,129},... | collective-permute-start | bytes 884744 | tf_op jit(solution)/shard_map/ppermute | solution.py:24
  123.9 2.5 %reduce_sum.32 = bf16[512,384]{1,0:T(8,128)(2,1)} reduce(bf16[4,512,384]{2,1,0:T(8,128)(2,1)} %all-to-all-done.1, bf16[]{:T(256)} %constant.46.clone.1), dimensions={0}, to_apply=%region_2.3 | reduce | flops 589824 | bytes 1966082 | tf_op jit(solution)/shard_map/reduce_sum | solution.py:311
  126.4 19.2 %collective-permute-done.22 = bf16[384,384]{1,0:T(8,128)(2,1)S(1)} collective-permute-done((bf16[384,384]{1,0:T(8,128)(2,1)S(1)}, bf16[384,384]{1,0:T(8,128)(2,1)S(1)}, u32[]{:S(2)}, u32[]{:S(2)}) %collective-permute-start.22) | collective-permute-done | bytes 294944 | tf_op jit(solution)/shard_map/ppermute | solution.py:24
  145.9 1.6 %collective-permute-start.26 = (f32[2,512]{1,0:T(2,128)S(1)}, f32[2,512]{1,0:T(2,128)S(1)}, u32[]{:S(2)}, u32[]{:S(2)}) collective-permute-start(f32[2,512]{1,0:T(2,128)S(1)} %fusion.10), channel_id=1, source_target_pairs={{0,2},{1,3},{2,0},{3,1},{4,6},{5,7},{6,4},{7,5},{8,10},{9,11},{10,... | collective-permute-start | bytes 12296 | tf_op jit(solution)/shard_map/ppermute | solution.py:24
  150.6 2.3 %fusion.6 = bf16[512,384]{1,0:T(8,128)(2,1)} fusion(bf16[512,384]{1,0:T(8,128)(2,1)} %param.4, bf16[512,384]{1,0:T(8,128)(2,1)S(1)} %slice-done, f32[512,384]{1,0:T(8,128)S(1)} %copy-done.4, bf16[512,384]{1,0:T(8,128)(2,1)} %collective-permute-done.23, f32[512]{0:T(512)S(1)} %bitcast.25, f32[512]{0:T(512)S(1)} %bitcast.24, f32[384]{0:T(512)S(1)} %copy-done.22, ...), kind=kLoop, calls=%fused_computation.11 | loop fusion | flops 2555904 | bytes 2369024 | tf_op jit(solution)/shard_map/convert_element_type | solution.py:320
  (124 shorter events, 27.8 us)
Async XLA Ops:
  3.1 8.2 %collective-permute-start.2 = (f32[2,512]{1,0:T(2,128)S(1)}, f32[2,512]{1,0:T(2,128)S(1)}, u32[]{:S(2)}, u32[]{:S(2)}) collective-permute-start(f32[2,512]{1,0:T(2,128)S(1)} %pad_maximum_fusion.5), channel_id=1, source_target_pairs={{0,1},{1,0},{2,3},{3,2},{4,5},{5,4},{6,7},{7,6},{8,9},{9,8},{10,11... | collective-permute-start | bytes 12296 | tf_op jit(solution)/shard_map/ppermute | solution.py:24
  5.4 7.4 %collective-permute-start.4 = (bf16[384,384]{1,0:T(8,128)(2,1)S(1)}, bf16[384,384]{1,0:T(8,128)(2,1)S(1)}, u32[]{:S(2)}, u32[]{:S(2)}) collective-permute-start(bf16[384,384]{1,0:T(8,128)(2,1)S(1)} %get-tuple-element.125), channel_id=1, source_target_pairs={{0,1},{1,0},{2,17},{3,16},{16,19},{17,18},{18,3},{19,2},{4,5},{5,4... | collective-permute-start | bytes 884744 | tf_op jit(solution)/shard_map/ppermute | solution.py:24
  7.4 9.5 %collective-permute-start.3 = (bf16[384,384]{1,0:T(8,128)(2,1)S(1)}, bf16[384,384]{1,0:T(8,128)(2,1)S(1)}, u32[]{:S(2)}, u32[]{:S(2)}) collective-permute-start(bf16[384,384]{1,0:T(8,128)(2,1)S(1)} %get-tuple-element.126), channel_id=1, source_target_pairs={{0,0},{1,1},{2,16},{3,17},{16,18},{17,19},{18,2},{19,3},{4,4},{5,5... | collective-permute-start | bytes 884744 | tf_op jit(solution)/shard_map/ppermute | solution.py:24
  16.9 6.1 %collective-permute-start.5 = (f32[2,512]{1,0:T(2,128)S(1)}, f32[2,512]{1,0:T(2,128)S(1)}, u32[]{:S(2)}, u32[]{:S(2)}) collective-permute-start(f32[2,512]{1,0:T(2,128)S(1)} %pad_maximum_fusion.6), channel_id=1, source_target_pairs={{0,2},{1,3},{2,0},{3,1},{4,6},{5,7},{6,4},{7,5},{8,10},{9,11},{10,... | collective-permute-start | bytes 12296 | tf_op jit(solution)/shard_map/ppermute | solution.py:24
  19.0 17.9 %collective-permute-start.1 = (bf16[512,384]{1,0:T(8,128)(2,1)}, bf16[512,384]{1,0:T(8,128)(2,1)}, u32[]{:S(2)}, u32[]{:S(2)}) collective-permute-start(bf16[512,384]{1,0:T(8,128)(2,1)} %param.4), channel_id=1, source_target_pairs={{0,4},{4,0},{8,12},{12,8},{1,5},{5,1},{9,13},{13,9},{2,6},{6,2},{1... | collective-permute-start | bytes 1179656 | tf_op jit(solution)/shard_map/ppermute | solution.py:24
  20.0 20.6 %collective-permute-start = (bf16[512,384]{1,0:T(8,128)(2,1)}, bf16[512,384]{1,0:T(8,128)(2,1)}, u32[]{:S(2)}, u32[]{:S(2)}) collective-permute-start(bf16[512,384]{1,0:T(8,128)(2,1)} %param.4), channel_id=1, source_target_pairs={{0,8},{4,12},{8,0},{12,4},{1,9},{5,13},{9,1},{13,5},{2,10},{6,14},... | collective-permute-start | bytes 1179656 | tf_op jit(solution)/shard_map/ppermute | solution.py:24
  23.1 29.3 %collective-permute-start.8 = (bf16[384,768]{1,0:T(8,128)(2,1)S(1)}, bf16[384,768]{1,0:T(8,128)(2,1)S(1)}, u32[]{:S(2)}, u32[]{:S(2)}) collective-permute-start(bf16[384,768]{1,0:T(8,128)(2,1)S(1)} %constant_dynamic-update-slice_fusion.refs_0_), channel_id=1, source_target_pairs={{0,96},{32,64},{64,32},{96,0},{1,97},{33,65},{65,33},{97,1},{2,98}... | collective-permute-start | bytes 1769480 | tf_op jit(solution)/shard_map/ppermute | solution.py:24
  25.7 26.7 %collective-permute-start.7 = (bf16[384,768]{1,0:T(8,128)(2,1)S(1)}, bf16[384,768]{1,0:T(8,128)(2,1)S(1)}, u32[]{:S(2)}, u32[]{:S(2)}) collective-permute-start(bf16[384,768]{1,0:T(8,128)(2,1)S(1)} %constant_dynamic-update-slice_fusion.refs_0_), channel_id=1, source_target_pairs={{0,64},{32,96},{64,0},{96,32},{1,65},{33,97},{65,1},{97,33},{2,66}... | collective-permute-start | bytes 1769480 | tf_op jit(solution)/shard_map/ppermute | solution.py:24
  26.2 26.8 %collective-permute-start.6 = (bf16[384,768]{1,0:T(8,128)(2,1)S(1)}, bf16[384,768]{1,0:T(8,128)(2,1)}, u32[]{:S(2)}, u32[]{:S(2)}) collective-permute-start(bf16[384,768]{1,0:T(8,128)(2,1)S(1)} %constant_dynamic-update-slice_fusion.refs_0_), channel_id=1, source_target_pairs={{0,32},{32,0},{64,96},{96,64},{1,33},{33,1},{65,97},{97,65},{2,34}... | collective-permute-start | bytes 1769480 | tf_op jit(solution)/shard_map/ppermute | solution.py:24
  27.8 33.4 %all-to-all-start = ((bf16[4,512,384]{2,1,0:T(8,128)(2,1)}), bf16[4,512,384]{2,1,0:T(8,128)(2,1)S(1)}, u32[]{:S(2)}, u32[]{:S(2)}) async-start(bf16[4,512,384]{2,1,0:T(8,128)(2,1)} %broadcast_in_dim.18), calls=%async_computation | async-start | bytes 3145728 | tf_op jit(solution)/shard_map/all_to_all | solution.py:215
  40.6 3.0 %collective-permute-start.10 = (f32[1408]{0:T(1024)S(1)}, f32[1408]{0:T(1024)S(1)}, u32[]{:S(2)}, u32[]{:S(2)}) collective-permute-start(f32[1408]{0:T(1024)S(1)} %pad_maximum_fusion.1), channel_id=1, source_target_pairs={{0,4},{4,0},{8,12},{12,8},{1,5},{5,1},{9,13},{13,9},{2,6},{6,2},{1... | collective-permute-start | bytes 16904 | tf_op jit(solution)/shard_map/ppermute | solution.py:24
  40.8 11.7 %collective-permute-start.9 = (bf16[512,384]{1,0:T(8,128)(2,1)}, bf16[512,384]{1,0:T(8,128)(2,1)S(1)}, u32[]{:S(2)}, u32[]{:S(2)}) collective-permute-start(bf16[512,384]{1,0:T(8,128)(2,1)} %collective-permute-done), channel_id=1, source_target_pairs={{0,4},{4,0},{8,12},{12,8},{1,5},{5,1},{9,13},{13,9},{2,6},{6,2},{1... | collective-permute-start | bytes 1179656 | tf_op jit(solution)/shard_map/ppermute | solution.py:24
  43.7 6.4 %collective-permute-start.11 = (f32[1792]{0:T(1024)S(1)}, f32[1792]{0:T(1024)S(1)}, u32[]{:S(2)}, u32[]{:S(2)}) collective-permute-start(f32[1792]{0:T(1024)S(1)} %pad_maximum_fusion.2), channel_id=1, source_target_pairs={{0,8},{4,12},{8,0},{12,4},{1,9},{5,13},{9,1},{13,5},{2,10},{6,14},... | collective-permute-start | bytes 21512 | tf_op jit(solution)/shard_map/ppermute | solution.py:24
  53.1 2.7 %collective-permute-start.12 = (bf16[384,768]{1,0:T(8,128)(2,1)S(1)}, bf16[384,768]{1,0:T(8,128)(2,1)S(1)}, u32[]{:S(2)}, u32[]{:S(2)}) collective-permute-start(bf16[384,768]{1,0:T(8,128)(2,1)S(1)} %constant_dynamic-update-slice_fusion.refs_0_), channel_id=1, source_target_pairs={{0,16},{16,0},{1,17},{17,1},{2,18},{18,2},{3,19},{19,3},{4,20},{20... | collective-permute-start | bytes 1769480 | tf_op jit(solution)/shard_map/ppermute | solution.py:24
  53.6 3.4 %collective-permute-start.13 = (bf16[384,768]{1,0:T(8,128)(2,1)}, bf16[384,768]{1,0:T(8,128)(2,1)S(1)}, u32[]{:S(2)}, u32[]{:S(2)}) collective-permute-start(bf16[384,768]{1,0:T(8,128)(2,1)} %collective-permute-done.6.refs_1_), channel_id=1, source_target_pairs={{0,16},{16,0},{1,17},{17,1},{2,18},{18,2},{3,19},{19,3},{4,20},{20... | collective-permute-start | bytes 1769480 | tf_op jit(solution)/shard_map/ppermute | solution.py:24
  53.6 4.2 %collective-permute-start.14 = (bf16[384,768]{1,0:T(8,128)(2,1)S(1)}, bf16[384,768]{1,0:T(8,128)(2,1)S(1)}, u32[]{:S(2)}, u32[]{:S(2)}) collective-permute-start(bf16[384,768]{1,0:T(8,128)(2,1)S(1)} %collective-permute-done.7.refs_2_), channel_id=1, source_target_pairs={{0,16},{16,0},{1,17},{17,1},{2,18},{18,2},{3,19},{19,3},{4,20},{20... | collective-permute-start | bytes 1769480 | tf_op jit(solution)/shard_map/ppermute | solution.py:24
  54.9 3.7 %collective-permute-start.15 = (bf16[384,768]{1,0:T(8,128)(2,1)S(1)}, bf16[384,768]{1,0:T(8,128)(2,1)S(1)}, u32[]{:S(2)}, u32[]{:S(2)}) collective-permute-start(bf16[384,768]{1,0:T(8,128)(2,1)S(1)} %collective-permute-done.8.refs_3_), channel_id=1, source_target_pairs={{0,16},{16,0},{1,17},{17,1},{2,18},{18,2},{3,19},{19,3},{4,20},{20... | collective-permute-start | bytes 1769480 | tf_op jit(solution)/shard_map/ppermute | solution.py:24
  63.7 12.3 %collective-permute-start.17 = (bf16[4,384,768]{2,1,0:T(8,128)(2,1)S(1)}, bf16[4,384,768]{2,1,0:T(8,128)(2,1)S(1)}, u32[]{:S(2)}, u32[]{:S(2)}) collective-permute-start(bf16[4,384,768]{2,1,0:T(8,128)(2,1)S(1)} %get-tuple-element.98), channel_id=1, source_target_pairs={{0,16},{16,0},{1,17},{17,1},{2,18},{18,2},{3,19},{19,3},{4,20},{20... | collective-permute-start | bytes 7077896 | tf_op jit(solution)/shard_map/ppermute | solution.py:24
  74.0 11.8 %collective-permute-start.16 = (bf16[528,384]{1,0:T(8,128)(2,1)S(1)}, bf16[528,384]{1,0:T(8,128)(2,1)S(1)}, u32[]{:S(2)}, u32[]{:S(2)}) collective-permute-start(bf16[528,384]{1,0:T(8,128)(2,1)S(1)} %get-tuple-element.96), channel_id=1, source_target_pairs={{0,4},{4,0},{8,12},{12,8},{1,5},{5,1},{9,13},{13,9},{2,6},{6,2},{1... | collective-permute-start | bytes 1216520 | tf_op jit(solution)/shard_map/ppermute | solution.py:24
  78.2 28.0 %collective-permute-start.18 = (bf16[384,768]{1,0:T(8,128)(2,1)}, bf16[384,768]{1,0:T(8,128)(2,1)}, u32[]{:S(2)}, u32[]{:S(2)}) collective-permute-start(bf16[384,768]{1,0:T(8,128)(2,1)} %get-tuple-element.101), channel_id=1, source_target_pairs={{0,32},{32,0},{64,96},{96,64},{1,33},{33,1},{65,97},{97,65},{2,34}... | collective-permute-start | bytes 1769480 | tf_op jit(solution)/shard_map/ppermute | solution.py:24
  79.5 29.1 %collective-permute-start.19 = (bf16[384,768]{1,0:T(8,128)(2,1)}, bf16[384,768]{1,0:T(8,128)(2,1)}, u32[]{:S(2)}, u32[]{:S(2)}) collective-permute-start(bf16[384,768]{1,0:T(8,128)(2,1)} %get-tuple-element.102), channel_id=1, source_target_pairs={{0,64},{32,96},{64,0},{96,32},{1,65},{33,97},{65,1},{97,33},{2,66}... | collective-permute-start | bytes 1769480 | tf_op jit(solution)/shard_map/ppermute | solution.py:24
  82.6 27.8 %collective-permute-start.20 = (bf16[384,768]{1,0:T(8,128)(2,1)S(1)}, bf16[384,768]{1,0:T(8,128)(2,1)}, u32[]{:S(2)}, u32[]{:S(2)}) collective-permute-start(bf16[384,768]{1,0:T(8,128)(2,1)S(1)} %get-tuple-element.103), channel_id=1, source_target_pairs={{0,96},{32,64},{64,32},{96,0},{1,97},{33,65},{65,33},{97,1},{2,98}... | collective-permute-start | bytes 1769480 | tf_op jit(solution)/shard_map/ppermute | solution.py:24
  86.0 20.2 %collective-permute-start.21 = (bf16[528,384]{1,0:T(8,128)(2,1)S(1)}, bf16[528,384]{1,0:T(8,128)(2,1)S(1)}, u32[]{:S(2)}, u32[]{:S(2)}) collective-permute-start(bf16[528,384]{1,0:T(8,128)(2,1)S(1)} %get-tuple-element.109), channel_id=1, source_target_pairs={{0,8},{4,12},{8,0},{12,4},{1,9},{5,13},{9,1},{13,5},{2,10},{6,14},... | collective-permute-start | bytes 1216520 | tf_op jit(solution)/shard_map/ppermute | solution.py:24
  87.9 36.0 %all-to-all-start.1 = ((bf16[4,512,384]{2,1,0:T(8,128)(2,1)}), bf16[4,512,384]{2,1,0:T(8,128)(2,1)}, u32[]{:S(2)}, u32[]{:S(2)}) async-start(bf16[4,512,384]{2,1,0:T(8,128)(2,1)} %copy-done), calls=%async_computation.1 | async-start | bytes 3145728 | tf_op jit(solution)/shard_map/all_to_all | solution.py:309
  92.2 57.9 %collective-permute-start.23 = (bf16[512,384]{1,0:T(8,128)(2,1)S(1)}, bf16[512,384]{1,0:T(8,128)(2,1)}, u32[]{:S(2)}, u32[]{:S(2)}) collective-permute-start(bf16[512,384]{1,0:T(8,128)(2,1)S(1)} %copy-done.18), channel_id=1, source_target_pairs={{0,4},{4,0},{8,12},{12,8},{1,5},{5,1},{9,13},{13,9},{2,6},{6,2},{1... | collective-permute-start | bytes 1179656 | tf_op jit(solution)/shard_map/ppermute | solution.py:24
  112.2 35.3 %collective-permute-start.28 = (bf16[384,384]{1,0:T(8,128)(2,1)S(1)}, bf16[384,384]{1,0:T(8,128)(2,1)S(1)}, u32[]{:S(2)}, u32[]{:S(2)}) collective-permute-start(bf16[384,384]{1,0:T(8,128)(2,1)S(1)} %get-tuple-element.123), channel_id=1, source_target_pairs={{0,0},{1,1},{2,18},{3,19},{16,2},{17,3},{18,16},{19,17},{128,128},... | collective-permute-start | bytes 884744 | tf_op jit(solution)/shard_map/ppermute | solution.py:24
  115.4 30.2 %collective-permute-start.24 = (bf16[384,384]{1,0:T(8,128)(2,1)S(1)}, bf16[384,384]{1,0:T(8,128)(2,1)S(1)}, u32[]{:S(2)}, u32[]{:S(2)}) collective-permute-start(bf16[384,384]{1,0:T(8,128)(2,1)S(1)} %get-tuple-element.123), channel_id=1, source_target_pairs={{0,128},{1,129},{2,146},{3,147},{16,130},{17,131},{18,144},{19,145... | collective-permute-start | bytes 884744 | tf_op jit(solution)/shard_map/ppermute | solution.py:24
  120.7 28.1 %collective-permute-start.29 = (bf16[384,384]{1,0:T(8,128)(2,1)S(1)}, bf16[384,384]{1,0:T(8,128)(2,1)S(1)}, u32[]{:S(2)}, u32[]{:S(2)}) collective-permute-start(bf16[384,384]{1,0:T(8,128)(2,1)S(1)} %get-tuple-element.124), channel_id=1, source_target_pairs={{0,1},{1,0},{2,19},{3,18},{16,3},{17,2},{18,17},{19,16},{128,129},... | collective-permute-start | bytes 884744 | tf_op jit(solution)/shard_map/ppermute | solution.py:24
  122.3 23.2 %collective-permute-start.22 = (bf16[384,384]{1,0:T(8,128)(2,1)S(1)}, bf16[384,384]{1,0:T(8,128)(2,1)S(1)}, u32[]{:S(2)}, u32[]{:S(2)}) collective-permute-start(bf16[384,384]{1,0:T(8,128)(2,1)S(1)} %get-tuple-element.124), channel_id=1, source_target_pairs={{0,129},{1,128},{2,147},{3,146},{16,131},{17,130},{18,145},{19,144... | collective-permute-start | bytes 884744 | tf_op jit(solution)/shard_map/ppermute | solution.py:24
  145.6 4.5 %collective-permute-start.27 = (f32[2,512]{1,0:T(2,128)S(1)}, f32[2,512]{1,0:T(2,128)S(1)}, u32[]{:S(2)}, u32[]{:S(2)}) collective-permute-start(f32[2,512]{1,0:T(2,128)S(1)} %fusion.10), channel_id=1, source_target_pairs={{0,3},{1,2},{2,1},{3,0},{4,7},{5,6},{6,5},{7,4},{8,11},{9,10},{10,... | collective-permute-start | bytes 12296 | tf_op jit(solution)/shard_map/ppermute | solution.py:24
  145.9 4.2 %collective-permute-start.26 = (f32[2,512]{1,0:T(2,128)S(1)}, f32[2,512]{1,0:T(2,128)S(1)}, u32[]{:S(2)}, u32[]{:S(2)}) collective-permute-start(f32[2,512]{1,0:T(2,128)S(1)} %fusion.10), channel_id=1, source_target_pairs={{0,2},{1,3},{2,0},{3,1},{4,6},{5,7},{6,4},{7,5},{8,10},{9,11},{10,... | collective-permute-start | bytes 12296 | tf_op jit(solution)/shard_map/ppermute | solution.py:24
  147.5 2.6 %collective-permute-start.25 = (f32[2,512]{1,0:T(2,128)S(1)}, f32[2,512]{1,0:T(2,128)S(1)}, u32[]{:S(2)}, u32[]{:S(2)}) collective-permute-start(f32[2,512]{1,0:T(2,128)S(1)} %fusion.10), channel_id=1, source_target_pairs={{0,1},{1,0},{2,3},{3,2},{4,5},{5,4},{6,7},{7,6},{8,9},{9,8},{10,11... | collective-permute-start | bytes 12296 | tf_op jit(solution)/shard_map/ppermute | solution.py:24
  (24 other events, 130.0 us)

commit v4 on v3

--- a/solution.py
+++ b/solution.py
@@ -294,7 +294,7 @@
 
 
     block = sum(p.astype(F32) for p in gw_parts).astype(BF16)
-    block, grad_parts[2] = after(block, grad_parts[2])
+    block, grad_parts = after(block, grad_parts)
     blocks = [block[:, :F], block[:, F:]]
 
     def home(a):
@@ -310,8 +310,10 @@
 
     query = jnp.sum(query_parts.astype(F32), axis=0).astype(BF16)
     far[1], query = after(far[1], query)
-    sums, far = after(sums, far)
-    sums = sums + sum(swap(sums, "y", e) for e in (1, 2, 3))
+    sums, near = after(sums, near)
+    parts = [swap(sums, "y", e) for e in (1, 2, 3)]
+    parts, far = after(parts, far)
+    sums = sums + sum(parts)
     got_a, got_b = (n.astype(F32) + f.astype(F32) for n, f in zip(near, far))
     even = odd == 0
     grad_w = jnp.concatenate([jnp.where(even, got_a, got_b), jnp.where(even, got_b, got_a)])

time: 155 us -> 149 us (0.961)
  waiting for transfers between devices: 65.1 us -> 59.3 us
    ppermute x30, waiting for transfers between devices: 65.1 us -> 59.3 us  [send(): return lax.ppermute(value, axes if len(axes) > 1 else axes[0], perm)]
    unnamed x49 -> x53, local copies, waits for them, and re-layouts: 7.39 us -> 7.58 us
  transfers between devices with their start and end apart: 32 -> 32, of which waited for: 14 -> 16; matrix products, arithmetic and copies ran while one was open for 6% -> 5% of each run, Pallas kernels for 6% -> 7%
where the time goes in v4:
time: 149 us; the launch traced here: 148 us
  waiting for transfers between devices  59.3 us (40%)
  starting transfers between devices  54.1 us (36%)
  Pallas kernels  12.3 us (8%)
  other arithmetic  11.9 us (8%)
  local copies, waits for them, and re-layouts  9.33 us (6%)
    ppermute x30, waiting for transfers between devices, send(): return lax.ppermute(value, axes if len(axes) > 1 else axes[0], perm)  59.3 us
    ppermute x30, starting transfers between devices, send(): return lax.ppermute(value, axes if len(axes) > 1 else axes[0], perm)  46.1 us
    pallas_call x4, Pallas kernels, outer(): pl.pallas_call(kernel, out_shape=out_shape, in_specs=[pl.BlockSpec(memory...  12.3 us
    unnamed x53, local copies, waits for them, and re-layouts  7.58 us
    all_to_all x1, starting transfers between devices, on_device(): query_parts = lax.all_to_all(query_out, 'y', 0, 0, tiled=True)  4.36 us
    all_to_all x1, starting transfers between devices, on_device(): lax.all_to_all(jnp.broadcast_to(cot, (4, T, F)), 'y', 0, 0, tiled=True)  3.69 us
  transfers between devices with their start and end apart: 32, of which 16 were waited for; matrix products, arithmetic and copies ran while one was open for 5% of the time, Pallas kernels for 7%

profile of v4, /device:TPU:1, one launch (start us, length us, event | category | flops | bytes accessed | tf_op | source)
XLA Modules:
  0.0 148.2 jit_solution(7400546389067023142)
XLA Ops:
  3.1 2.2 %collective-permute-start.2 = (f32[2,512]{1,0:T(2,128)S(1)}, f32[2,512]{1,0:T(2,128)S(1)}, u32[]{:S(2)}, u32[]{:S(2)}) collective-permute-start(f32[2,512]{1,0:T(2,128)S(1)} %pad_maximum_fusion.5), channel_id=1, source_target_pairs={{0,1},{1,0},{2,3},{3,2},{4,5},{5,4},{6,7},{7,6},{8,9},{9,8},{10,11... | collective-permute-start | bytes 12296 | tf_op jit(solution)/shard_map/ppermute | solution.py:24
  5.4 2.0 %collective-permute-start.4 = (bf16[384,384]{1,0:T(8,128)(2,1)S(1)}, bf16[384,384]{1,0:T(8,128)(2,1)S(1)}, u32[]{:S(2)}, u32[]{:S(2)}) collective-permute-start(bf16[384,384]{1,0:T(8,128)(2,1)S(1)} %get-tuple-element.139), channel_id=1, source_target_pairs={{0,1},{1,0},{2,17},{3,16},{16,19},{17,18},{18,3},{19,2},{4,5},{5,4... | collective-permute-start | bytes 884744 | tf_op jit(solution)/shard_map/ppermute | solution.py:24
  7.4 3.9 %collective-permute-start.3 = (bf16[384,384]{1,0:T(8,128)(2,1)S(1)}, bf16[384,384]{1,0:T(8,128)(2,1)S(1)}, u32[]{:S(2)}, u32[]{:S(2)}) collective-permute-start(bf16[384,384]{1,0:T(8,128)(2,1)S(1)} %get-tuple-element.140), channel_id=1, source_target_pairs={{0,0},{1,1},{2,16},{3,17},{16,18},{17,19},{18,2},{19,3},{4,4},{5,5... | collective-permute-start | bytes 884744 | tf_op jit(solution)/shard_map/ppermute | solution.py:24
  12.8 4.1 %collective-permute-done.3 = bf16[384,384]{1,0:T(8,128)(2,1)S(1)} collective-permute-done((bf16[384,384]{1,0:T(8,128)(2,1)S(1)}, bf16[384,384]{1,0:T(8,128)(2,1)S(1)}, u32[]{:S(2)}, u32[]{:S(2)}) %collective-permute-start.3) | collective-permute-done | bytes 294944 | tf_op jit(solution)/shard_map/ppermute | solution.py:24
  16.9 2.1 %collective-permute-start.5 = (f32[2,512]{1,0:T(2,128)S(1)}, f32[2,512]{1,0:T(2,128)S(1)}, u32[]{:S(2)}, u32[]{:S(2)}) collective-permute-start(f32[2,512]{1,0:T(2,128)S(1)} %pad_maximum_fusion.6), channel_id=1, source_target_pairs={{0,2},{1,3},{2,0},{3,1},{4,6},{5,7},{6,4},{7,5},{8,10},{9,11},{10,... | collective-permute-start | bytes 12296 | tf_op jit(solution)/shard_map/ppermute | solution.py:24
  20.0 3.0 %collective-permute-start = (bf16[512,384]{1,0:T(8,128)(2,1)}, bf16[512,384]{1,0:T(8,128)(2,1)}, u32[]{:S(2)}, u32[]{:S(2)}) collective-permute-start(bf16[512,384]{1,0:T(8,128)(2,1)} %param.4), channel_id=1, source_target_pairs={{0,8},{4,12},{8,0},{12,4},{1,9},{5,13},{9,1},{13,5},{2,10},{6,14},... | collective-permute-start | bytes 1179656 | tf_op jit(solution)/shard_map/ppermute | solution.py:24
  23.1 2.6 %collective-permute-start.8 = (bf16[384,768]{1,0:T(8,128)(2,1)S(1)}, bf16[384,768]{1,0:T(8,128)(2,1)S(1)}, u32[]{:S(2)}, u32[]{:S(2)}) collective-permute-start(bf16[384,768]{1,0:T(8,128)(2,1)S(1)} %constant_dynamic-update-slice_fusion.refs_0_), channel_id=1, source_target_pairs={{0,96},{32,64},{64,32},{96,0},{1,97},{33,65},{65,33},{97,1},{2,98}... | collective-permute-start | bytes 1769480 | tf_op jit(solution)/shard_map/ppermute | solution.py:24
  27.8 3.7 %all-to-all-start = ((bf16[4,512,384]{2,1,0:T(8,128)(2,1)}), bf16[4,512,384]{2,1,0:T(8,128)(2,1)S(1)}, u32[]{:S(2)}, u32[]{:S(2)}) async-start(bf16[4,512,384]{2,1,0:T(8,128)(2,1)} %broadcast_in_dim.18), calls=%async_computation | async-start | bytes 3145728 | tf_op jit(solution)/shard_map/all_to_all | solution.py:215
  31.5 5.5 %collective-permute-done.1 = bf16[512,384]{1,0:T(8,128)(2,1)} collective-permute-done((bf16[512,384]{1,0:T(8,128)(2,1)}, bf16[512,384]{1,0:T(8,128)(2,1)}, u32[]{:S(2)}, u32[]{:S(2)}) %collective-permute-start.1) | collective-permute-done | bytes 393248 | tf_op jit(solution)/shard_map/ppermute | solution.py:24
  37.0 3.7 %collective-permute-done = bf16[512,384]{1,0:T(8,128)(2,1)} collective-permute-done((bf16[512,384]{1,0:T(8,128)(2,1)}, bf16[512,384]{1,0:T(8,128)(2,1)}, u32[]{:S(2)}, u32[]{:S(2)}) %collective-permute-start) | collective-permute-done | bytes 393248 | tf_op jit(solution)/shard_map/ppermute | solution.py:24
  44.8 5.3 %collective-permute-done.11 = f32[1792]{0:T(1024)S(1)} collective-permute-done((f32[1792]{0:T(1024)S(1)}, f32[1792]{0:T(1024)S(1)}, u32[]{:S(2)}, u32[]{:S(2)}) %collective-permute-start.11) | collective-permute-done | bytes 7200 | tf_op jit(solution)/shard_map/ppermute | solution.py:24
  50.1 2.3 %collective-permute-done.9 = bf16[512,384]{1,0:T(8,128)(2,1)S(1)} collective-permute-done((bf16[512,384]{1,0:T(8,128)(2,1)}, bf16[512,384]{1,0:T(8,128)(2,1)S(1)}, u32[]{:S(2)}, u32[]{:S(2)}) %collective-permute-start.9) | collective-permute-done | bytes 393248 | tf_op jit(solution)/shard_map/ppermute | solution.py:24
  59.4 1.8 %multiply_convert_fusion = (bf16[512,384]{1,0:T(8,128)(2,1)S(1)}, bf16[512,384]{1,0:T(8,128)(2,1)S(1)}, bf16[512,384]{1,0:T(8,128)(2,1)S(1)}, bf16[512,384]{1,0:T(8,128)(2,1)S(1)}) fusion(bf16[512,384]{1,0:T(8,128)(2,1)S(1)} %collective-permute-done.9, f32[384]{0:T(512)S(1)} %get-tuple-element.145, f32[512]{0:T(512)S(1)} %get-tuple-element.142, ...), kind=kLoop, calls=%fused_computation.12 | loop fusion | flops 3932160 | bytes 3155968 | tf_op jit(solution)/shard_map/convert_element_type | solution.py:240
  61.3 2.4 %shard_map.67 = (bf16[4,384,768]{2,1,0:T(8,128)(2,1)S(1)}, bf16[4,384,512]{2,1,0:T(8,128)(2,1)S(1)}) custom-call(bf16[512,384]{1,0:T(8,128)(2,1)S(1)} %get-tuple-element.156.refs_0_.refs_9_, bf16[512,384]{1,0:T(8,128)(2,1)S(1)} %get-tuple-element.154.refs_1_.refs_10_, bf16[512,384]{1,0:T(8,128)(2,1)S(1)} %get-tuple-element.155.refs_2_.refs_11_, ...), custom_call_target="tpu_custom_call" | custom-call | flops 1 | bytes 1 | tf_op jit(solution)/shard_map/pallas_call | solution.py:50
  66.4 7.6 %shard_map.68 = (f32[512,384]{1,0:T(8,128)S(1)}, bf16[512,384]{1,0:T(8,128)(2,1)S(1)}, bf16[512,384]{1,0:T(8,128)(2,1)S(1)}, bf16[528,384]{1,0:T(8,128)(2,1)S(1)...) custom-call(bf16[384,768]{1,0:T(8,128)(2,1)S(1)} %copy-done.2, ...), custom_call_target="tpu_custom_call" | custom-call | flops 40000000 | bytes 40000000 | tf_op jit(solution)/shard_map/pallas_call | solution.py:50
  74.0 2.1 %collective-permute-start.16 = (bf16[528,384]{1,0:T(8,128)(2,1)S(1)}, bf16[528,384]{1,0:T(8,128)(2,1)S(1)}, u32[]{:S(2)}, u32[]{:S(2)}) collective-permute-start(bf16[528,384]{1,0:T(8,128)(2,1)S(1)} %get-tuple-element.103), channel_id=1, source_target_pairs={{0,4},{4,0},{8,12},{12,8},{1,5},{5,1},{9,13},{13,9},{2,6},{6,2},{1... | collective-permute-start | bytes 1216520 | tf_op jit(solution)/shard_map/ppermute | solution.py:24
  76.1 2.1 %shard_map.69 = (f32[384,768]{1,0:T(8,128)S(1)}, bf16[384,768]{1,0:T(8,128)(2,1)}, bf16[384,768]{1,0:T(8,128)(2,1)}, bf16[384,768]{1,0:T(8,128)(2,1)S(1)}) custom-call(bf16[4,512,384]{2,1,0:T(8,128)(2,1)S(1)} %all-to-all-done.refs_4_.refs_8_.refs_0_, bf16[4,384,512]{2,1,0:T(8,128)(2,1)S(1)} %get-tuple-element.104.refs_1_, ...), custom_call_target="tpu_custom_call" | custom-call | flops 1 | bytes 1 | tf_op jit(solution)/shard_map/pallas_call | solution.py:50
  79.5 3.1 %collective-permute-start.19 = (bf16[384,768]{1,0:T(8,128)(2,1)}, bf16[384,768]{1,0:T(8,128)(2,1)}, u32[]{:S(2)}, u32[]{:S(2)}) collective-permute-start(bf16[384,768]{1,0:T(8,128)(2,1)} %get-tuple-element.109), channel_id=1, source_target_pairs={{0,64},{32,96},{64,0},{96,32},{1,65},{33,97},{65,1},{97,33},{2,66}... | collective-permute-start | bytes 1769480 | tf_op jit(solution)/shard_map/ppermute | solution.py:24
  82.6 3.2 %collective-permute-done.16.relay = bf16[528,384]{1,0:T(8,128)(2,1)S(1)} collective-permute-done((bf16[528,384]{1,0:T(8,128)(2,1)S(1)}, bf16[528,384]{1,0:T(8,128)(2,1)S(1)}, u32[]{:S(2)}, u32[]{:S(2)}) %collective-permute-start.16) | collective-permute-done | bytes 405536 | tf_op jit(solution)/shard_map/ppermute | solution.py:24
  86.0 1.9 %collective-permute-start.22 = (bf16[528,384]{1,0:T(8,128)(2,1)S(1)}, bf16[528,384]{1,0:T(8,128)(2,1)S(1)}, u32[]{:S(2)}, u32[]{:S(2)}) collective-permute-start(bf16[528,384]{1,0:T(8,128)(2,1)S(1)} %get-tuple-element.118), channel_id=1, source_target_pairs={{0,8},{4,12},{8,0},{12,4},{1,9},{5,13},{9,1},{13,5},{2,10},{6,14},... | collective-permute-start | bytes 1216520 | tf_op jit(solution)/shard_map/ppermute | solution.py:24
  87.9 4.4 %all-to-all-start.1 = ((bf16[4,512,384]{2,1,0:T(8,128)(2,1)}), bf16[4,512,384]{2,1,0:T(8,128)(2,1)}, u32[]{:S(2)}, u32[]{:S(2)}) async-start(bf16[4,512,384]{2,1,0:T(8,128)(2,1)} %copy-done), calls=%async_computation.1 | async-start | bytes 3145728 | tf_op jit(solution)/shard_map/all_to_all | solution.py:309
  92.6 13.6 %collective-permute-done.22 = bf16[528,384]{1,0:T(8,128)(2,1)S(1)} collective-permute-done((bf16[528,384]{1,0:T(8,128)(2,1)S(1)}, bf16[528,384]{1,0:T(8,128)(2,1)S(1)}, u32[]{:S(2)}, u32[]{:S(2)}) %collective-permute-start.22) | collective-permute-done | bytes 405536 | tf_op jit(solution)/shard_map/ppermute | solution.py:24
  106.2 2.4 %collective-permute-done.19 = bf16[384,768]{1,0:T(8,128)(2,1)} collective-permute-done((bf16[384,768]{1,0:T(8,128)(2,1)}, bf16[384,768]{1,0:T(8,128)(2,1)}, u32[]{:S(2)}, u32[]{:S(2)}) %collective-permute-start.19) | collective-permute-done | bytes 589856 | tf_op jit(solution)/shard_map/ppermute | solution.py:24
  108.6 1.8 %collective-permute-done.20 = bf16[384,768]{1,0:T(8,128)(2,1)} collective-permute-done((bf16[384,768]{1,0:T(8,128)(2,1)S(1)}, bf16[384,768]{1,0:T(8,128)(2,1)}, u32[]{:S(2)}, u32[]{:S(2)}) %collective-permute-start.20) | collective-permute-done | bytes 589856 | tf_op jit(solution)/shard_map/ppermute | solution.py:24
  112.2 8.5 %collective-permute-start.29 = (bf16[384,384]{1,0:T(8,128)(2,1)S(1)}, bf16[384,384]{1,0:T(8,128)(2,1)S(1)}, u32[]{:S(2)}, u32[]{:S(2)}) collective-permute-start(bf16[384,384]{1,0:T(8,128)(2,1)S(1)} %get-tuple-element.137), channel_id=1, source_target_pairs={{0,128},{1,129},{2,146},{3,147},{16,130},{17,131},{18,144},{19,145... | collective-permute-start | bytes 884744 | tf_op jit(solution)/shard_map/ppermute | solution.py:24
  120.7 1.9 %collective-permute-start.24 = (bf16[384,384]{1,0:T(8,128)(2,1)S(1)}, bf16[384,384]{1,0:T(8,128)(2,1)S(1)}, u32[]{:S(2)}, u32[]{:S(2)}) collective-permute-start(bf16[384,384]{1,0:T(8,128)(2,1)S(1)} %get-tuple-element.137), channel_id=1, source_target_pairs={{0,0},{1,1},{2,18},{3,19},{16,2},{17,3},{18,16},{19,17},{128,128},... | collective-permute-start | bytes 884744 | tf_op jit(solution)/shard_map/ppermute | solution.py:24
  122.9 1.8 %collective-permute-start.23 = (bf16[384,384]{1,0:T(8,128)(2,1)S(1)}, bf16[384,384]{1,0:T(8,128)(2,1)S(1)}, u32[]{:S(2)}, u32[]{:S(2)}) collective-permute-start(bf16[384,384]{1,0:T(8,128)(2,1)S(1)} %get-tuple-element.138), channel_id=1, source_target_pairs={{0,129},{1,128},{2,147},{3,146},{16,131},{17,130},{18,145},{19,144... | collective-permute-start | bytes 884744 | tf_op jit(solution)/shard_map/ppermute | solution.py:24
  124.8 9.3 %collective-permute-done.24 = bf16[384,384]{1,0:T(8,128)(2,1)S(1)} collective-permute-done((bf16[384,384]{1,0:T(8,128)(2,1)S(1)}, bf16[384,384]{1,0:T(8,128)(2,1)S(1)}, u32[]{:S(2)}, u32[]{:S(2)}) %collective-permute-start.24) | collective-permute-done | bytes 294944 | tf_op jit(solution)/shard_map/ppermute | solution.py:24
  134.8 2.5 %collective-permute-start.27 = (f32[2,512]{1,0:T(2,128)S(1)}, f32[2,512]{1,0:T(2,128)S(1)}, u32[]{:S(2)}, u32[]{:S(2)}) collective-permute-start(f32[2,512]{1,0:T(2,128)S(1)} %fusion.10), channel_id=1, source_target_pairs={{0,2},{1,3},{2,0},{3,1},{4,6},{5,7},{6,4},{7,5},{8,10},{9,11},{10,... | collective-permute-start | bytes 12296 | tf_op jit(solution)/shard_map/ppermute | solution.py:24
  138.0 2.5 %reduce_sum.32 = bf16[512,384]{1,0:T(8,128)(2,1)} reduce(bf16[4,512,384]{2,1,0:T(8,128)(2,1)} %all-to-all-done.1, bf16[]{:T(256)} %constant.46.clone.1), dimensions={0}, to_apply=%region_2.3 | reduce | flops 589824 | bytes 1966082 | tf_op jit(solution)/shard_map/reduce_sum | solution.py:311
  140.5 3.5 %collective-permute-done.23 = bf16[384,384]{1,0:T(8,128)(2,1)S(1)} collective-permute-done((bf16[384,384]{1,0:T(8,128)(2,1)S(1)}, bf16[384,384]{1,0:T(8,128)(2,1)S(1)}, u32[]{:S(2)}, u32[]{:S(2)}) %collective-permute-start.23) | collective-permute-done | bytes 294944 | tf_op jit(solution)/shard_map/ppermute | solution.py:24
  146.0 2.1 %fusion.6 = bf16[512,384]{1,0:T(8,128)(2,1)} fusion(bf16[512,384]{1,0:T(8,128)(2,1)} %param.4, bf16[512,384]{1,0:T(8,128)(2,1)S(1)} %slice-done, f32[512,384]{1,0:T(8,128)S(1)} %copy-done.4, bf16[512,384]{1,0:T(8,128)(2,1)S(1)} %copy-done.23, f32[512]{0:T(512)S(1)} %bitcast.25, f32[512]{0:T(512)S(1)} %bitcast.24, f32[384]{0:T(512)S(1)} %copy-done.24, ...), kind=kLoop, calls=%fused_computation.11 | loop fusion | flops 2555904 | bytes 2369024 | tf_op jit(solution)/shard_map/convert_element_type | solution.py:322
  (128 shorter events, 28.1 us)
Async XLA Ops:
  3.1 8.2 %collective-permute-start.2 = (f32[2,512]{1,0:T(2,128)S(1)}, f32[2,512]{1,0:T(2,128)S(1)}, u32[]{:S(2)}, u32[]{:S(2)}) collective-permute-start(f32[2,512]{1,0:T(2,128)S(1)} %pad_maximum_fusion.5), channel_id=1, source_target_pairs={{0,1},{1,0},{2,3},{3,2},{4,5},{5,4},{6,7},{7,6},{8,9},{9,8},{10,11... | collective-permute-start | bytes 12296 | tf_op jit(solution)/shard_map/ppermute | solution.py:24
  5.4 7.4 %collective-permute-start.4 = (bf16[384,384]{1,0:T(8,128)(2,1)S(1)}, bf16[384,384]{1,0:T(8,128)(2,1)S(1)}, u32[]{:S(2)}, u32[]{:S(2)}) collective-permute-start(bf16[384,384]{1,0:T(8,128)(2,1)S(1)} %get-tuple-element.139), channel_id=1, source_target_pairs={{0,1},{1,0},{2,17},{3,16},{16,19},{17,18},{18,3},{19,2},{4,5},{5,4... | collective-permute-start | bytes 884744 | tf_op jit(solution)/shard_map/ppermute | solution.py:24
  7.4 9.5 %collective-permute-start.3 = (bf16[384,384]{1,0:T(8,128)(2,1)S(1)}, bf16[384,384]{1,0:T(8,128)(2,1)S(1)}, u32[]{:S(2)}, u32[]{:S(2)}) collective-permute-start(bf16[384,384]{1,0:T(8,128)(2,1)S(1)} %get-tuple-element.140), channel_id=1, source_target_pairs={{0,0},{1,1},{2,16},{3,17},{16,18},{17,19},{18,2},{19,3},{4,4},{5,5... | collective-permute-start | bytes 884744 | tf_op jit(solution)/shard_map/ppermute | solution.py:24
  16.9 6.1 %collective-permute-start.5 = (f32[2,512]{1,0:T(2,128)S(1)}, f32[2,512]{1,0:T(2,128)S(1)}, u32[]{:S(2)}, u32[]{:S(2)}) collective-permute-start(f32[2,512]{1,0:T(2,128)S(1)} %pad_maximum_fusion.6), channel_id=1, source_target_pairs={{0,2},{1,3},{2,0},{3,1},{4,6},{5,7},{6,4},{7,5},{8,10},{9,11},{10,... | collective-permute-start | bytes 12296 | tf_op jit(solution)/shard_map/ppermute | solution.py:24
  19.0 17.9 %collective-permute-start.1 = (bf16[512,384]{1,0:T(8,128)(2,1)}, bf16[512,384]{1,0:T(8,128)(2,1)}, u32[]{:S(2)}, u32[]{:S(2)}) collective-permute-start(bf16[512,384]{1,0:T(8,128)(2,1)} %param.4), channel_id=1, source_target_pairs={{0,4},{4,0},{8,12},{12,8},{1,5},{5,1},{9,13},{13,9},{2,6},{6,2},{1... | collective-permute-start | bytes 1179656 | tf_op jit(solution)/shard_map/ppermute | solution.py:24
  20.0 20.6 %collective-permute-start = (bf16[512,384]{1,0:T(8,128)(2,1)}, bf16[512,384]{1,0:T(8,128)(2,1)}, u32[]{:S(2)}, u32[]{:S(2)}) collective-permute-start(bf16[512,384]{1,0:T(8,128)(2,1)} %param.4), channel_id=1, source_target_pairs={{0,8},{4,12},{8,0},{12,4},{1,9},{5,13},{9,1},{13,5},{2,10},{6,14},... | collective-permute-start | bytes 1179656 | tf_op jit(solution)/shard_map/ppermute | solution.py:24
  23.1 29.3 %collective-permute-start.8 = (bf16[384,768]{1,0:T(8,128)(2,1)S(1)}, bf16[384,768]{1,0:T(8,128)(2,1)S(1)}, u32[]{:S(2)}, u32[]{:S(2)}) collective-permute-start(bf16[384,768]{1,0:T(8,128)(2,1)S(1)} %constant_dynamic-update-slice_fusion.refs_0_), channel_id=1, source_target_pairs={{0,96},{32,64},{64,32},{96,0},{1,97},{33,65},{65,33},{97,1},{2,98}... | collective-permute-start | bytes 1769480 | tf_op jit(solution)/shard_map/ppermute | solution.py:24
  25.7 26.7 %collective-permute-start.7 = (bf16[384,768]{1,0:T(8,128)(2,1)S(1)}, bf16[384,768]{1,0:T(8,128)(2,1)S(1)}, u32[]{:S(2)}, u32[]{:S(2)}) collective-permute-start(bf16[384,768]{1,0:T(8,128)(2,1)S(1)} %constant_dynamic-update-slice_fusion.refs_0_), channel_id=1, source_target_pairs={{0,64},{32,96},{64,0},{96,32},{1,65},{33,97},{65,1},{97,33},{2,66}... | collective-permute-start | bytes 1769480 | tf_op jit(solution)/shard_map/ppermute | solution.py:24
  26.2 26.8 %collective-permute-start.6 = (bf16[384,768]{1,0:T(8,128)(2,1)S(1)}, bf16[384,768]{1,0:T(8,128)(2,1)}, u32[]{:S(2)}, u32[]{:S(2)}) collective-permute-start(bf16[384,768]{1,0:T(8,128)(2,1)S(1)} %constant_dynamic-update-slice_fusion.refs_0_), channel_id=1, source_target_pairs={{0,32},{32,0},{64,96},{96,64},{1,33},{33,1},{65,97},{97,65},{2,34}... | collective-permute-start | bytes 1769480 | tf_op jit(solution)/shard_map/ppermute | solution.py:24
  27.8 33.4 %all-to-all-start = ((bf16[4,512,384]{2,1,0:T(8,128)(2,1)}), bf16[4,512,384]{2,1,0:T(8,128)(2,1)S(1)}, u32[]{:S(2)}, u32[]{:S(2)}) async-start(bf16[4,512,384]{2,1,0:T(8,128)(2,1)} %broadcast_in_dim.18), calls=%async_computation | async-start | bytes 3145728 | tf_op jit(solution)/shard_map/all_to_all | solution.py:215
  40.6 3.0 %collective-permute-start.10 = (f32[1408]{0:T(1024)S(1)}, f32[1408]{0:T(1024)S(1)}, u32[]{:S(2)}, u32[]{:S(2)}) collective-permute-start(f32[1408]{0:T(1024)S(1)} %pad_maximum_fusion.1), channel_id=1, source_target_pairs={{0,4},{4,0},{8,12},{12,8},{1,5},{5,1},{9,13},{13,9},{2,6},{6,2},{1... | collective-permute-start | bytes 16904 | tf_op jit(solution)/shard_map/ppermute | solution.py:24
  40.8 11.7 %collective-permute-start.9 = (bf16[512,384]{1,0:T(8,128)(2,1)}, bf16[512,384]{1,0:T(8,128)(2,1)S(1)}, u32[]{:S(2)}, u32[]{:S(2)}) collective-permute-start(bf16[512,384]{1,0:T(8,128)(2,1)} %collective-permute-done), channel_id=1, source_target_pairs={{0,4},{4,0},{8,12},{12,8},{1,5},{5,1},{9,13},{13,9},{2,6},{6,2},{1... | collective-permute-start | bytes 1179656 | tf_op jit(solution)/shard_map/ppermute | solution.py:24
  43.7 6.4 %collective-permute-start.11 = (f32[1792]{0:T(1024)S(1)}, f32[1792]{0:T(1024)S(1)}, u32[]{:S(2)}, u32[]{:S(2)}) collective-permute-start(f32[1792]{0:T(1024)S(1)} %pad_maximum_fusion.2), channel_id=1, source_target_pairs={{0,8},{4,12},{8,0},{12,4},{1,9},{5,13},{9,1},{13,5},{2,10},{6,14},... | collective-permute-start | bytes 21512 | tf_op jit(solution)/shard_map/ppermute | solution.py:24
  53.1 2.7 %collective-permute-start.12 = (bf16[384,768]{1,0:T(8,128)(2,1)S(1)}, bf16[384,768]{1,0:T(8,128)(2,1)S(1)}, u32[]{:S(2)}, u32[]{:S(2)}) collective-permute-start(bf16[384,768]{1,0:T(8,128)(2,1)S(1)} %constant_dynamic-update-slice_fusion.refs_0_), channel_id=1, source_target_pairs={{0,16},{16,0},{1,17},{17,1},{2,18},{18,2},{3,19},{19,3},{4,20},{20... | collective-permute-start | bytes 1769480 | tf_op jit(solution)/shard_map/ppermute | solution.py:24
  53.6 3.4 %collective-permute-start.13 = (bf16[384,768]{1,0:T(8,128)(2,1)}, bf16[384,768]{1,0:T(8,128)(2,1)S(1)}, u32[]{:S(2)}, u32[]{:S(2)}) collective-permute-start(bf16[384,768]{1,0:T(8,128)(2,1)} %collective-permute-done.6.refs_1_), channel_id=1, source_target_pairs={{0,16},{16,0},{1,17},{17,1},{2,18},{18,2},{3,19},{19,3},{4,20},{20... | collective-permute-start | bytes 1769480 | tf_op jit(solution)/shard_map/ppermute | solution.py:24
  53.6 4.2 %collective-permute-start.14 = (bf16[384,768]{1,0:T(8,128)(2,1)S(1)}, bf16[384,768]{1,0:T(8,128)(2,1)S(1)}, u32[]{:S(2)}, u32[]{:S(2)}) collective-permute-start(bf16[384,768]{1,0:T(8,128)(2,1)S(1)} %collective-permute-done.7.refs_2_), channel_id=1, source_target_pairs={{0,16},{16,0},{1,17},{17,1},{2,18},{18,2},{3,19},{19,3},{4,20},{20... | collective-permute-start | bytes 1769480 | tf_op jit(solution)/shard_map/ppermute | solution.py:24
  54.9 3.7 %collective-permute-start.15 = (bf16[384,768]{1,0:T(8,128)(2,1)S(1)}, bf16[384,768]{1,0:T(8,128)(2,1)S(1)}, u32[]{:S(2)}, u32[]{:S(2)}) collective-permute-start(bf16[384,768]{1,0:T(8,128)(2,1)S(1)} %collective-permute-done.8.refs_3_), channel_id=1, source_target_pairs={{0,16},{16,0},{1,17},{17,1},{2,18},{18,2},{3,19},{19,3},{4,20},{20... | collective-permute-start | bytes 1769480 | tf_op jit(solution)/shard_map/ppermute | solution.py:24
  63.7 12.3 %collective-permute-start.17 = (bf16[4,384,768]{2,1,0:T(8,128)(2,1)S(1)}, bf16[4,384,768]{2,1,0:T(8,128)(2,1)S(1)}, u32[]{:S(2)}, u32[]{:S(2)}) collective-permute-start(bf16[4,384,768]{2,1,0:T(8,128)(2,1)S(1)} %get-tuple-element.105), channel_id=1, source_target_pairs={{0,16},{16,0},{1,17},{17,1},{2,18},{18,2},{3,19},{19,3},{4,20},{20... | collective-permute-start | bytes 7077896 | tf_op jit(solution)/shard_map/ppermute | solution.py:24
  74.0 11.8 %collective-permute-start.16 = (bf16[528,384]{1,0:T(8,128)(2,1)S(1)}, bf16[528,384]{1,0:T(8,128)(2,1)S(1)}, u32[]{:S(2)}, u32[]{:S(2)}) collective-permute-start(bf16[528,384]{1,0:T(8,128)(2,1)S(1)} %get-tuple-element.103), channel_id=1, source_target_pairs={{0,4},{4,0},{8,12},{12,8},{1,5},{5,1},{9,13},{13,9},{2,6},{6,2},{1... | collective-permute-start | bytes 1216520 | tf_op jit(solution)/shard_map/ppermute | solution.py:24
  78.2 28.0 %collective-permute-start.18 = (bf16[384,768]{1,0:T(8,128)(2,1)}, bf16[384,768]{1,0:T(8,128)(2,1)}, u32[]{:S(2)}, u32[]{:S(2)}) collective-permute-start(bf16[384,768]{1,0:T(8,128)(2,1)} %get-tuple-element.108), channel_id=1, source_target_pairs={{0,32},{32,0},{64,96},{96,64},{1,33},{33,1},{65,97},{97,65},{2,34}... | collective-permute-start | bytes 1769480 | tf_op jit(solution)/shard_map/ppermute | solution.py:24
  79.5 29.1 %collective-permute-start.19 = (bf16[384,768]{1,0:T(8,128)(2,1)}, bf16[384,768]{1,0:T(8,128)(2,1)}, u32[]{:S(2)}, u32[]{:S(2)}) collective-permute-start(bf16[384,768]{1,0:T(8,128)(2,1)} %get-tuple-element.109), channel_id=1, source_target_pairs={{0,64},{32,96},{64,0},{96,32},{1,65},{33,97},{65,1},{97,33},{2,66}... | collective-permute-start | bytes 1769480 | tf_op jit(solution)/shard_map/ppermute | solution.py:24
  82.6 27.8 %collective-permute-start.20 = (bf16[384,768]{1,0:T(8,128)(2,1)S(1)}, bf16[384,768]{1,0:T(8,128)(2,1)}, u32[]{:S(2)}, u32[]{:S(2)}) collective-permute-start(bf16[384,768]{1,0:T(8,128)(2,1)S(1)} %get-tuple-element.110), channel_id=1, source_target_pairs={{0,96},{32,64},{64,32},{96,0},{1,97},{33,65},{65,33},{97,1},{2,98}... | collective-permute-start | bytes 1769480 | tf_op jit(solution)/shard_map/ppermute | solution.py:24
  86.0 20.2 %collective-permute-start.22 = (bf16[528,384]{1,0:T(8,128)(2,1)S(1)}, bf16[528,384]{1,0:T(8,128)(2,1)S(1)}, u32[]{:S(2)}, u32[]{:S(2)}) collective-permute-start(bf16[528,384]{1,0:T(8,128)(2,1)S(1)} %get-tuple-element.118), channel_id=1, source_target_pairs={{0,8},{4,12},{8,0},{12,4},{1,9},{5,13},{9,1},{13,5},{2,10},{6,14},... | collective-permute-start | bytes 1216520 | tf_op jit(solution)/shard_map/ppermute | solution.py:24
  87.9 50.1 %all-to-all-start.1 = ((bf16[4,512,384]{2,1,0:T(8,128)(2,1)}), bf16[4,512,384]{2,1,0:T(8,128)(2,1)}, u32[]{:S(2)}, u32[]{:S(2)}) async-start(bf16[4,512,384]{2,1,0:T(8,128)(2,1)} %copy-done), calls=%async_computation.1 | async-start | bytes 3145728 | tf_op jit(solution)/shard_map/all_to_all | solution.py:309
  92.2 19.8 %collective-permute-start.21 = (bf16[512,384]{1,0:T(8,128)(2,1)S(1)}, bf16[512,384]{1,0:T(8,128)(2,1)S(1)}, u32[]{:S(2)}, u32[]{:S(2)}) collective-permute-start(bf16[512,384]{1,0:T(8,128)(2,1)S(1)} %copy-done.18), channel_id=1, source_target_pairs={{0,4},{4,0},{8,12},{12,8},{1,5},{5,1},{9,13},{13,9},{2,6},{6,2},{1... | collective-permute-start | bytes 1179656 | tf_op jit(solution)/shard_map/ppermute | solution.py:24
  112.2 31.9 %collective-permute-start.29 = (bf16[384,384]{1,0:T(8,128)(2,1)S(1)}, bf16[384,384]{1,0:T(8,128)(2,1)S(1)}, u32[]{:S(2)}, u32[]{:S(2)}) collective-permute-start(bf16[384,384]{1,0:T(8,128)(2,1)S(1)} %get-tuple-element.137), channel_id=1, source_target_pairs={{0,128},{1,129},{2,146},{3,147},{16,130},{17,131},{18,144},{19,145... | collective-permute-start | bytes 884744 | tf_op jit(solution)/shard_map/ppermute | solution.py:24
  120.7 13.4 %collective-permute-start.24 = (bf16[384,384]{1,0:T(8,128)(2,1)S(1)}, bf16[384,384]{1,0:T(8,128)(2,1)S(1)}, u32[]{:S(2)}, u32[]{:S(2)}) collective-permute-start(bf16[384,384]{1,0:T(8,128)(2,1)S(1)} %get-tuple-element.137), channel_id=1, source_target_pairs={{0,0},{1,1},{2,18},{3,19},{16,2},{17,3},{18,16},{19,17},{128,128},... | collective-permute-start | bytes 884744 | tf_op jit(solution)/shard_map/ppermute | solution.py:24
  122.6 12.2 %collective-permute-start.25 = (bf16[384,384]{1,0:T(8,128)(2,1)S(1)}, bf16[384,384]{1,0:T(8,128)(2,1)S(1)}, u32[]{:S(2)}, u32[]{:S(2)}) collective-permute-start(bf16[384,384]{1,0:T(8,128)(2,1)S(1)} %get-tuple-element.138), channel_id=1, source_target_pairs={{0,1},{1,0},{2,19},{3,18},{16,3},{17,2},{18,17},{19,16},{128,129},... | collective-permute-start | bytes 884744 | tf_op jit(solution)/shard_map/ppermute | solution.py:24
  122.9 21.1 %collective-permute-start.23 = (bf16[384,384]{1,0:T(8,128)(2,1)S(1)}, bf16[384,384]{1,0:T(8,128)(2,1)S(1)}, u32[]{:S(2)}, u32[]{:S(2)}) collective-permute-start(bf16[384,384]{1,0:T(8,128)(2,1)S(1)} %get-tuple-element.138), channel_id=1, source_target_pairs={{0,129},{1,128},{2,147},{3,146},{16,131},{17,130},{18,145},{19,144... | collective-permute-start | bytes 884744 | tf_op jit(solution)/shard_map/ppermute | solution.py:24
  134.8 9.3 %collective-permute-start.28 = (f32[2,512]{1,0:T(2,128)S(1)}, f32[2,512]{1,0:T(2,128)S(1)}, u32[]{:S(2)}, u32[]{:S(2)}) collective-permute-start(f32[2,512]{1,0:T(2,128)S(1)} %fusion.10), channel_id=1, source_target_pairs={{0,3},{1,2},{2,1},{3,0},{4,7},{5,6},{6,5},{7,4},{8,11},{9,10},{10,... | collective-permute-start | bytes 12296 | tf_op jit(solution)/shard_map/ppermute | solution.py:24
  134.8 9.3 %collective-permute-start.27 = (f32[2,512]{1,0:T(2,128)S(1)}, f32[2,512]{1,0:T(2,128)S(1)}, u32[]{:S(2)}, u32[]{:S(2)}) collective-permute-start(f32[2,512]{1,0:T(2,128)S(1)} %fusion.10), channel_id=1, source_target_pairs={{0,2},{1,3},{2,0},{3,1},{4,6},{5,7},{6,4},{7,5},{8,10},{9,11},{10,... | collective-permute-start | bytes 12296 | tf_op jit(solution)/shard_map/ppermute | solution.py:24
  137.3 6.8 %collective-permute-start.26 = (f32[2,512]{1,0:T(2,128)S(1)}, f32[2,512]{1,0:T(2,128)S(1)}, u32[]{:S(2)}, u32[]{:S(2)}) collective-permute-start(f32[2,512]{1,0:T(2,128)S(1)} %fusion.10), channel_id=1, source_target_pairs={{0,1},{1,0},{2,3},{3,2},{4,5},{5,4},{6,7},{7,6},{8,9},{9,8},{10,11... | collective-permute-start | bytes 12296 | tf_op jit(solution)/shard_map/ppermute | solution.py:24
  (26 other events, 145.5 us)
